TPU v7x, 512 devices: a whole 4x4x16 slice. The times are simulated.
512 devices in a mesh: depth: 32 (over x, y, z_hi), height: 16 (over z_lo, core).
Axes of the slice: x: 4, y: 4, z: 16 (z_hi: 2, z_lo: 8; z = z_hi * 8 + z_lo), core: 2. Of those that a mesh axis runs over, the one named last changes fastest.
Arguments:
- volume: bfloat16 [64, 64, 64, 128], P(None, 'depth', 'height'), may hold values from -6 to 6
- kernel_one: bfloat16 [3, 3, 3, 64, 128], replicated, may hold values from -0.15625 to 0.15625
- kernel_two: bfloat16 [3, 3, 3, 128, 128], replicated, may hold values from -0.109375 to 0.109375
- cotangent: bfloat16 [128, 32, 32, 64], P('height', 'depth'), may hold values from -6 to 6
Outputs:
- next_acts: bfloat16 [128, 32, 32, 64], P('height', 'depth')
- volume_grad: bfloat16 [64, 64, 64, 128], P(None, 'depth', 'height')
- kernel_one_grad: float32 [3, 3, 3, 64, 128], P(None, None, None, 'depth', 'height')
- kernel_two_grad: float32 [3, 3, 3, 128, 128], P(None, None, None, 'depth', 'height')
All inputs are finite; a program needn't handle non-finite values.
Results may differ from a plain program's by a relative error of at most 0.0051.
Values may be sent and summed in bfloat16 or wider, within the bound.
No kernel may reach another device: no remote copies, remote signals or barrier semaphores. Data moves between devices by JAX's collectives and lax.ppermute only.
A program may use at most 64 MiB of HBM per device.

v0:
```python
import math

import jax
import jax.numpy as jnp
from jax import lax
from jax.sharding import PartitionSpec as P

SLOPE = 0.2


def passed_along(block, axis, distance):
    devices = range(lax.axis_size(axis))
    route = [(i - distance, i) for i in devices if i - distance in devices]
    return lax.ppermute(block, axis, route)


def extended(array, sides, width):
    for axis, dim in sides:
        devices, length = (lax.axis_size(axis), array.shape[dim])
        up = [(i, (i + 1) % devices) for i in range(devices - 1)]
        down = [(j, i) for i, j in up]
        last = lax.slice_in_dim(array, length - width, length, axis=dim)
        leading = lax.slice_in_dim(array, 0, width, axis=dim)
        before = lax.ppermute(last, axis, up)
        after = lax.ppermute(leading, axis, down)
        array = jnp.concatenate([before, array, after], axis=dim)
    return array


def conv_local(inputs, kernel, stride, padding, dilation):
    result = lax.conv_general_dilated(
        inputs[None],
        kernel,
        window_strides=(stride, stride, stride),
        padding=padding,
        lhs_dilation=(dilation, dilation, dilation),
        dimension_numbers=("NCDHW", "DHWIO", "NCDHW"),
        preferred_element_type=jnp.float32,
    )
    return result[0]


def flip_swap(kernel):
    return jnp.flip(kernel, (0, 1, 2)).transpose(0, 1, 2, 4, 3)


def weight_grad(padded, cotan, stride):
    cin = padded.shape[0]
    cout = cotan.shape[0]
    sizes = cotan.shape[1:]
    flat_cot = cotan.reshape(cout, -1)
    pieces = []
    for off_d in range(3):
        for off_h in range(3):
            for off_w in range(3):
                starts = (0, off_d, off_h, off_w)
                limits = (
                    cin,
                    off_d + stride * (sizes[0] - 1) + 1,
                    off_h + stride * (sizes[1] - 1) + 1,
                    off_w + stride * (sizes[2] - 1) + 1,
                )
                window = lax.slice(padded, starts, limits, (1, stride, stride, stride))
                pieces.append(
                    lax.dot_general(
                        window.reshape(cin, -1),
                        flat_cot,
                        (((1,), (1,)), ((), ())),
                        preferred_element_type=jnp.float32,
                    )
                )
    return jnp.stack(pieces).reshape(3, 3, 3, cin, cout)


def per_device(volume, kernel_one, kernel_two, cotangent):
    zero3 = [(0, 0), (0, 0), (0, 0)]
    below = passed_along(volume[:, -1:], "depth", 1)
    deeper = jnp.concatenate([below, volume], axis=1)
    beside = passed_along(deeper[:, :, -1:], "height", 1)
    vol_pad = jnp.pad(jnp.concatenate([beside, deeper], axis=2), ((0, 0), (0, 0), (0, 0), (1, 0)))
    act_one = conv_local(vol_pad, kernel_one, 2, zero3, 1)
    hidden = (SLOPE * act_one + (1.0 - SLOPE) * jax.nn.softplus(act_one)).astype(jnp.bfloat16)
    cells = (
        act_one.shape[1]
        * act_one.shape[2]
        * act_one.shape[3]
        * lax.axis_size("depth")
        * lax.axis_size("height")
    )
    scale = 1.0 / math.sqrt(cells)
    groups = cotangent.shape[0]
    deep_hidden = extended(hidden, (("depth", 1),), 1)
    whole = lax.all_gather(deep_hidden, "height", axis=2, tiled=True)
    whole_pad = jnp.pad(whole, ((0, 0), (0, 0), (1, 1), (1, 1)))
    own_kernel = lax.dynamic_slice_in_dim(kernel_two, lax.axis_index("height") * groups, groups, 4)
    next_acts = conv_local(whole_pad, own_kernel, 1, zero3, 1).astype(jnp.bfloat16)
    partial_two = weight_grad(whole_pad, cotangent, 1)
    kernel_two_grad = (
        lax.psum_scatter(partial_two, "depth", scatter_dimension=3, tiled=True) * scale
    )
    cot_slab = lax.all_to_all(cotangent, "height", split_axis=2, concat_axis=0, tiled=True)
    cot_pad = extended(cot_slab, (("depth", 1), ("height", 2)), 1)
    cot_pad = jnp.pad(cot_pad, ((0, 0), (0, 0), (0, 0), (1, 1)))
    hidden_grad = conv_local(cot_pad, flip_swap(kernel_two), 1, zero3, 1)
    act_grad = (hidden_grad * (SLOPE + (1.0 - SLOPE) * jax.nn.sigmoid(act_one))).astype(
        jnp.bfloat16
    )
    upper = passed_along(act_grad[:, :1], "depth", -1)
    taller = jnp.concatenate([act_grad, upper], axis=1)
    upper_side = passed_along(taller[:, :, :1], "height", -1)
    grad_ext = jnp.concatenate([taller, upper_side], axis=2)
    volume_grad = conv_local(
        grad_ext, flip_swap(kernel_one), 1, [(1, 0), (1, 0), (1, 2)], 2
    ).astype(jnp.bfloat16)
    partial_one = weight_grad(vol_pad, act_grad, 2)
    one_depth = lax.psum_scatter(partial_one, "depth", scatter_dimension=3, tiled=True)
    kernel_one_grad = lax.psum_scatter(one_depth, "height", scatter_dimension=4, tiled=True) * scale
    return (next_acts, volume_grad, kernel_one_grad, kernel_two_grad)


def solution(mesh):
    placed = (P(None, "depth", "height", None), P(), P(), P("height", "depth", None, None))
    return jax.shard_map(
        per_device,
        mesh=mesh,
        in_specs=placed,
        out_specs=(
            P("height", "depth", None, None),
            P(None, "depth", "height", None),
            P(None, None, None, "depth", "height"),
            P(None, None, None, "depth", "height"),
        ),
        check_vma=False,
    )
```

profile of v0, /device:TPU:1, one launch (start us, length us, event | category | flops | bytes accessed | tf_op | source)
XLA Modules:
  0.0 1084.1 jit_solution(11699692657858405661)
XLA Ops:
  8.1 16.3 %collective-permute-start = (bf16[64,1,4,128]{3,0,2,1:T(8,128)(2,1)S(1)}, bf16[64,1,4,128]{3,0,2,1:T(8,128)(2,1)S(1)}, u32[]{:S(2)}, u32[]{:S(2)}) collective-permute-start(bf16[64,1,4,128]{3,0,2,1:T(8,128)(2,1)S(1)} %copy.422), channel_id=1, source_target_pairs={{0,16},{16,32},{32,48},{48,64},{64,80},{80,96},{96,112},{112,128},... | collective-permute-start | bytes 196616 | tf_op jit(solution)/shard_map/ppermute | solution.py:14
  26.0 6.0 all-to-all-start
  33.0 3.5 collective-permute-start.1
  36.6 1.3 dynamic-slice.2
  37.9 1.3 dynamic-slice
  42.0 1.3 collective-permute-start.5
  43.3 12.7 %collective-permute-start.4 = (bf16[128,1,2,64]{3,0,2,1:T(8,128)(2,1)S(1)}, bf16[128,1,2,64]{3,0,2,1:T(8,128)(2,1)S(1)}, u32[]{:S(2)}, u32[]{:S(2)}) collective-permute-start(bf16[128,1,2,64]{3,0,2,1:T(8,128)(2,1)S(1)} %bitcast.577), channel_id=1, source_target_pairs={{0,16},{16,32},{32,48},{48,64},{64,80},{80,96},{96,112},{112,128},... | collective-permute-start | bytes 98312 | tf_op jit(solution)/shard_map/ppermute | solution.py:24
  57.1 2.8 collective-permute-done.4
  60.0 1.9 collective-permute-start.6
  61.9 2.4 collective-permute-start.7
  87.2 1.3 collective-permute-start.3
  88.5 13.5 %collective-permute-start.2 = (bf16[128,1,2,64]{0,3,2,1:T(8,128)(2,1)S(1)}, bf16[128,1,2,64]{0,3,2,1:T(8,128)(2,1)S(1)}, u32[]{:S(2)}, u32[]{:S(2)}) collective-permute-start(bf16[128,1,2,64]{0,3,2,1:T(8,128)(2,1)S(1)} %get-tuple-element.31), channel_id=1, source_target_pairs={{0,16},{16,32},{32,48},{48,64},{64,80},{80,96},{96,112},{112,128},... | collective-permute-start | bytes 98312 | tf_op jit(solution)/shard_map/ppermute | solution.py:24
  102.1 1.3 collective-permute-start.8
  109.1 8.1 collective-permute-done.8
  117.2 2.6 collective-permute-start.9
  120.0 3.2 collective-permute-done.9
  124.1 96.4 %all-gather.2.cloned.1.call-done = bf16[128,3,32,64]{0,3,2,1:T(8,128)(2,1)} async-done(((bf16[128,3,2,64]{0,3,2,1:T(8,128)(2,1)}), bf16[128,3,32,64]{0,3,2,1:T(8,128)(2,1)}) %all-gather.2.cloned.1.call-update) | async-done | bytes 1572880 | tf_op jit(solution)/shard_map/all_gather | solution.py:93
  220.5 1.4 fusion.64
  228.7 1.8 copy.311
  231.4 1.0 pad_bitcast_fusion
  233.5 4.4 fusion.3
  239.2 716.0 %all-reduce.9.cloned.1.call-done = (f32[3,3,3,64,128]{4,3,2,1,0:T(8,128)}, f32[3,3,3,128,8]{4,3,2,1,0:T(8,128)}) async-done(((f32[3,3,3,64,128]{4,3,2,1,0:T(8,128)}, f32[3,3,3,128,8]{4,3,2,1,0:T(8,128)}), (f32[3,3,3,64,128]{4,3,2,1,0:T(8,128)}, f32[3,3,3,128,8]{4,3,2,1,0:T(8,128)})) %all-reduce.9.cloned.1.call-update) | async-done | bytes 995344
  956.1 118.9 %all-reduce.4 = f32[3,3,3,2,128]{4,3,2,1,0:T(2,128)S(1)} all-reduce(f32[3,3,3,2,128]{4,3,2,1,0:T(2,128)S(1)} %constant_dynamic-slice_fusion), channel_id=3, replica_groups=mesh['depth'=32,'height'=16] {'height'}, use_global_device_ids=true, to_apply=%region_1.2.clone | all-reduce | flops 6912 | bytes 55296
  1075.7 1.5 dynamic-slice_multiply_fusion
  (160 shorter events, 46.6 us)
Async XLA Ops:
  7.2 79.5 %copy-start = (bf16[3,3,3,128,128]{4,3,2,1,0:T(8,128)(2,1)S(1)}, bf16[3,3,3,128,128]{4,3,2,1,0:T(8,128)(2,1)}, u32[]{:S(2)}) copy-start(bf16[3,3,3,128,128]{4,3,2,1,0:T(8,128)(2,1)} %param.6) | copy-start | bytes 2654212
  8.1 23.9 %collective-permute-start = (bf16[64,1,4,128]{3,0,2,1:T(8,128)(2,1)S(1)}, bf16[64,1,4,128]{3,0,2,1:T(8,128)(2,1)S(1)}, u32[]{:S(2)}, u32[]{:S(2)}) collective-permute-start(bf16[64,1,4,128]{3,0,2,1:T(8,128)(2,1)S(1)} %copy.422), channel_id=1, source_target_pairs={{0,16},{16,32},{32,48},{48,64},{64,80},{80,96},{96,112},{112,128},... | collective-permute-start | bytes 196616 | tf_op jit(solution)/shard_map/ppermute | solution.py:14
  26.0 15.8 %all-to-all-start = ((bf16[16,2,512]{2,1,0:T(2,128)(2,1)}), bf16[16,2,512]{2,1,0:T(2,128)(2,1)S(1)}, u32[]{:S(2)}, u32[]{:S(2)}) async-start(bf16[16,2,512]{2,1,0:T(2,128)(2,1)} %reshape.638), calls=%async_computation | async-start | bytes 65536 | tf_op jit(solution)/shard_map/all_to_all | solution.py:101
  32.0 188.5 %all-gather.2.cloned.1.call-start = ((), (), s32[]{:S(2)}) async-start(), calls=%async_computation.1 | async-start | bytes 1671168 | tf_op jit(solution)/shard_map/all_gather | solution.py:93
  33.0 23.0 %collective-permute-start.1 = (bf16[64,3,1,128]{3,0,2,1:T(8,128)(2,1)S(1)}, bf16[64,3,1,128]{3,0,2,1:T(8,128)(2,1)S(1)}, u32[]{:S(2)}, u32[]{:S(2)}) collective-permute-start(bf16[64,3,1,128]{3,0,2,1:T(8,128)(2,1)S(1)} %slice.276), channel_id=1, source_target_pairs={{0,1},{1,2},{2,3},{3,4},{4,5},{5,6},{6,7},{7,8},{8,9},{9,10},{10,1... | collective-permute-start | bytes 147464 | tf_op jit(solution)/shard_map/ppermute | solution.py:14
  42.0 15.1 %collective-permute-start.5 = (bf16[128,1,2,64]{3,0,2,1:T(8,128)(2,1)S(1)}, bf16[128,1,2,64]{3,0,2,1:T(8,128)(2,1)S(1)}, u32[]{:S(2)}, u32[]{:S(2)}) collective-permute-start(bf16[128,1,2,64]{3,0,2,1:T(8,128)(2,1)S(1)} %bitcast.576), channel_id=1, source_target_pairs={{16,0},{32,16},{48,32},{64,48},{80,64},{96,80},{112,96},{128,112},... | collective-permute-start | bytes 98312 | tf_op jit(solution)/shard_map/ppermute | solution.py:25
  43.3 16.6 %collective-permute-start.4 = (bf16[128,1,2,64]{3,0,2,1:T(8,128)(2,1)S(1)}, bf16[128,1,2,64]{3,0,2,1:T(8,128)(2,1)S(1)}, u32[]{:S(2)}, u32[]{:S(2)}) collective-permute-start(bf16[128,1,2,64]{3,0,2,1:T(8,128)(2,1)S(1)} %bitcast.577), channel_id=1, source_target_pairs={{0,16},{16,32},{32,48},{48,64},{64,80},{80,96},{96,112},{112,128},... | collective-permute-start | bytes 98312 | tf_op jit(solution)/shard_map/ppermute | solution.py:24
  56.7 7.6 copy-start.5
  56.8 7.6 copy-start.7
  60.0 26.0 %collective-permute-start.6 = (bf16[128,3,1,64]{3,0,2,1:T(8,128)(2,1)S(1)}, bf16[128,3,1,64]{3,0,2,1:T(8,128)(2,1)S(1)}, u32[]{:S(2)}, u32[]{:S(2)}) collective-permute-start(bf16[128,3,1,64]{3,0,2,1:T(8,128)(2,1)S(1)} %get-tuple-element.28), channel_id=1, source_target_pairs={{0,1},{1,2},{2,3},{3,4},{4,5},{5,6},{6,7},{7,8},{8,9},{9,10},{10,1... | collective-permute-start | bytes 147464 | tf_op jit(solution)/shard_map/ppermute | solution.py:24
  61.9 24.1 %collective-permute-start.7 = (bf16[128,3,1,64]{3,0,2,1:T(8,128)(2,1)S(1)}, bf16[128,3,1,64]{3,0,2,1:T(8,128)(2,1)S(1)}, u32[]{:S(2)}, u32[]{:S(2)}) collective-permute-start(bf16[128,3,1,64]{3,0,2,1:T(8,128)(2,1)S(1)} %get-tuple-element.29), channel_id=1, source_target_pairs={{1,0},{2,1},{3,2},{4,3},{5,4},{6,5},{7,6},{8,7},{9,8},{10,9},{11,1... | collective-permute-start | bytes 147464 | tf_op jit(solution)/shard_map/ppermute | solution.py:25
  87.2 19.2 %collective-permute-start.3 = (bf16[128,1,2,64]{0,3,2,1:T(8,128)(2,1)S(1)}, bf16[128,1,2,64]{0,3,2,1:T(8,128)(2,1)S(1)}, u32[]{:S(2)}, u32[]{:S(2)}) collective-permute-start(bf16[128,1,2,64]{0,3,2,1:T(8,128)(2,1)S(1)} %get-tuple-element.31), channel_id=1, source_target_pairs={{16,0},{32,16},{48,32},{64,48},{80,64},{96,80},{112,96},{128,112},... | collective-permute-start | bytes 98312 | tf_op jit(solution)/shard_map/ppermute | solution.py:25
  88.5 17.9 %collective-permute-start.2 = (bf16[128,1,2,64]{0,3,2,1:T(8,128)(2,1)S(1)}, bf16[128,1,2,64]{0,3,2,1:T(8,128)(2,1)S(1)}, u32[]{:S(2)}, u32[]{:S(2)}) collective-permute-start(bf16[128,1,2,64]{0,3,2,1:T(8,128)(2,1)S(1)} %get-tuple-element.31), channel_id=1, source_target_pairs={{0,16},{16,32},{32,48},{48,64},{64,80},{80,96},{96,112},{112,128},... | collective-permute-start | bytes 98312 | tf_op jit(solution)/shard_map/ppermute | solution.py:24
  102.1 15.2 %collective-permute-start.8 = (bf16[128,1,2,64]{0,3,2,1:T(8,128)(2,1)S(1)}, bf16[128,1,2,64]{0,3,2,1:T(8,128)(2,1)S(1)}, u32[]{:S(2)}, u32[]{:S(2)}) collective-permute-start(bf16[128,1,2,64]{0,3,2,1:T(8,128)(2,1)S(1)} %get-tuple-element.30), channel_id=1, source_target_pairs={{16,0},{32,16},{48,32},{64,48},{80,64},{96,80},{112,96},{128,112},... | collective-permute-start | bytes 98312 | tf_op jit(solution)/shard_map/ppermute | solution.py:14
  104.9 18.6 %copy-start.6 = (pred[8,18]{0,1:T(8,128)(4,1)S(1)}, pred[8,18]{0,1:T(8,128)(4,1)}, u32[]{:S(2)}) copy-start(pred[8,18]{0,1:T(8,128)(4,1)} %constant.50) | copy-start | bytes 436
  107.1 848.1 %all-reduce.9.cloned.1.call-start = ((), (), s32[]{:S(2)}) async-start(), calls=%async_computation.2 | async-start | bytes 5308416
  107.9 112.5 %copy-start.2 = (bf16[8,1,32,64]{3,2,1,0:T(8,128)(2,1)S(1)}, bf16[8,1,32,64]{3,2,1,0:T(8,128)(2,1)}, u32[]{:S(2)}) copy-start(bf16[8,1,32,64]{3,2,1,0:T(8,128)(2,1)} %param.7) | copy-start | bytes 98308
  117.2 6.0 collective-permute-start.9
  120.0 4.1 copy-start.3
  220.5 1.6 copy-start.1
  233.5 4.8 copy-start.4
Sparse Core Ops, SparseCore 0:
  107.2 113.1 all-gather.1
  230.6 724.4 all-reduce.8
where the time goes:
time: 1090 us; the launch traced here: 1080 us
  waiting for transfers between devices  827 us (76%)
  blocking collectives  119 us (11%)
  starting transfers between devices  62.8 us (6%)
  local copies, waits for them, and re-layouts  35.7 us (3%)
  matrix products  18.8 us (2%)
  between operations  16.7 us (2%)
    unnamed x3, waiting for transfers between devices  716 us
    unnamed x1, blocking collectives  119 us
    all_gather x1, waiting for transfers between devices, per_device(): whole = lax.all_gather(deep_hidden, 'height', axis=2, tiled=True)  96.4 us
    ppermute x3, starting transfers between devices, extended(): before = lax.ppermute(last, axis, up)  28.1 us
    ppermute x4, starting transfers between devices, passed_along(): return lax.ppermute(block, axis, route)  23.7 us
  transfers between devices with their start and end apart: 13, of which 6 were waited for; matrix products, arithmetic and copies ran while one was open for 4% of the time, Pallas kernels for 0%

commit v1 on v0

v1 whole, which is shorter than its diff:
```python
import math

import jax
import jax.numpy as jnp
from jax import lax
from jax.sharding import Mesh, PartitionSpec as P

SLOPE = 0.2
DEPTH = ("x", "y", "zh")
HEIGHT = ("zl", "core")
PLANE = ("x", "y")
LINE = ("zh", "zl", "core")


def shifted(block, axis, distance):
    size = lax.axis_size(axis)
    route = [(i, i + distance) for i in range(size) if 0 <= i + distance < size]
    return lax.ppermute(block, axis, route)


def conv_local(inputs, kernel, stride, padding, dilation):
    result = lax.conv_general_dilated(
        inputs[None],
        kernel,
        window_strides=(stride, stride, stride),
        padding=padding,
        lhs_dilation=(dilation, dilation, dilation),
        dimension_numbers=("NCDHW", "DHWIO", "NCDHW"),
        preferred_element_type=jnp.float32,
    )
    return result[0]


def flip_swap(kernel):
    return jnp.flip(kernel, (0, 1, 2)).transpose(0, 1, 2, 4, 3)


def weight_grad(padded, cotan, stride):
    cin = padded.shape[0]
    cout = cotan.shape[0]
    sizes = cotan.shape[1:]
    flat_cot = cotan.reshape(cout, -1)
    pieces = []
    for off_d in range(3):
        for off_h in range(3):
            for off_w in range(3):
                starts = (0, off_d, off_h, off_w)
                limits = (
                    cin,
                    off_d + stride * (sizes[0] - 1) + 1,
                    off_h + stride * (sizes[1] - 1) + 1,
                    off_w + stride * (sizes[2] - 1) + 1,
                )
                window = lax.slice(padded, starts, limits, (1, stride, stride, stride))
                pieces.append(window.reshape(cin, -1))
    return lax.dot_general(
        jnp.stack(pieces),
        flat_cot,
        (((2,), (1,)), ((), ())),
        preferred_element_type=jnp.float32,
    )


def plane_sum(partial):
    taps, cin, cout = partial.shape
    parts = lax.axis_size(PLANE)
    sent = partial.astype(jnp.bfloat16).reshape(taps, parts, cin // parts, cout).transpose(1, 0, 2, 3)
    got = lax.all_to_all(sent, PLANE, 0, 0)
    return jnp.sum(got.astype(jnp.float32), axis=0)


def line_pieces(partial):
    taps, cin, cout = partial.shape
    far, near = (lax.axis_size("zh"), lax.axis_size(HEIGHT))
    cut = partial.reshape(taps, far, cin // far, near, cout // near)
    return cut.transpose(1, 3, 0, 2, 4).reshape(far * near, -1)


def per_device(volume, kernel_one, kernel_two, cotangent):
    zero3 = [(0, 0), (0, 0), (0, 0)]
    heights = lax.axis_size(HEIGHT)
    below = shifted(volume[:, -1:], DEPTH, 1)
    deeper = jnp.concatenate([below, volume], axis=1)
    beside = shifted(deeper[:, :, -1:], HEIGHT, 1)
    vol_pad = jnp.pad(jnp.concatenate([beside, deeper], axis=2), ((0, 0), (0, 0), (0, 0), (1, 0)))

    rows = cotangent.shape[2] // heights
    padded = jnp.pad(cotangent[:, 0], ((0, 0), (1, 1), (0, 0)))
    slabs = jnp.stack([padded[:, rows * i : rows * i + rows + 2] for i in range(heights)])
    slab = lax.all_to_all(slabs, HEIGHT, 0, 0)
    slab = slab.reshape((-1, 1) + slab.shape[2:])
    cot_ext = jnp.concatenate([shifted(slab, DEPTH, 1), slab, shifted(slab, DEPTH, -1)], axis=1)
    cot_ext = jnp.pad(cot_ext, ((0, 0), (0, 0), (0, 0), (1, 1)))
    cot_own = slab[:, :, 1:-1]

    act_one = conv_local(vol_pad, kernel_one, 2, zero3, 1)
    hidden = (SLOPE * act_one + (1.0 - SLOPE) * jax.nn.softplus(act_one)).astype(jnp.bfloat16)
    cells = (
        act_one.shape[1]
        * act_one.shape[2]
        * act_one.shape[3]
        * lax.axis_size(DEPTH)
        * lax.axis_size(HEIGHT)
    )
    scale = 1.0 / math.sqrt(cells)

    tall = jnp.concatenate(
        [shifted(hidden[:, :, -1:], HEIGHT, 1), hidden, shifted(hidden[:, :, :1], HEIGHT, -1)], axis=2
    )
    hid_ext = jnp.concatenate([shifted(tall, DEPTH, 1), tall, shifted(tall, DEPTH, -1)], axis=1)
    hid_pad = jnp.pad(hid_ext, ((0, 0), (0, 0), (0, 0), (1, 1)))

    own_next = conv_local(hid_pad, kernel_two, 1, zero3, 1).astype(jnp.bfloat16)
    groups = own_next.shape[0] // heights
    swapped = lax.all_to_all(own_next.reshape((heights, groups) + own_next.shape[1:]), HEIGHT, 0, 0)
    next_acts = swapped.transpose(1, 2, 0, 3, 4).reshape(cotangent.shape)

    two = plane_sum(weight_grad(hid_pad, cot_own, 1))

    hidden_grad = conv_local(cot_ext, flip_swap(kernel_two), 1, zero3, 1)
    act_grad = (hidden_grad * (SLOPE + (1.0 - SLOPE) * jax.nn.sigmoid(act_one))).astype(
        jnp.bfloat16
    )
    one = plane_sum(weight_grad(vol_pad, act_grad, 2))

    taller = jnp.concatenate([act_grad, shifted(act_grad[:, :, :1], HEIGHT, -1)], axis=2)
    grad_ext = jnp.concatenate([taller, shifted(taller, DEPTH, -1)], axis=1)
    volume_grad = conv_local(
        grad_ext, flip_swap(kernel_one), 1, [(1, 0), (1, 0), (1, 2)], 2
    ).astype(jnp.bfloat16)

    pieces = jnp.concatenate([line_pieces(one), line_pieces(two)], axis=1)
    total = jnp.sum(lax.all_to_all(pieces, LINE, 0, 0, tiled=True), axis=0) * scale
    line = lax.axis_size("zh")
    one_shape = (3, 3, 3, one.shape[1] // line, one.shape[2] // heights)
    two_shape = (3, 3, 3, two.shape[1] // line, two.shape[2] // heights)
    cut = math.prod(one_shape)
    return (next_acts, volume_grad, total[:cut].reshape(one_shape), total[cut:].reshape(two_shape))


def solution(mesh):
    fine = Mesh(mesh.devices.reshape(4, 4, 2, 8, 2), DEPTH + HEIGHT)
    placed = (P(None, DEPTH, HEIGHT, None), P(), P(), P(HEIGHT, DEPTH, None, None))
    return jax.shard_map(
        per_device,
        mesh=fine,
        in_specs=placed,
        out_specs=(
            P(HEIGHT, DEPTH, None, None),
            P(None, DEPTH, HEIGHT, None),
            P(None, None, None, DEPTH, HEIGHT),
            P(None, None, None, DEPTH, HEIGHT),
        ),
        check_vma=False,
    )
```

time: 1090 us -> 602 us (0.55)
  waiting for transfers between devices: 827 us -> 42.7 us
  local copies, waits for them, and re-layouts: 35.7 us -> 435 us
  blocking collectives: 119 us -> 0 us
  starting transfers between devices: 62.8 us -> 115 us
  matrix products: 18.8 us -> 2.28 us
  between operations: 16.7 us -> 2.2 us
    unnamed x3 -> x0, waiting for transfers between devices: 716 us -> none
    slice x27 -> x30, local copies, waits for them, and re-layouts: 21 us -> 380 us  [weight_grad(): window = lax.slice(padded, starts, limits, (1, stride, stride, stride))]
    unnamed x1 -> x0, blocking collectives: 119 us -> none
    all_gather x1 -> x0, waiting for transfers between devices: 96.4 us -> none  [per_device(): whole = lax.all_gather(deep_hidden, 'height', axis=2, tiled=True)]
    all_to_all x1 -> x5, starting transfers between devices: 5.99 us -> 52.4 us  [the longest x2 32.6 us: plane_sum(): got = lax.all_to_all(sent, PLANE, 0, 0)]
    all_to_all x1 -> x5, waiting for transfers between devices: 0.78 us -> 32.1 us  [the longest x1 14.6 us: per_device(): lax.all_to_all(pieces, LINE, 0, 0, tiled=True)]
    another operation x0 -> x56, local copies, waits for them, and re-layouts: none -> 26.8 us  [the longest x55 26.8 us: weight_grad(): jnp.stack(pieces)]
    dot_general x54 -> x2, matrix products: 13.2 us -> 0.62 us  [weight_grad(): lax.dot_general(jnp.stack(pieces), flat_cot, (((2,), (1,)), ((), ())), pr...]
  transfers between devices with their start and end apart: 13 -> 15, of which waited for: 6 -> 6; matrix products, arithmetic and copies ran while one was open for 4% -> 72% of each run, Pallas kernels for 0% -> 0%
where the time goes in v1:
time: 602 us; the launch traced here: 600 us
  local copies, waits for them, and re-layouts  435 us (72%)
  starting transfers between devices  115 us (19%)
  waiting for transfers between devices  42.7 us (7%)
    slice x30, local copies, waits for them, and re-layouts, weight_grad(): window = lax.slice(padded, starts, limits, (1, stride, stride, stride))  380 us
    ppermute x10, starting transfers between devices, shifted(): return lax.ppermute(block, axis, route)  62.2 us
    all_to_all x2, starting transfers between devices, plane_sum(): got = lax.all_to_all(sent, PLANE, 0, 0)  32.6 us
    another operation x55, local copies, waits for them, and re-layouts, weight_grad(): jnp.stack(pieces)  26.8 us
    unnamed x141, local copies, waits for them, and re-layouts  16.9 us
    all_to_all x1, waiting for transfers between devices, per_device(): lax.all_to_all(pieces, LINE, 0, 0, tiled=True)  14.6 us
  transfers between devices with their start and end apart: 15, of which 6 were waited for; matrix products, arithmetic and copies ran while one was open for 72% of the time, Pallas kernels for 0%

profile of v1, /device:TPU:1, one launch (start us, length us, event | category | flops | bytes accessed | tf_op | source)
XLA Modules:
  0.0 599.8 jit_solution(15482479200119002136)
XLA Ops:
  1.6 16.3 %collective-permute-start = (bf16[64,1,4,128]{3,2,1,0:T(4,128)(2,1)S(1)}, bf16[64,1,4,128]{3,2,1,0:T(4,128)(2,1)S(1)}, u32[]{:S(2)}, u32[]{:S(2)}) collective-permute-start(bf16[64,1,4,128]{3,2,1,0:T(4,128)(2,1)S(1)} %slice.297), channel_id=1, source_target_pairs={{0,16},{16,32},{32,48},{48,64},{64,80},{80,96},{96,112},{112,128},... | collective-permute-start | bytes 196616 | tf_op jit(solution)/shard_map/ppermute | solution.py:18
  40.0 22.6 %slice.341 = bf16[64,1,2,64]{3,2,1,0:T(2,128)(2,1)} slice(bf16[64,3,5,129]{3,2,1,0:T(8,128)(2,1)S(1)} %get-tuple-element.20), slice={[0:64:1], [2:3:1], [1:4:2], [2:129:2]} | slice | bytes 32768 | tf_op jit(solution)/shard_map/slice | solution.py:54
  62.6 22.5 %slice.340 = bf16[64,1,2,64]{3,2,1,0:T(2,128)(2,1)} slice(bf16[64,3,5,129]{3,2,1,0:T(8,128)(2,1)S(1)} %get-tuple-element.20), slice={[0:64:1], [2:3:1], [1:4:2], [1:128:2]} | slice | bytes 32768 | tf_op jit(solution)/shard_map/slice | solution.py:54
  85.1 22.4 %slice.339 = bf16[64,1,2,64]{3,2,1,0:T(2,128)(2,1)} slice(bf16[64,3,5,129]{3,2,1,0:T(8,128)(2,1)S(1)} %get-tuple-element.20), slice={[0:64:1], [2:3:1], [1:4:2], [0:127:2]} | slice | bytes 32768 | tf_op jit(solution)/shard_map/slice | solution.py:54
  107.5 22.6 %slice.338 = bf16[64,1,2,64]{3,2,1,0:T(2,128)(2,1)} slice(bf16[64,3,5,129]{3,2,1,0:T(8,128)(2,1)S(1)} %get-tuple-element.20), slice={[0:64:1], [2:3:1], [0:3:2], [2:129:2]} | slice | bytes 32768 | tf_op jit(solution)/shard_map/slice | solution.py:54
  130.0 22.5 %slice.337 = bf16[64,1,2,64]{3,2,1,0:T(2,128)(2,1)} slice(bf16[64,3,5,129]{3,2,1,0:T(8,128)(2,1)S(1)} %get-tuple-element.20), slice={[0:64:1], [2:3:1], [0:3:2], [1:128:2]} | slice | bytes 32768 | tf_op jit(solution)/shard_map/slice | solution.py:54
  152.5 22.5 %slice.336 = bf16[64,1,2,64]{3,2,1,0:T(2,128)(2,1)} slice(bf16[64,3,5,129]{3,2,1,0:T(8,128)(2,1)S(1)} %get-tuple-element.20), slice={[0:64:1], [2:3:1], [0:3:2], [0:127:2]} | slice | bytes 32768 | tf_op jit(solution)/shard_map/slice | solution.py:54
  175.0 22.5 %slice.335 = bf16[64,1,2,64]{3,2,1,0:T(2,128)(2,1)} slice(bf16[64,3,5,129]{3,2,1,0:T(8,128)(2,1)S(1)} %get-tuple-element.20), slice={[0:64:1], [1:2:1], [2:5:2], [2:129:2]} | slice | bytes 32768 | tf_op jit(solution)/shard_map/slice | solution.py:54
  197.5 21.2 %slice.334 = bf16[64,1,2,64]{3,2,1,0:T(2,128)(2,1)} slice(bf16[64,3,5,129]{3,2,1,0:T(8,128)(2,1)S(1)} %get-tuple-element.20), slice={[0:64:1], [1:2:1], [2:5:2], [1:128:2]} | slice | bytes 32768 | tf_op jit(solution)/shard_map/slice | solution.py:54
  218.7 21.2 %slice.333 = bf16[64,1,2,64]{3,2,1,0:T(2,128)(2,1)} slice(bf16[64,3,5,129]{3,2,1,0:T(8,128)(2,1)S(1)} %get-tuple-element.20), slice={[0:64:1], [1:2:1], [2:5:2], [0:127:2]} | slice | bytes 32768 | tf_op jit(solution)/shard_map/slice | solution.py:54
  250.0 10.0 %slice.331 = bf16[64,1,2,64]{3,2,1,0:T(2,128)(2,1)S(1)} slice(bf16[64,3,5,129]{3,2,1,0:T(8,128)(2,1)S(1)} %get-tuple-element.20), slice={[0:64:1], [1:2:1], [1:4:2], [1:128:2]} | slice | bytes 32768 | tf_op jit(solution)/shard_map/slice | solution.py:54
  270.0 10.0 %slice.329 = bf16[64,1,2,64]{3,2,1,0:T(2,128)(2,1)S(1)} slice(bf16[64,3,5,129]{3,2,1,0:T(8,128)(2,1)S(1)} %get-tuple-element.20), slice={[0:64:1], [1:2:1], [0:3:2], [2:129:2]} | slice | bytes 32768 | tf_op jit(solution)/shard_map/slice | solution.py:54
  280.1 10.0 %slice.328 = bf16[64,1,2,64]{3,2,1,0:T(2,128)(2,1)S(1)} slice(bf16[64,3,5,129]{3,2,1,0:T(8,128)(2,1)S(1)} %get-tuple-element.20), slice={[0:64:1], [1:2:1], [0:3:2], [1:128:2]} | slice | bytes 32768 | tf_op jit(solution)/shard_map/slice | solution.py:54
  300.1 10.0 %slice.326 = bf16[64,1,2,64]{3,2,1,0:T(2,128)(2,1)S(1)} slice(bf16[64,3,5,129]{3,2,1,0:T(8,128)(2,1)S(1)} %get-tuple-element.20), slice={[0:64:1], [0:1:1], [2:5:2], [2:129:2]} | slice | bytes 32768 | tf_op jit(solution)/shard_map/slice | solution.py:54
  310.2 10.0 %slice.325 = bf16[64,1,2,64]{3,2,1,0:T(2,128)(2,1)S(1)} slice(bf16[64,3,5,129]{3,2,1,0:T(8,128)(2,1)S(1)} %get-tuple-element.20), slice={[0:64:1], [0:1:1], [2:5:2], [1:128:2]} | slice | bytes 32768 | tf_op jit(solution)/shard_map/slice | solution.py:54
  360.3 10.0 %slice.320 = bf16[64,1,2,64]{3,2,1,0:T(2,128)(2,1)S(1)} slice(bf16[64,3,5,129]{3,2,1,0:T(8,128)(2,1)S(1)} %get-tuple-element.20), slice={[0:64:1], [0:1:1], [0:3:2], [2:129:2]} | slice | bytes 32768 | tf_op jit(solution)/shard_map/slice | solution.py:54
  426.7 10.0 %slice.343 = bf16[64,1,2,64]{3,2,1,0:T(2,128)(2,1)S(1)} slice(bf16[64,3,5,129]{3,2,1,0:T(8,128)(2,1)S(1)} %get-tuple-element.20), slice={[0:64:1], [2:3:1], [2:5:2], [1:128:2]} | slice | bytes 32768 | tf_op jit(solution)/shard_map/slice | solution.py:54
  436.7 10.0 %slice.344 = bf16[64,1,2,64]{3,2,1,0:T(2,128)(2,1)S(1)} slice(bf16[64,3,5,129]{3,2,1,0:T(8,128)(2,1)S(1)} %get-tuple-element.20), slice={[0:64:1], [2:3:1], [2:5:2], [2:129:2]} | slice | bytes 32768 | tf_op jit(solution)/shard_map/slice | solution.py:54
  448.8 12.7 %collective-permute-start.6 = (bf16[128,1,4,64]{3,0,2,1:T(8,128)(2,1)S(1)}, bf16[128,1,4,64]{3,0,2,1:T(8,128)(2,1)S(1)}, u32[]{:S(2)}, u32[]{:S(2)}) collective-permute-start(bf16[128,1,4,64]{3,0,2,1:T(8,128)(2,1)S(1)} %bitcast.250), channel_id=1, source_target_pairs={{0,16},{16,32},{32,48},{48,64},{64,80},{80,96},{96,112},{112,128},... | collective-permute-start | bytes 196616 | tf_op jit(solution)/shard_map/ppermute | solution.py:18
  484.4 20.1 %all-to-all-start.2 = ((bf16[16,27,4,128]{3,2,1,0:T(4,128)(2,1)}), bf16[16,27,4,128]{3,2,1,0:T(4,128)(2,1)S(1)}, u32[]{:S(2)}, u32[]{:S(2)}) async-start(bf16[16,27,4,128]{3,2,1,0:T(4,128)(2,1)} %bitcast.225), calls=%async_computation.2 | async-start | bytes 884736 | tf_op jit(solution)/shard_map/all_to_all | solution.py:68
  505.9 12.7 %collective-permute-start.4 = (bf16[128,1,4,64]{0,3,2,1:T(8,128)(2,1)S(1)}, bf16[128,1,4,64]{0,3,2,1:T(8,128)(2,1)S(1)}, u32[]{:S(2)}, u32[]{:S(2)}) collective-permute-start(bf16[128,1,4,64]{0,3,2,1:T(8,128)(2,1)S(1)} %pad_maximum_fusion.1), channel_id=1, source_target_pairs={{0,16},{16,32},{32,48},{48,64},{64,80},{80,96},{96,112},{112,128},... | collective-permute-start | bytes 196616 | tf_op jit(solution)/shard_map/ppermute | solution.py:18
  529.1 12.5 %all-to-all-start.3 = ((bf16[16,27,8,128]{3,2,1,0:T(8,128)(2,1)}), bf16[16,27,8,128]{3,2,1,0:T(8,128)(2,1)S(1)}, u32[]{:S(2)}, u32[]{:S(2)}) async-start(bf16[16,27,8,128]{3,2,1,0:T(8,128)(2,1)} %bitcast.224), calls=%async_computation.3 | async-start | bytes 1769472 | tf_op jit(solution)/shard_map/all_to_all | solution.py:68
  544.3 10.9 %all-to-all-done.3 = bf16[16,27,8,128]{3,2,1,0:T(8,128)(2,1)S(1)} async-done(((bf16[16,27,8,128]{3,2,1,0:T(8,128)(2,1)}), bf16[16,27,8,128]{3,2,1,0:T(8,128)(2,1)S(1)}, u32[]{:S(2)}, u32[]{:S(2)}) %all-to-all-start.3) | async-done | bytes 884768 | tf_op jit(solution)/shard_map/all_to_all | solution.py:68
  583.5 14.6 %all-to-all-done.4 = f32[32,1,1296]{2,1,0:T(1,128)S(1)} async-done(((f32[32,1,1296]{2,1,0:T(1,128)}), f32[32,1,1296]{2,1,0:T(1,128)S(1)}, u32[]{:S(2)}, u32[]{:S(2)}) %all-to-all-start.4) | async-done | bytes 165920 | tf_op jit(solution)/shard_map/all_to_all | solution.py:133
  (303 shorter events, 217.6 us)
Async XLA Ops:
  0.6 469.0 %copy-start = (bf16[3,3,3,128,128]{4,3,2,1,0:T(8,128)(2,1)S(1)}, bf16[3,3,3,128,128]{4,3,2,1,0:T(8,128)(2,1)}, u32[]{:S(2)}) copy-start(bf16[3,3,3,128,128]{4,3,2,1,0:T(8,128)(2,1)} %param.6) | copy-start | bytes 2654212
  0.6 33.2 %copy-start.1 = (bf16[8,1,32,64]{3,2,1,0:T(8,128)(2,1)S(1)}, bf16[8,1,32,64]{3,2,1,0:T(8,128)(2,1)}, u32[]{:S(2)}) copy-start(bf16[8,1,32,64]{3,2,1,0:T(8,128)(2,1)} %param.7) | copy-start | bytes 98308
  1.6 27.6 %collective-permute-start = (bf16[64,1,4,128]{3,2,1,0:T(4,128)(2,1)S(1)}, bf16[64,1,4,128]{3,2,1,0:T(4,128)(2,1)S(1)}, u32[]{:S(2)}, u32[]{:S(2)}) collective-permute-start(bf16[64,1,4,128]{3,2,1,0:T(4,128)(2,1)S(1)} %slice.297), channel_id=1, source_target_pairs={{0,16},{16,32},{32,48},{48,64},{64,80},{80,96},{96,112},{112,128},... | collective-permute-start | bytes 196616 | tf_op jit(solution)/shard_map/ppermute | solution.py:18
  30.3 9.0 %collective-permute-start.1 = (bf16[64,3,1,128]{3,2,1,0:T(2,128)(2,1)S(1)}, bf16[64,3,1,128]{3,2,1,0:T(2,128)(2,1)S(1)}, u32[]{:S(2)}, u32[]{:S(2)}) collective-permute-start(bf16[64,3,1,128]{3,2,1,0:T(2,128)(2,1)S(1)} %slice.384), channel_id=1, source_target_pairs={{0,1},{1,2},{2,3},{3,4},{4,5},{5,6},{6,7},{7,8},{8,9},{9,10},{10,1... | collective-permute-start | bytes 147464 | tf_op jit(solution)/shard_map/ppermute | solution.py:18
  34.6 412.7 %all-to-all-start.1 = ((bf16[16,2,1024]{2,1,0:T(2,128)(2,1)}), bf16[16,2,1024]{2,1,0:T(2,128)(2,1)S(1)}, u32[]{:S(2)}, u32[]{:S(2)}) async-start(bf16[16,2,1024]{2,1,0:T(2,128)(2,1)} %reshape.327), calls=%async_computation.1 | async-start | bytes 131072 | tf_op jit(solution)/shard_map/all_to_all | solution.py:90
  414.8 1.0 copy-start.4
  414.8 1.0 copy-start.3
  414.8 1.1 copy-start.26
  414.8 1.1 copy-start.29
  447.5 15.7 %collective-permute-start.7 = (bf16[128,1,4,64]{3,0,2,1:T(8,128)(2,1)S(1)}, bf16[128,1,4,64]{3,0,2,1:T(8,128)(2,1)S(1)}, u32[]{:S(2)}, u32[]{:S(2)}) collective-permute-start(bf16[128,1,4,64]{3,0,2,1:T(8,128)(2,1)S(1)} %bitcast.249), channel_id=1, source_target_pairs={{16,0},{32,16},{48,32},{64,48},{80,64},{96,80},{112,96},{128,112},... | collective-permute-start | bytes 196616 | tf_op jit(solution)/shard_map/ppermute | solution.py:18
  448.8 20.2 %collective-permute-start.6 = (bf16[128,1,4,64]{3,0,2,1:T(8,128)(2,1)S(1)}, bf16[128,1,4,64]{3,0,2,1:T(8,128)(2,1)S(1)}, u32[]{:S(2)}, u32[]{:S(2)}) collective-permute-start(bf16[128,1,4,64]{3,0,2,1:T(8,128)(2,1)S(1)} %bitcast.250), channel_id=1, source_target_pairs={{0,16},{16,32},{32,48},{48,64},{64,80},{80,96},{96,112},{112,128},... | collective-permute-start | bytes 196616 | tf_op jit(solution)/shard_map/ppermute | solution.py:18
  470.2 48.4 %collective-permute-start.8 = (bf16[128,1,1,64]{0,3,2,1:T(8,128)(2,1)S(1)}, bf16[128,1,1,64]{0,3,2,1:T(8,128)(2,1)S(1)}, u32[]{:S(2)}, u32[]{:S(2)}) collective-permute-start(bf16[128,1,1,64]{0,3,2,1:T(8,128)(2,1)S(1)} %slice.407), channel_id=1, source_target_pairs={{1,0},{2,1},{3,2},{4,3},{5,4},{6,5},{7,6},{8,7},{9,8},{10,9},{11,1... | collective-permute-start | bytes 49160 | tf_op jit(solution)/shard_map/ppermute | solution.py:18
  473.5 31.0 %collective-permute-start.2 = (bf16[128,1,1,64]{0,3,2,1:T(8,128)(2,1)S(1)}, bf16[128,1,1,64]{0,3,2,1:T(8,128)(2,1)S(1)}, u32[]{:S(2)}, u32[]{:S(2)}) collective-permute-start(bf16[128,1,1,64]{0,3,2,1:T(8,128)(2,1)S(1)} %get-tuple-element.50), channel_id=1, source_target_pairs={{0,1},{1,2},{2,3},{3,4},{4,5},{5,6},{6,7},{7,8},{8,9},{9,10},{10,1... | collective-permute-start | bytes 49160 | tf_op jit(solution)/shard_map/ppermute | solution.py:18
  481.3 23.2 %collective-permute-start.3 = (bf16[128,1,1,64]{0,3,2,1:T(8,128)(2,1)S(1)}, bf16[128,1,1,64]{0,3,2,1:T(8,128)(2,1)S(1)}, u32[]{:S(2)}, u32[]{:S(2)}) collective-permute-start(bf16[128,1,1,64]{0,3,2,1:T(8,128)(2,1)S(1)} %get-tuple-element.51), channel_id=1, source_target_pairs={{1,0},{2,1},{3,2},{4,3},{5,4},{6,5},{7,6},{8,7},{9,8},{10,9},{11,1... | collective-permute-start | bytes 49160 | tf_op jit(solution)/shard_map/ppermute | solution.py:18
  484.4 44.6 %all-to-all-start.2 = ((bf16[16,27,4,128]{3,2,1,0:T(4,128)(2,1)}), bf16[16,27,4,128]{3,2,1,0:T(4,128)(2,1)S(1)}, u32[]{:S(2)}, u32[]{:S(2)}) async-start(bf16[16,27,4,128]{3,2,1,0:T(4,128)(2,1)} %bitcast.225), calls=%async_computation.2 | async-start | bytes 884736 | tf_op jit(solution)/shard_map/all_to_all | solution.py:68
  504.6 19.4 %collective-permute-start.5 = (bf16[128,1,4,64]{0,3,2,1:T(8,128)(2,1)S(1)}, bf16[128,1,4,64]{0,3,2,1:T(8,128)(2,1)S(1)}, u32[]{:S(2)}, u32[]{:S(2)}) collective-permute-start(bf16[128,1,4,64]{0,3,2,1:T(8,128)(2,1)S(1)} %pad_maximum_fusion.1), channel_id=1, source_target_pairs={{16,0},{32,16},{48,32},{64,48},{80,64},{96,80},{112,96},{128,112},... | collective-permute-start | bytes 196616 | tf_op jit(solution)/shard_map/ppermute | solution.py:18
  505.9 17.7 %collective-permute-start.4 = (bf16[128,1,4,64]{0,3,2,1:T(8,128)(2,1)S(1)}, bf16[128,1,4,64]{0,3,2,1:T(8,128)(2,1)S(1)}, u32[]{:S(2)}, u32[]{:S(2)}) collective-permute-start(bf16[128,1,4,64]{0,3,2,1:T(8,128)(2,1)S(1)} %pad_maximum_fusion.1), channel_id=1, source_target_pairs={{0,16},{16,32},{32,48},{48,64},{64,80},{80,96},{96,112},{112,128},... | collective-permute-start | bytes 196616 | tf_op jit(solution)/shard_map/ppermute | solution.py:18
  518.6 61.5 %collective-permute-start.9 = (bf16[128,1,3,64]{0,3,2,1:T(8,128)(2,1)S(1)}, bf16[128,1,3,64]{0,3,2,1:T(8,128)(2,1)}, u32[]{:S(2)}, u32[]{:S(2)}) collective-permute-start(bf16[128,1,3,64]{0,3,2,1:T(8,128)(2,1)S(1)} %pad_maximum_fusion.2), channel_id=1, source_target_pairs={{16,0},{32,16},{48,32},{64,48},{80,64},{96,80},{112,96},{128,112},... | collective-permute-start | bytes 147464 | tf_op jit(solution)/shard_map/ppermute | solution.py:18
  529.1 12.5 %copy-start.30 = (pred[8,9]{0,1:T(8,128)(4,1)S(1)}, pred[8,9]{0,1:T(8,128)(4,1)}, u32[]{:S(2)}) copy-start(pred[8,9]{0,1:T(8,128)(4,1)} %constant.41) | copy-start | bytes 220
  529.1 26.1 %all-to-all-start.3 = ((bf16[16,27,8,128]{3,2,1,0:T(8,128)(2,1)}), bf16[16,27,8,128]{3,2,1,0:T(8,128)(2,1)S(1)}, u32[]{:S(2)}, u32[]{:S(2)}) async-start(bf16[16,27,8,128]{3,2,1,0:T(8,128)(2,1)} %bitcast.224), calls=%async_computation.3 | async-start | bytes 1769472 | tf_op jit(solution)/shard_map/all_to_all | solution.py:68
  555.2 18.3 %all-to-all-start = ((bf16[16,2,512]{2,1,0:T(2,128)(2,1)}), bf16[16,2,512]{2,1,0:T(2,128)(2,1)S(1)}, u32[]{:S(2)}, u32[]{:S(2)}) async-start(bf16[16,2,512]{2,1,0:T(2,128)(2,1)} %reshape.325), calls=%async_computation | async-start | bytes 65536 | tf_op jit(solution)/shard_map/all_to_all | solution.py:115
  566.0 15.3 %copy-start.27 = (bf16[3,3,3,64,128]{4,3,2,1,0:T(8,128)(2,1)S(1)}, bf16[3,3,3,64,128]{4,3,2,1,0:T(8,128)(2,1)}, u32[]{:S(2)}) copy-start(bf16[3,3,3,64,128]{4,3,2,1,0:T(8,128)(2,1)} %param.5) | copy-start | bytes 1327108
  566.0 15.3 %copy-start.28 = (pred[8,18]{0,1:T(8,128)(4,1)S(1)}, pred[8,18]{0,1:T(8,128)(4,1)}, u32[]{:S(2)}) copy-start(pred[8,18]{0,1:T(8,128)(4,1)} %constant.43) | copy-start | bytes 436
  573.5 24.6 %all-to-all-start.4 = ((f32[32,1,1296]{2,1,0:T(1,128)}), f32[32,1,1296]{2,1,0:T(1,128)S(1)}, u32[]{:S(2)}, u32[]{:S(2)}) async-start(f32[32,1,1296]{2,1,0:T(1,128)} %all_to_all.22), calls=%async_computation.4 | async-start | bytes 360448 | tf_op jit(solution)/shard_map/all_to_all | solution.py:133
  (22 other events, 17.9 us)

commit v2 on v1

v2 whole, which is shorter than its diff:
```python
import functools
import math

import jax
import jax.numpy as jnp
from jax import lax
from jax.experimental import pallas as pl
from jax.experimental.pallas import tpu as pltpu
from jax.sharding import Mesh, PartitionSpec as P

SLOPE = 0.2
DEPTH = ("x", "y", "zh")
HEIGHT = ("zl", "core")
PLANE = ("x", "y")
LINE = ("zh", "zl", "core")
BF = jnp.bfloat16
F32 = jnp.float32
PAIRS = tuple((a, b) for a in range(3) for b in range(3))


def dot(a, b, ca=1, cb=0):
    return lax.dot_general(a, b, (((ca,), (cb,)), ((), ())), preferred_element_type=F32)


def iota(shape, dim):
    return lax.broadcasted_iota(jnp.int32, shape, dim)


def one_hot(mask):
    return jnp.where(mask, 1.0, 0.0).astype(BF)


def earlier(x):
    return jnp.where(iota(x.shape, 0) % 64 == 0, 0.0, pltpu.roll(x, 1, 0))


def later(x):
    return jnp.where(iota(x.shape, 0) % 64 == 63, 0.0, pltpu.roll(x, x.shape[0] - 1, 0))


def call(body, outs, *args, scalars=0):
    smem = pl.BlockSpec(memory_space=pltpu.SMEM)
    vmem = pl.BlockSpec(memory_space=pltpu.VMEM)
    many = isinstance(outs, list)
    return pl.pallas_call(
        body,
        out_shape=outs,
        in_specs=[smem] * scalars + [vmem] * (len(args) - scalars),
        out_specs=[vmem] * len(outs) if many else vmem,
        compiler_params=pltpu.CompilerParams(vmem_limit_bytes=48 * 1024 * 1024),
    )(*args)


def prep_body(vol_ref, cot_ref, volt_ref, slab_ref):
    shape = (512, 512)
    to, of = iota(shape, 0), iota(shape, 1)
    rows = dot(one_hot(of == (to % 64) * 8 + to // 64), vol_ref[...]).astype(BF)
    half = (64, 128)
    even = one_hot(iota(half, 1) == 2 * iota(half, 0))
    odd = one_hot(iota(half, 1) == 2 * iota(half, 0) + 1)
    zero = jnp.zeros((64, 128), BF)
    for i in range(8):
        block = rows[64 * i : 64 * i + 64]
        left = jnp.concatenate([block, zero], axis=0)
        right = jnp.concatenate([zero, block], axis=0)
        volt_ref[i // 4, i % 4] = (dot(even, left, 1, 1) + dot(odd, right, 1, 1)).astype(BF)
    for i in range(16):
        for j in range(3):
            pair = i + j - 1
            if 0 <= pair < 16:
                piece = cot_ref[:, 128 * pair : 128 * pair + 128]
            else:
                piece = jnp.zeros((8, 128), BF)
            slab_ref[i, :, 128 * j : 128 * j + 128] = piece
            slab_ref[16 + i, :, 128 * j : 128 * j + 128] = piece


def turn_body(got_ref, out_ref):
    eye = one_hot(iota((128, 128), 0) == iota((128, 128), 1))
    for q in range(2):
        for j in range(3):
            block = got_ref[128 * q : 128 * q + 128, 128 * j : 128 * j + 128]
            turned = dot(eye, block, 1, 1).astype(BF)
            out_ref[q, 2 * j] = turned[:64]
            out_ref[q, 2 * j + 1] = turned[64:]


def conv_one_body(h_ref, v_ref, k_ref, act_ref, hid_ref):
    acc = jnp.zeros((512, 256), F32)
    for i, (a, b) in enumerate(PAIRS):
        x = jnp.concatenate([v_ref[2 * q + a, 2 * r + b] for q in range(2) for r in range(4)], axis=0)
        taps = k_ref[i]
        right = jnp.concatenate([jnp.zeros((64, 128), BF), taps[:64]], axis=0)
        acc += dot(x, jnp.concatenate([taps[64:], right], axis=1))
    act = acc[:, :128] + earlier(acc[:, 128:])
    soft = jnp.maximum(act, 0.0) + jnp.log1p(jnp.exp(-jnp.abs(act)))
    hidden = SLOPE * act + (1.0 - SLOPE) * soft
    row = iota((512, 128), 0) // 64 % 4 + 2 * h_ref[0] - 1
    hidden = jnp.where((row >= 0) & (row < 32), hidden, 0.0).astype(BF)
    for q in range(2):
        for r in range(4):
            at = 64 * (4 * q + r)
            act_ref[q, r] = act[at : at + 64]
            hid_ref[q, r] = hidden[at : at + 64]


def grads_body(s_ref, c_ref, k_ref, act_ref, hid_ref, v_ref, ag_ref, out_ref):
    h, zh = s_ref[0], s_ref[1]
    acc = jnp.zeros((384, 384), F32)
    for a, b in PAIRS:
        x = jnp.concatenate(
            [c_ref[q + a, r + 1 + b] for q in range(2) for r in range(3)], axis=0
        )
        acc += dot(x, k_ref[3 * (2 - a) + 2 - b], 1, 1)
    grad = acc[:, 128:256] + earlier(acc[:, 256:]) + later(acc[:, :128])
    act = jnp.concatenate([act_ref[q, r + 1] for q in range(2) for r in range(3)], axis=0)
    small = jnp.exp(-jnp.abs(act))
    sigmoid = jnp.where(act >= 0.0, 1.0, small) / (1.0 + small)
    grad = grad * (SLOPE + (1.0 - SLOPE) * sigmoid)
    row = iota((384, 128), 0) // 64 % 3 + 2 * h
    ag = jnp.where(row < 32, grad, 0.0).astype(BF)
    for q in range(2):
        for r in range(3):
            at = 64 * (3 * q + r)
            ag_ref[q, r] = ag[at : at + 64]
    own_ag = jnp.concatenate([ag[:128], ag[192:320]], axis=0)

    lane = iota((128, 256), 1)
    source = iota((128, 256), 0)
    device, slot = lane // 16, lane % 16
    pick_two = one_hot((slot < 12) & (source == device * 8 + zh * 4 + slot % 4))
    own_hid = jnp.concatenate([hid_ref[q, r + 1] for q in range(2) for r in range(2)], axis=0)
    flat = dot(own_hid, pick_two)
    tap = iota((256, 256), 1) % 16 // 4
    hid_rows = jnp.where(tap == 0, earlier(flat), jnp.where(tap == 1, flat, later(flat))).astype(BF)
    pick_one = one_hot(
        (slot >= 12) & (source == (slot - 12) // 2 * 64 + device * 4 + zh * 2 + slot % 2)
    )
    first = jnp.zeros((256, 256), F32)
    last = None
    for i, (a, b) in enumerate(PAIRS):
        x = jnp.concatenate(
            [v_ref[2 * q + a, 2 * r + 2 + b] for q in range(2) for r in range(2)], axis=0
        )
        vol_rows = dot(x, pick_one).astype(BF)
        cot = jnp.concatenate(
            [c_ref[q + 2 - a, r + 3 - b] for q in range(2) for r in range(2)], axis=0
        )
        both = dot(hid_rows, cot, 0, 0) + dot(vol_rows, own_ag, 0, 0)
        out_ref[:, :, 128 * i : 128 * i + 128] = both.astype(BF).reshape(16, 16, 128)
        here = one_hot(
            (slot // 2 == i % 8) & (source == 64 + device * 4 + zh * 2 + slot % 2)
        )
        picked = dot(x, here)
        if i < 8:
            first += picked
        else:
            last = picked
    for i, rows in ((9, first), (10, last)):
        part = dot(earlier(rows).astype(BF), own_ag, 0, 0)
        out_ref[:, :, 128 * i : 128 * i + 128] = part.astype(BF).reshape(16, 16, 128)


def conv_two_body(h_ref, k_ref, out_ref):
    acc = jnp.zeros((128, 128), F32)
    for i, (a, b) in enumerate(PAIRS):
        x = jnp.concatenate([h_ref[a, b], h_ref[a, b + 1]], axis=0)
        wide = x.astype(F32)
        taps = jnp.concatenate([earlier(wide).astype(BF), x, later(wide).astype(BF)], axis=1)
        acc += dot(taps, k_ref[i])
    out_ref[...] = acc.T.astype(BF)


def volume_grad_body(a_ref, k_ref, out_ref):
    zero = jnp.zeros((64, 128), BF)
    half = (64, 256)
    spread = one_hot(iota(half, 1) % 128 == 2 * iota(half, 0) + iota(half, 1) // 128)
    offsets = (((1, 0),), ((0, 1), (2, 0)))
    blocks = [None] * 8
    for pi in range(2):
        for pj in range(2):
            acc = jnp.zeros((128, 256), F32)
            for a, plane in offsets[pi]:
                for b, row in offsets[pj]:
                    x = jnp.concatenate([a_ref[plane, row], a_ref[plane, row + 1]], axis=0)
                    taps = k_ref[3 * a + b]
                    weights = jnp.concatenate([taps[64:], zero, taps[:64]], axis=0)
                    acc += dot(x, weights, 1, 1)
            cells = (acc[:, :128] + later(acc[:, 128:])).astype(BF)
            for r in range(2):
                wide = dot(cells[64 * r : 64 * r + 64], spread, 0, 0)
                blocks[4 * pi + 2 * r + pj] = (wide[:64, :128] + wide[64:, 128:]).astype(BF)
    shape = (512, 512)
    to, of = iota(shape, 0), iota(shape, 1)
    turn = one_hot(of == (to % 8) * 64 + to // 8)
    out_ref[...] = dot(turn, jnp.concatenate(blocks, axis=0)).astype(BF)


def plane_sum_body(got_ref, out_ref):
    total = got_ref[0].astype(F32)
    for i in range(1, 16):
        total += got_ref[i].astype(F32)
    pieces = [total[:, 128 * j : 128 * j + 128] for j in range(11)]
    rows = jnp.concatenate(pieces + [jnp.zeros((80, 128), F32)], axis=0)
    out_ref[...] = rows.T


def line_sum_body(scale, got_ref, out_ref):
    total = got_ref[0]
    for i in range(1, 16):
        total += got_ref[i]
    out_ref[...] = total * scale


def shifted(block, axis, distance):
    size = lax.axis_size(axis)
    route = [(i, i + distance) for i in range(size) if 0 <= i + distance < size]
    return lax.ppermute(block, axis, route)


def shape(dims, kind=BF):
    return jax.ShapeDtypeStruct(dims, kind)


def per_device(volume, kernel_one, kernel_two, cotangent):
    zh = lax.axis_index("zh")
    h = lax.axis_index(HEIGHT)
    here = jnp.stack([h, zh]).astype(jnp.int32)
    one = kernel_one.reshape(9, 192, 128)
    two = kernel_two.reshape(9, 384, 128)
    planes = lax.axis_size(PLANE)

    own, slabs = call(
        prep_body,
        [shape((2, 4, 64, 128)), shape((32, 8, 384))],
        volume.reshape(512, 128),
        cotangent.reshape(8, 2048),
    )
    other = lax.ppermute(own, "zh", [(0, 1), (1, 0)])
    slab = lax.all_to_all(slabs, LINE, 0, 0, tiled=True)
    low = jnp.where(zh == 0, own, other)
    high = jnp.where(zh == 0, other, own)
    deep = jnp.concatenate([shifted(high[1:], PLANE, 1), low, high], axis=0)
    vol = jnp.concatenate(
        [shifted(deep[:, 1:], HEIGHT, 1), deep, shifted(deep[:, :2], HEIGHT, -1)], axis=1
    )
    cot = call(turn_body, shape((2, 6, 64, 128)), slab.reshape(256, 384))
    cot = jnp.concatenate([shifted(cot[1:], PLANE, 1), cot, shifted(cot[:1], PLANE, -1)], axis=0)

    act, hidden = call(
        conv_one_body,
        [shape((2, 4, 64, 128), F32), shape((2, 4, 64, 128))],
        here,
        vol,
        one,
        scalars=1,
    )
    ag, partial = call(
        grads_body,
        [shape((2, 3, 64, 128)), shape((16, 16, 1408))],
        here,
        cot,
        two,
        act,
        hidden,
        vol,
        scalars=1,
    )
    parts = lax.all_to_all(partial, PLANE, 0, 0, tiled=True)

    up = [(2 * k, 2 * k + 2) for k in range(planes - 1)]
    down = [(2 * k + 1, 2 * k - 1) for k in range(1, planes)]
    edge = lax.ppermute(jnp.where(zh == 0, hidden[1:], hidden[:1]), DEPTH, up + down)
    three = jnp.where(
        zh == 0, jnp.concatenate([edge, hidden], axis=0), jnp.concatenate([hidden, edge], axis=0)
    )
    next_own = call(conv_two_body, shape((128, 128)), three, two)
    swapped = lax.all_to_all(next_own.reshape(16, 8, 128), HEIGHT, 0, 0, tiled=True)
    next_acts = swapped.reshape(16, 8, 2, 64).transpose(1, 0, 2, 3).reshape(cotangent.shape)

    after = lax.ppermute(ag[:1], DEPTH, down)
    pair = jnp.where(zh == 0, ag, jnp.concatenate([ag[1:], after], axis=0))
    volume_grad = call(volume_grad_body, shape((512, 128)), pair, one).reshape(volume.shape)

    summed = call(plane_sum_body, shape((128, 256), F32), parts)
    rows = lax.all_to_all(summed.reshape(16, 8, 256), HEIGHT, 0, 0, tiled=True)
    total = call(functools.partial(line_sum_body, 1.0 / math.sqrt(65536)), shape((8, 256), F32), rows)
    table = total.T
    slots = table[:144].reshape(9, 16, 8)
    two_grad = slots[:, :12].reshape(3, 3, 3, 4, 8)
    before = table[144:162].reshape(9, 1, 2, 8)
    one_grad = jnp.concatenate([before, slots[:, 12:].reshape(9, 2, 2, 8)], axis=1)
    return (next_acts, volume_grad, one_grad.reshape(3, 3, 3, 2, 8), two_grad)


def solution(mesh):
    fine = Mesh(mesh.devices.reshape(4, 4, 2, 8, 2), DEPTH + HEIGHT)
    placed = (P(None, DEPTH, HEIGHT, None), P(), P(), P(HEIGHT, DEPTH, None, None))
    return jax.shard_map(
        per_device,
        mesh=fine,
        in_specs=placed,
        out_specs=(
            P(HEIGHT, DEPTH, None, None),
            P(None, DEPTH, HEIGHT, None),
            P(None, None, None, DEPTH, HEIGHT),
            P(None, None, None, DEPTH, HEIGHT),
        ),
        check_vma=False,
    )
```

time: 602 us -> 134 us (0.22)
  local copies, waits for them, and re-layouts: 435 us -> 3.96 us
  starting transfers between devices: 115 us -> 66.9 us
  Pallas kernels: 0 us -> 11.9 us
  waiting for transfers between devices: 42.7 us -> 49 us
    slice x39 -> x10, local copies, waits for them, and re-layouts: 382 us -> 0.57 us  [the longest x2 0.22 us: per_device(): slots[:, 12:].reshape(9, 2, 2, 8)]
    ppermute x10 -> x5, starting transfers between devices: 62.2 us -> 14 us  [shifted(): return lax.ppermute(block, axis, route)]
    another operation x56 -> x0, local copies, waits for them, and re-layouts: 26.8 us -> none  [the longest x55 26.8 us: weight_grad(): jnp.stack(pieces)]
    ppermute x0 -> x3, waiting for transfers between devices: none -> 25.5 us  [the longest x1 18.9 us: per_device(): other = lax.ppermute(own, 'zh', [(0, 1), (1, 0)])]
    unnamed x141 -> x6, local copies, waits for them, and re-layouts: 16.9 us -> 0.91 us
    ppermute x0 -> x3, starting transfers between devices: none -> 15.9 us  [the longest x1 12 us: per_device(): other = lax.ppermute(own, 'zh', [(0, 1), (1, 0)])]
    all_to_all x5 -> x4, starting transfers between devices: 52.4 us -> 36.9 us  [the longest x1 16.8 us: per_device(): slab = lax.all_to_all(slabs, LINE, 0, 0, tiled=True)]
    all_to_all x5 -> x4, waiting for transfers between devices: 32.1 us -> 19.3 us  [the longest x1 9.11 us: per_device(): lax.all_to_all(next_own.reshape(16, 8, 128), HEIGHT, 0, 0, tiled=True)]
  transfers between devices with their start and end apart: 15 -> 12, of which waited for: 6 -> 7; matrix products, arithmetic and copies ran while one was open for 72% -> 1% of each run, Pallas kernels for 0% -> 4%
where the time goes in v2:
time: 134 us
  starting transfers between devices  66.9 us (50%)
  waiting for transfers between devices  49 us (37%)
  Pallas kernels  11.9 us (9%)
  local copies, waits for them, and re-layouts  3.96 us (3%)
    ppermute x1, waiting for transfers between devices, per_device(): other = lax.ppermute(own, 'zh', [(0, 1), (1, 0)])  18.9 us
    all_to_all x1, starting transfers between devices, per_device(): slab = lax.all_to_all(slabs, LINE, 0, 0, tiled=True)  16.8 us
    ppermute x5, starting transfers between devices, shifted(): return lax.ppermute(block, axis, route)  14 us
    ppermute x1, starting transfers between devices, per_device(): other = lax.ppermute(own, 'zh', [(0, 1), (1, 0)])  12 us
    pallas_call x8, Pallas kernels, call(): pl.pallas_call(body, out_shape=outs, in_specs=[smem] * scalars + [vmem] *...  11.9 us
    all_to_all x1, starting transfers between devices, per_device(): parts = lax.all_to_all(partial, PLANE, 0, 0, tiled=True)  10.1 us
    all_to_all x1, waiting for transfers between devices, per_device(): lax.all_to_all(next_own.reshape(16, 8, 128), HEIGHT, 0, 0, tiled=True)  9.11 us
    all_to_all x1, waiting for transfers between devices, per_device(): rows = lax.all_to_all(summed.reshape(16, 8, 256), HEIGHT, 0, 0, tiled=True)  9.06 us
  transfers between devices with their start and end apart: 12, of which 7 were waited for; matrix products, arithmetic and copies ran while one was open for 1% of the time, Pallas kernels for 4%

profile of v2, /device:TPU:1, one launch (start us, length us, event | category | flops | bytes accessed | tf_op | source)
XLA Modules:
  0.0 133.5 jit_solution(5473777744869116294)
XLA Ops:
  0.6 1.0 reshape.52.cot_ref
  2.5 1.2 shard_map.75
  3.7 16.8 %all-to-all-start.1 = ((bf16[32,8,384]{2,1,0:T(8,128)(2,1)}), bf16[32,8,384]{2,1,0:T(8,128)(2,1)S(1)}, u32[]{:S(2)}, u32[]{:S(2)}) async-start(bf16[32,8,384]{2,1,0:T(8,128)(2,1)} %get-tuple-element.12), calls=%async_computation.1 | async-start | bytes 393216 | tf_op jit(solution)/shard_map/all_to_all | solution.py:240
  20.5 12.0 %collective-permute-start = (bf16[2,4,64,128]{3,2,1,0:T(8,128)(2,1)S(1)}, bf16[2,4,64,128]{3,2,1,0:T(8,128)(2,1)S(1)}, u32[]{:S(2)}, u32[]{:S(2)}) collective-permute-start(bf16[2,4,64,128]{3,2,1,0:T(8,128)(2,1)S(1)} %get-tuple-element.10), channel_id=1, source_target_pairs={{0,16},{16,0},{1,17},{17,1},{2,18},{18,2},{3,19},{19,3},{4,20},{20... | collective-permute-start | bytes 393224 | tf_op jit(solution)/shard_map/ppermute | solution.py:239
  32.5 18.9 %collective-permute-done = bf16[2,4,64,128]{3,2,1,0:T(8,128)(2,1)S(1)} collective-permute-done((bf16[2,4,64,128]{3,2,1,0:T(8,128)(2,1)S(1)}, bf16[2,4,64,128]{3,2,1,0:T(8,128)(2,1)S(1)}, u32[]{:S(2)}, u32[]{:S(2)}) %collective-permute-start) | collective-permute-done | bytes 131104 | tf_op jit(solution)/shard_map/ppermute | solution.py:239
  51.5 3.2 %collective-permute-start.1 = (bf16[1,4,64,128]{3,2,1,0:T(8,128)(2,1)S(1)}, bf16[1,4,64,128]{3,2,1,0:T(8,128)(2,1)S(1)}, u32[]{:S(2)}, u32[]{:S(2)}) collective-permute-start(bf16[1,4,64,128]{3,2,1,0:T(8,128)(2,1)S(1)} %slice.52), channel_id=1, source_target_pairs={{0,32},{32,64},{64,96},{96,128},{128,160},{160,192},{192,224},{224... | collective-permute-start | bytes 196616 | tf_op jit(solution)/shard_map/ppermute | solution.py:218
  54.7 1.3 collective-permute-done.1
  56.1 3.5 %collective-permute-start.2 = (bf16[5,3,64,128]{3,2,1,0:T(8,128)(2,1)S(1)}, bf16[5,3,64,128]{3,2,1,0:T(8,128)(2,1)S(1)}, u32[]{:S(2)}, u32[]{:S(2)}) collective-permute-start(bf16[5,3,64,128]{3,2,1,0:T(8,128)(2,1)S(1)} %slice.53), channel_id=1, source_target_pairs={{0,1},{1,2},{2,3},{3,4},{4,5},{5,6},{6,7},{7,8},{8,9},{9,10},{10,1... | collective-permute-start | bytes 737288 | tf_op jit(solution)/shard_map/ppermute | solution.py:218
  59.7 1.9 %collective-permute-start.3 = (bf16[5,2,64,128]{3,2,1,0:T(8,128)(2,1)S(1)}, bf16[5,2,64,128]{3,2,1,0:T(8,128)(2,1)S(1)}, u32[]{:S(2)}, u32[]{:S(2)}) collective-permute-start(bf16[5,2,64,128]{3,2,1,0:T(8,128)(2,1)S(1)} %slice.54), channel_id=1, source_target_pairs={{1,0},{2,1},{3,2},{4,3},{5,4},{6,5},{7,6},{8,7},{9,8},{10,9},{11,1... | collective-permute-start | bytes 491528 | tf_op jit(solution)/shard_map/ppermute | solution.py:218
  61.9 4.0 %collective-permute-start.5 = (bf16[1,6,64,128]{3,2,1,0:T(8,128)(2,1)S(1)}, bf16[1,6,64,128]{3,2,1,0:T(8,128)(2,1)S(1)}, u32[]{:S(2)}, u32[]{:S(2)}) collective-permute-start(bf16[1,6,64,128]{3,2,1,0:T(8,128)(2,1)S(1)} %get-tuple-element.18), channel_id=1, source_target_pairs={{0,32},{32,64},{64,96},{96,128},{128,160},{160,192},{192,224},{224... | collective-permute-start | bytes 294920 | tf_op jit(solution)/shard_map/ppermute | solution.py:218
  65.9 1.4 %collective-permute-start.6 = (bf16[1,6,64,128]{3,2,1,0:T(8,128)(2,1)S(1)}, bf16[1,6,64,128]{3,2,1,0:T(8,128)(2,1)S(1)}, u32[]{:S(2)}, u32[]{:S(2)}) collective-permute-start(bf16[1,6,64,128]{3,2,1,0:T(8,128)(2,1)S(1)} %get-tuple-element.19), channel_id=1, source_target_pairs={{32,0},{64,32},{96,64},{128,96},{160,128},{192,160},{224,192},{256... | collective-permute-start | bytes 294920 | tf_op jit(solution)/shard_map/ppermute | solution.py:218
  67.5 1.5 %shard_map.76 = (f32[2,4,64,128]{3,2,1,0:T(8,128)S(1)}, bf16[2,4,64,128]{3,2,1,0:T(8,128)(2,1)S(1)}) custom-call(s32[2]{0:T(128)S(1)} %pad_add_fusion.h_ref.s_ref, bf16[5,9,64,128]{3,2,1,0:T(8,128)(2,1)S(1)} %pad_maximum_fusion.v_ref, bf16[9,192,128]{2,1,0:T(8,128)(2,1)S(1)} %bitcast.23), custom_call_target="tpu_custom_call" | custom-call | tf_op jit(solution)/shard_map/pallas_call | solution.py:45
  69.0 2.8 %collective-permute-done.6 = bf16[1,6,64,128]{3,2,1,0:T(8,128)(2,1)S(1)} collective-permute-done((bf16[1,6,64,128]{3,2,1,0:T(8,128)(2,1)S(1)}, bf16[1,6,64,128]{3,2,1,0:T(8,128)(2,1)S(1)}, u32[]{:S(2)}, u32[]{:S(2)}) %collective-permute-start.6) | collective-permute-done | bytes 98336 | tf_op jit(solution)/shard_map/ppermute | solution.py:218
  71.8 5.5 %shard_map.79 = (bf16[2,3,64,128]{3,2,1,0:T(8,128)(2,1)S(1)}, bf16[16,16,1408]{2,1,0:T(8,128)(2,1)}) custom-call(s32[2]{0:T(128)S(1)} %pad_add_fusion.h_ref.s_ref, bf16[4,6,64,128]{3,2,1,0:T(8,128)(2,1)S(1)} %pad_maximum_fusion.1.c_ref, bf16[9,384,128]{2,1,0:T(8,128)(2,1)S(1)} %bitcast.21, f32[2,4,64,128]{3,2,1,0:T(8,128)S(1)} %get-tuple-element.13.act_ref, ...), custom_call_target="tpu_custom_call" | custom-call | tf_op jit(solution)/shard_map/pallas_call | solution.py:45
  77.3 10.1 %all-to-all-start.2 = ((bf16[16,16,1408]{2,1,0:T(8,128)(2,1)}), bf16[16,16,1408]{2,1,0:T(8,128)(2,1)S(1)}, u32[]{:S(2)}, u32[]{:S(2)}) async-start(bf16[16,16,1408]{2,1,0:T(8,128)(2,1)} %get-tuple-element.15), calls=%async_computation.2 | async-start | bytes 1441792 | tf_op jit(solution)/shard_map/all_to_all | solution.py:269
  87.4 3.3 %collective-permute-start.4 = (bf16[1,4,64,128]{3,2,1,0:T(8,128)(2,1)S(1)}, bf16[1,4,64,128]{3,2,1,0:T(8,128)(2,1)S(1)}, u32[]{:S(2)}, u32[]{:S(2)}) collective-permute-start(bf16[1,4,64,128]{3,2,1,0:T(8,128)(2,1)S(1)} %slice_select_fusion), channel_id=1, source_target_pairs={{0,32},{32,64},{64,96},{96,128},{128,160},{160,192},{192,224},{224... | collective-permute-start | bytes 196616 | tf_op jit(solution)/shard_map/ppermute | solution.py:273
  90.7 6.6 %collective-permute-done.4 = bf16[1,4,64,128]{3,2,1,0:T(8,128)(2,1)S(1)} collective-permute-done((bf16[1,4,64,128]{3,2,1,0:T(8,128)(2,1)S(1)}, bf16[1,4,64,128]{3,2,1,0:T(8,128)(2,1)S(1)}, u32[]{:S(2)}, u32[]{:S(2)}) %collective-permute-start.4) | collective-permute-done | bytes 65568 | tf_op jit(solution)/shard_map/ppermute | solution.py:273
  97.3 1.1 shard_map.77
  98.4 1.1 all-to-all-done.2.got_ref
  99.5 5.9 %all-to-all-start = ((bf16[16,8,128]{2,1,0:T(8,128)(2,1)}), bf16[16,8,128]{2,1,0:T(8,128)(2,1)S(1)}, u32[]{:S(2)}, u32[]{:S(2)}) async-start(bf16[16,8,128]{2,1,0:T(8,128)(2,1)} %bitcast.5), calls=%async_computation | async-start | bytes 65536 | tf_op jit(solution)/shard_map/all_to_all | solution.py:278
  106.3 9.1 %all-to-all-done = bf16[16,8,128]{2,1,0:T(8,128)(2,1)S(1)} async-done(((bf16[16,8,128]{2,1,0:T(8,128)(2,1)}), bf16[16,8,128]{2,1,0:T(8,128)(2,1)S(1)}, u32[]{:S(2)}, u32[]{:S(2)}) %all-to-all-start) | async-done | bytes 32800 | tf_op jit(solution)/shard_map/all_to_all | solution.py:278
  115.4 4.1 %all-to-all-start.3 = ((f32[16,8,256]{2,1,0:T(8,128)}), f32[16,8,256]{2,1,0:T(8,128)S(1)}, u32[]{:S(2)}, u32[]{:S(2)}) async-start(f32[16,8,256]{2,1,0:T(8,128)} %bitcast.10), calls=%async_computation.3 | async-start | bytes 262144 | tf_op jit(solution)/shard_map/all_to_all | solution.py:286
  121.0 1.6 %shard_map.80 = bf16[512,128]{1,0:T(8,128)(2,1)} custom-call(bf16[2,3,64,128]{3,2,1,0:T(8,128)(2,1)S(1)} %maximum_select_fusion.1.a_ref, bf16[9,192,128]{2,1,0:T(8,128)(2,1)S(1)} %bitcast.24), custom_call_target="tpu_custom_call" | custom-call | tf_op jit(solution)/shard_map/pallas_call | solution.py:45
  122.6 9.1 %all-to-all-done.3.got_ref = f32[16,8,256]{2,1,0:T(8,128)S(1)} async-done(((f32[16,8,256]{2,1,0:T(8,128)}), f32[16,8,256]{2,1,0:T(8,128)S(1)}, u32[]{:S(2)}, u32[]{:S(2)}) %all-to-all-start.3) | async-done | bytes 131104 | tf_op jit(solution)/shard_map/all_to_all | solution.py:286
  (39 shorter events, 5.7 us)
Async XLA Ops:
  1.6 0.9 copy-start.2
  3.7 57.9 %all-to-all-start.1 = ((bf16[32,8,384]{2,1,0:T(8,128)(2,1)}), bf16[32,8,384]{2,1,0:T(8,128)(2,1)S(1)}, u32[]{:S(2)}, u32[]{:S(2)}) async-start(bf16[32,8,384]{2,1,0:T(8,128)(2,1)} %get-tuple-element.12), calls=%async_computation.1 | async-start | bytes 393216 | tf_op jit(solution)/shard_map/all_to_all | solution.py:240
  20.5 30.9 %collective-permute-start = (bf16[2,4,64,128]{3,2,1,0:T(8,128)(2,1)S(1)}, bf16[2,4,64,128]{3,2,1,0:T(8,128)(2,1)S(1)}, u32[]{:S(2)}, u32[]{:S(2)}) collective-permute-start(bf16[2,4,64,128]{3,2,1,0:T(8,128)(2,1)S(1)} %get-tuple-element.10), channel_id=1, source_target_pairs={{0,16},{16,0},{1,17},{17,1},{2,18},{18,2},{3,19},{19,3},{4,20},{20... | collective-permute-start | bytes 393224 | tf_op jit(solution)/shard_map/ppermute | solution.py:239
  51.5 4.5 %collective-permute-start.1 = (bf16[1,4,64,128]{3,2,1,0:T(8,128)(2,1)S(1)}, bf16[1,4,64,128]{3,2,1,0:T(8,128)(2,1)S(1)}, u32[]{:S(2)}, u32[]{:S(2)}) collective-permute-start(bf16[1,4,64,128]{3,2,1,0:T(8,128)(2,1)S(1)} %slice.52), channel_id=1, source_target_pairs={{0,32},{32,64},{64,96},{96,128},{128,160},{160,192},{192,224},{224... | collective-permute-start | bytes 196616 | tf_op jit(solution)/shard_map/ppermute | solution.py:218
  56.1 11.3 %collective-permute-start.2 = (bf16[5,3,64,128]{3,2,1,0:T(8,128)(2,1)S(1)}, bf16[5,3,64,128]{3,2,1,0:T(8,128)(2,1)S(1)}, u32[]{:S(2)}, u32[]{:S(2)}) collective-permute-start(bf16[5,3,64,128]{3,2,1,0:T(8,128)(2,1)S(1)} %slice.53), channel_id=1, source_target_pairs={{0,1},{1,2},{2,3},{3,4},{4,5},{5,6},{6,7},{7,8},{8,9},{9,10},{10,1... | collective-permute-start | bytes 737288 | tf_op jit(solution)/shard_map/ppermute | solution.py:218
  59.7 7.7 %collective-permute-start.3 = (bf16[5,2,64,128]{3,2,1,0:T(8,128)(2,1)S(1)}, bf16[5,2,64,128]{3,2,1,0:T(8,128)(2,1)S(1)}, u32[]{:S(2)}, u32[]{:S(2)}) collective-permute-start(bf16[5,2,64,128]{3,2,1,0:T(8,128)(2,1)S(1)} %slice.54), channel_id=1, source_target_pairs={{1,0},{2,1},{3,2},{4,3},{5,4},{6,5},{7,6},{8,7},{9,8},{10,9},{11,1... | collective-permute-start | bytes 491528 | tf_op jit(solution)/shard_map/ppermute | solution.py:218
  61.9 7.1 %collective-permute-start.5 = (bf16[1,6,64,128]{3,2,1,0:T(8,128)(2,1)S(1)}, bf16[1,6,64,128]{3,2,1,0:T(8,128)(2,1)S(1)}, u32[]{:S(2)}, u32[]{:S(2)}) collective-permute-start(bf16[1,6,64,128]{3,2,1,0:T(8,128)(2,1)S(1)} %get-tuple-element.18), channel_id=1, source_target_pairs={{0,32},{32,64},{64,96},{96,128},{128,160},{160,192},{192,224},{224... | collective-permute-start | bytes 294920 | tf_op jit(solution)/shard_map/ppermute | solution.py:218
  65.9 1.6 %copy-start.1 = (bf16[3,3,3,64,128]{4,3,2,1,0:T(8,128)(2,1)S(1)}, bf16[3,3,3,64,128]{4,3,2,1,0:T(8,128)(2,1)}, u32[]{:S(2)}) copy-start(bf16[3,3,3,64,128]{4,3,2,1,0:T(8,128)(2,1)} %param.5) | copy-start | bytes 1327108
  65.9 5.9 %collective-permute-start.6 = (bf16[1,6,64,128]{3,2,1,0:T(8,128)(2,1)S(1)}, bf16[1,6,64,128]{3,2,1,0:T(8,128)(2,1)S(1)}, u32[]{:S(2)}, u32[]{:S(2)}) collective-permute-start(bf16[1,6,64,128]{3,2,1,0:T(8,128)(2,1)S(1)} %get-tuple-element.19), channel_id=1, source_target_pairs={{32,0},{64,32},{96,64},{128,96},{160,128},{192,160},{224,192},{256... | collective-permute-start | bytes 294920 | tf_op jit(solution)/shard_map/ppermute | solution.py:218
  67.5 4.4 %copy-start = (bf16[3,3,3,128,128]{4,3,2,1,0:T(8,128)(2,1)S(1)}, bf16[3,3,3,128,128]{4,3,2,1,0:T(8,128)(2,1)}, u32[]{:S(2)}) copy-start(bf16[3,3,3,128,128]{4,3,2,1,0:T(8,128)(2,1)} %param.6) | copy-start | bytes 2654212
  77.3 22.2 %all-to-all-start.2 = ((bf16[16,16,1408]{2,1,0:T(8,128)(2,1)}), bf16[16,16,1408]{2,1,0:T(8,128)(2,1)S(1)}, u32[]{:S(2)}, u32[]{:S(2)}) async-start(bf16[16,16,1408]{2,1,0:T(8,128)(2,1)} %get-tuple-element.15), calls=%async_computation.2 | async-start | bytes 1441792 | tf_op jit(solution)/shard_map/all_to_all | solution.py:269
  87.4 9.9 %collective-permute-start.4 = (bf16[1,4,64,128]{3,2,1,0:T(8,128)(2,1)S(1)}, bf16[1,4,64,128]{3,2,1,0:T(8,128)(2,1)S(1)}, u32[]{:S(2)}, u32[]{:S(2)}) collective-permute-start(bf16[1,4,64,128]{3,2,1,0:T(8,128)(2,1)S(1)} %slice_select_fusion), channel_id=1, source_target_pairs={{0,32},{32,64},{64,96},{96,128},{128,160},{160,192},{192,224},{224... | collective-permute-start | bytes 196616 | tf_op jit(solution)/shard_map/ppermute | solution.py:273
  99.5 15.9 %all-to-all-start = ((bf16[16,8,128]{2,1,0:T(8,128)(2,1)}), bf16[16,8,128]{2,1,0:T(8,128)(2,1)S(1)}, u32[]{:S(2)}, u32[]{:S(2)}) async-start(bf16[16,8,128]{2,1,0:T(8,128)(2,1)} %bitcast.5), calls=%async_computation | async-start | bytes 65536 | tf_op jit(solution)/shard_map/all_to_all | solution.py:278
  115.4 16.2 %all-to-all-start.3 = ((f32[16,8,256]{2,1,0:T(8,128)}), f32[16,8,256]{2,1,0:T(8,128)S(1)}, u32[]{:S(2)}, u32[]{:S(2)}) async-start(f32[16,8,256]{2,1,0:T(8,128)} %bitcast.10), calls=%async_computation.3 | async-start | bytes 262144 | tf_op jit(solution)/shard_map/all_to_all | solution.py:286
  119.6 1.4 %collective-permute-start.7 = (bf16[1,3,64,128]{3,2,1,0:T(8,128)(2,1)S(1)}, bf16[1,3,64,128]{3,2,1,0:T(8,128)(2,1)S(1)}, u32[]{:S(2)}, u32[]{:S(2)}) collective-permute-start(bf16[1,3,64,128]{3,2,1,0:T(8,128)(2,1)S(1)} %get-tuple-element.21), channel_id=1, source_target_pairs={{48,16},{80,48},{112,80},{144,112},{176,144},{208,176},{240,208},{... | collective-permute-start | bytes 147464 | tf_op jit(solution)/shard_map/ppermute | solution.py:281

commit v3 on v2

--- a/solution.py
+++ b/solution.py
@@ -51,7 +51,7 @@
     )(*args)
 
 
-def prep_body(vol_ref, cot_ref, volt_ref, slab_ref):
+def columns_body(vol_ref, out_ref):
     shape = (512, 512)
     to, of = iota(shape, 0), iota(shape, 1)
     rows = dot(one_hot(of == (to % 64) * 8 + to // 64), vol_ref[...]).astype(BF)
@@ -63,7 +63,11 @@
         block = rows[64 * i : 64 * i + 64]
         left = jnp.concatenate([block, zero], axis=0)
         right = jnp.concatenate([zero, block], axis=0)
-        volt_ref[i // 4, i % 4] = (dot(even, left, 1, 1) + dot(odd, right, 1, 1)).astype(BF)
+        out_ref[i // 4, i % 4] = (dot(even, left, 1, 1) + dot(odd, right, 1, 1)).astype(BF)
+
+
+def slabs_body(cot_ref, after_ref, slab_ref):
+    del after_ref
     for i in range(16):
         for j in range(3):
             pair = i + j - 1
@@ -86,12 +90,14 @@
 
 
 def conv_one_body(h_ref, v_ref, k_ref, act_ref, hid_ref):
-    acc = jnp.zeros((512, 256), F32)
+    cells, weights = [], []
     for i, (a, b) in enumerate(PAIRS):
-        x = jnp.concatenate([v_ref[2 * q + a, 2 * r + b] for q in range(2) for r in range(4)], axis=0)
+        rows = [v_ref[2 * q + a, 2 * r + b] for q in range(2) for r in range(4)]
+        cells.append(jnp.concatenate(rows, axis=0))
         taps = k_ref[i]
         right = jnp.concatenate([jnp.zeros((64, 128), BF), taps[:64]], axis=0)
-        acc += dot(x, jnp.concatenate([taps[64:], right], axis=1))
+        weights.append(jnp.concatenate([taps[64:], right], axis=1))
+    acc = dot(jnp.concatenate(cells, axis=1), jnp.concatenate(weights, axis=0))
     act = acc[:, :128] + earlier(acc[:, 128:])
     soft = jnp.maximum(act, 0.0) + jnp.log1p(jnp.exp(-jnp.abs(act)))
     hidden = SLOPE * act + (1.0 - SLOPE) * soft
@@ -106,12 +112,12 @@
 
 def grads_body(s_ref, c_ref, k_ref, act_ref, hid_ref, v_ref, ag_ref, out_ref):
     h, zh = s_ref[0], s_ref[1]
-    acc = jnp.zeros((384, 384), F32)
+    cells, weights = [], []
     for a, b in PAIRS:
-        x = jnp.concatenate(
-            [c_ref[q + a, r + 1 + b] for q in range(2) for r in range(3)], axis=0
-        )
-        acc += dot(x, k_ref[3 * (2 - a) + 2 - b], 1, 1)
+        rows = [c_ref[q + a, r + 1 + b] for q in range(2) for r in range(3)]
+        cells.append(jnp.concatenate(rows, axis=0))
+        weights.append(k_ref[3 * (2 - a) + 2 - b])
+    acc = dot(jnp.concatenate(cells, axis=1), jnp.concatenate(weights, axis=1), 1, 1)
     grad = acc[:, 128:256] + earlier(acc[:, 256:]) + later(acc[:, :128])
     act = jnp.concatenate([act_ref[q, r + 1] for q in range(2) for r in range(3)], axis=0)
     small = jnp.exp(-jnp.abs(act))
@@ -125,49 +131,51 @@
             ag_ref[q, r] = ag[at : at + 64]
     own_ag = jnp.concatenate([ag[:128], ag[192:320]], axis=0)
 
-    lane = iota((128, 256), 1)
-    source = iota((128, 256), 0)
-    device, slot = lane // 16, lane % 16
+    slot_row = iota((256, 128), 0)
+    source = iota((256, 128), 1)
+    device, slot = slot_row // 16, slot_row % 16
     pick_two = one_hot((slot < 12) & (source == device * 8 + zh * 4 + slot % 4))
     own_hid = jnp.concatenate([hid_ref[q, r + 1] for q in range(2) for r in range(2)], axis=0)
-    flat = dot(own_hid, pick_two)
-    tap = iota((256, 256), 1) % 16 // 4
-    hid_rows = jnp.where(tap == 0, earlier(flat), jnp.where(tap == 1, flat, later(flat))).astype(BF)
-    pick_one = one_hot(
-        (slot >= 12) & (source == (slot - 12) // 2 * 64 + device * 4 + zh * 2 + slot % 2)
-    )
-    first = jnp.zeros((256, 256), F32)
-    last = None
+    flat = dot(pick_two, own_hid, 1, 1)
+    tap = iota((256, 256), 0) % 16 // 4
+    column = iota((256, 256), 1) % 64
+    before = jnp.where(column == 0, 0.0, pltpu.roll(flat, 1, 1))
+    after = jnp.where(column == 63, 0.0, pltpu.roll(flat, 255, 1))
+    hid_rows = jnp.where(tap == 0, before, jnp.where(tap == 1, flat, after)).astype(BF)
+    cots = [
+        jnp.concatenate([c_ref[q + 2 - a, r + 3 - b] for q in range(2) for r in range(2)], axis=0)
+        for a, b in PAIRS
+    ]
+    first = dot(hid_rows, jnp.concatenate(cots, axis=1))
+    channel = device * 4 + zh * 2 + slot % 2
+    pick_one = one_hot((slot >= 12) & (source == (slot - 12) // 2 * 64 + channel))
+    vols, picks = [], []
     for i, (a, b) in enumerate(PAIRS):
         x = jnp.concatenate(
             [v_ref[2 * q + a, 2 * r + 2 + b] for q in range(2) for r in range(2)], axis=0
         )
-        vol_rows = dot(x, pick_one).astype(BF)
-        cot = jnp.concatenate(
-            [c_ref[q + 2 - a, r + 3 - b] for q in range(2) for r in range(2)], axis=0
-        )
-        both = dot(hid_rows, cot, 0, 0) + dot(vol_rows, own_ag, 0, 0)
+        vol_rows = dot(pick_one, x, 1, 1).astype(BF)
+        both = first[:, 128 * i : 128 * i + 128] + dot(vol_rows, own_ag)
         out_ref[:, :, 128 * i : 128 * i + 128] = both.astype(BF).reshape(16, 16, 128)
-        here = one_hot(
-            (slot // 2 == i % 8) & (source == 64 + device * 4 + zh * 2 + slot % 2)
-        )
-        picked = dot(x, here)
-        if i < 8:
-            first += picked
-        else:
-            last = picked
-    for i, rows in ((9, first), (10, last)):
-        part = dot(earlier(rows).astype(BF), own_ag, 0, 0)
-        out_ref[:, :, 128 * i : 128 * i + 128] = part.astype(BF).reshape(16, 16, 128)
+        vols.append(x)
+        picks.append(one_hot((slot // 2 == i % 8) & (source == 64 + channel)))
+    groups = (
+        (9, jnp.concatenate(picks[:8], axis=1), jnp.concatenate(vols[:8], axis=1)),
+        (10, picks[8], vols[8]),
+    )
+    for i, pick, x in groups:
+        rows = dot(pick, x, 1, 1)
+        rows = jnp.where(column == 0, 0.0, pltpu.roll(rows, 1, 1)).astype(BF)
+        out_ref[:, :, 128 * i : 128 * i + 128] = dot(rows, own_ag).astype(BF).reshape(16, 16, 128)
 
 
 def conv_two_body(h_ref, k_ref, out_ref):
-    acc = jnp.zeros((128, 128), F32)
-    for i, (a, b) in enumerate(PAIRS):
+    cells = []
+    for a, b in PAIRS:
         x = jnp.concatenate([h_ref[a, b], h_ref[a, b + 1]], axis=0)
         wide = x.astype(F32)
-        taps = jnp.concatenate([earlier(wide).astype(BF), x, later(wide).astype(BF)], axis=1)
-        acc += dot(taps, k_ref[i])
+        cells += [earlier(wide).astype(BF), x, later(wide).astype(BF)]
+    acc = dot(jnp.concatenate(cells, axis=1), k_ref[...])
     out_ref[...] = acc.T.astype(BF)
 
 
@@ -196,20 +204,21 @@
     out_ref[...] = dot(turn, jnp.concatenate(blocks, axis=0)).astype(BF)
 
 
-def plane_sum_body(got_ref, out_ref):
+def plane_sum_body(got_ref, next_ref, out_ref):
     total = got_ref[0].astype(F32)
     for i in range(1, 16):
         total += got_ref[i].astype(F32)
     pieces = [total[:, 128 * j : 128 * j + 128] for j in range(11)]
     rows = jnp.concatenate(pieces + [jnp.zeros((80, 128), F32)], axis=0)
-    out_ref[...] = rows.T
+    out_ref[:, :128] = next_ref[...]
+    out_ref[:, 128:] = rows.T.astype(BF)
 
 
 def line_sum_body(scale, got_ref, out_ref):
-    total = got_ref[0]
+    total = got_ref[0].astype(F32)
     for i in range(1, 16):
-        total += got_ref[i]
-    out_ref[...] = total * scale
+        total += got_ref[i].astype(F32)
+    out_ref[...] = (total[:, 128:] * scale).T
 
 
 def shifted(block, axis, distance):
@@ -230,12 +239,8 @@
     two = kernel_two.reshape(9, 384, 128)
     planes = lax.axis_size(PLANE)
 
-    own, slabs = call(
-        prep_body,
-        [shape((2, 4, 64, 128)), shape((32, 8, 384))],
-        volume.reshape(512, 128),
-        cotangent.reshape(8, 2048),
-    )
+    own = call(columns_body, shape((2, 4, 64, 128)), volume.reshape(512, 128))
+    slabs = call(slabs_body, shape((32, 8, 384)), cotangent.reshape(8, 2048), own)
     other = lax.ppermute(own, "zh", [(0, 1), (1, 0)])
     slab = lax.all_to_all(slabs, LINE, 0, 0, tiled=True)
     low = jnp.where(zh == 0, own, other)
@@ -255,6 +260,10 @@
         one,
         scalars=1,
     )
+    up = [(2 * k, 2 * k + 2) for k in range(planes - 1)]
+    down = [(2 * k + 1, 2 * k - 1) for k in range(1, planes)]
+    edge = lax.ppermute(jnp.where(zh == 0, hidden[1:], hidden[:1]), DEPTH, up + down)
+    edge, cot = lax.optimization_barrier((edge, cot))
     ag, partial = call(
         grads_body,
         [shape((2, 3, 64, 128)), shape((16, 16, 1408))],
@@ -267,25 +276,20 @@
         scalars=1,
     )
     parts = lax.all_to_all(partial, PLANE, 0, 0, tiled=True)
-
-    up = [(2 * k, 2 * k + 2) for k in range(planes - 1)]
-    down = [(2 * k + 1, 2 * k - 1) for k in range(1, planes)]
-    edge = lax.ppermute(jnp.where(zh == 0, hidden[1:], hidden[:1]), DEPTH, up + down)
     three = jnp.where(
         zh == 0, jnp.concatenate([edge, hidden], axis=0), jnp.concatenate([hidden, edge], axis=0)
     )
-    next_own = call(conv_two_body, shape((128, 128)), three, two)
-    swapped = lax.all_to_all(next_own.reshape(16, 8, 128), HEIGHT, 0, 0, tiled=True)
-    next_acts = swapped.reshape(16, 8, 2, 64).transpose(1, 0, 2, 3).reshape(cotangent.shape)
+    next_own = call(conv_two_body, shape((128, 128)), three, kernel_two.reshape(3456, 128))
 
     after = lax.ppermute(ag[:1], DEPTH, down)
     pair = jnp.where(zh == 0, ag, jnp.concatenate([ag[1:], after], axis=0))
     volume_grad = call(volume_grad_body, shape((512, 128)), pair, one).reshape(volume.shape)
 
-    summed = call(plane_sum_body, shape((128, 256), F32), parts)
-    rows = lax.all_to_all(summed.reshape(16, 8, 256), HEIGHT, 0, 0, tiled=True)
-    total = call(functools.partial(line_sum_body, 1.0 / math.sqrt(65536)), shape((8, 256), F32), rows)
-    table = total.T
+    summed = call(plane_sum_body, shape((128, 384)), parts, next_own)
+    rows = lax.all_to_all(summed.reshape(16, 8, 384), HEIGHT, 0, 0, tiled=True)
+    swapped = rows[:, :, :128].reshape(16, 8, 2, 64)
+    next_acts = swapped.transpose(1, 0, 2, 3).reshape(cotangent.shape)
+    table = call(functools.partial(line_sum_body, 1.0 / math.sqrt(65536)), shape((256, 8), F32), rows)
     slots = table[:144].reshape(9, 16, 8)
     two_grad = slots[:, :12].reshape(3, 3, 3, 4, 8)
     before = table[144:162].reshape(9, 1, 2, 8)

time: 134 us -> 110 us (0.82)
  waiting for transfers between devices: 49 us -> 28.9 us
  Pallas kernels: 11.9 us -> 9.69 us
  starting transfers between devices: 66.9 us -> 64.7 us
    ppermute x1, waiting for transfers between devices: 18.9 us -> 0.01 us  [per_device(): other = lax.ppermute(own, 'zh', [(0, 1), (1, 0)])]
    all_to_all x1, waiting for transfers between devices: 1.14 us -> 12.7 us  [per_device(): parts = lax.all_to_all(partial, PLANE, 0, 0, tiled=True)]
    all_to_all x1, starting transfers between devices: 16.8 us -> 6.14 us  [per_device(): slab = lax.all_to_all(slabs, LINE, 0, 0, tiled=True)]
    all_to_all x2 -> x1, waiting for transfers between devices: 18.2 us -> 9.01 us  [per_device(): rows = lax.all_to_all(summed.reshape(16, 8, 384), HEIGHT, 0, 0, tiled=True)]
    ppermute x5, starting transfers between devices: 14 us -> 22.7 us  [shifted(): return lax.ppermute(block, axis, route)]
    all_to_all x2 -> x1, starting transfers between devices: 10.1 us -> 4.04 us  [per_device(): rows = lax.all_to_all(summed.reshape(16, 8, 384), HEIGHT, 0, 0, tiled=True)]
    ppermute x1, waiting for transfers between devices: 6.58 us -> 1.21 us  [per_device(): lax.ppermute(jnp.where(zh == 0, hidden[1:], hidden[:1]), DEPTH, up + down)]
    ppermute x1, starting transfers between devices: 12 us -> 16.3 us  [per_device(): other = lax.ppermute(own, 'zh', [(0, 1), (1, 0)])]
  transfers between devices with their start and end apart: 12 -> 11, of which waited for: 7 -> 5; matrix products, arithmetic and copies ran while one was open for 1% -> 0% of each run, Pallas kernels for 4% -> 4%
where the time goes in v3:
time: 110 us; the launch traced here: 109 us
  starting transfers between devices  64.7 us (59%)
  waiting for transfers between devices  28.9 us (26%)
  Pallas kernels  9.69 us (9%)
  local copies, waits for them, and re-layouts  3.86 us (4%)
    ppermute x5, starting transfers between devices, shifted(): return lax.ppermute(block, axis, route)  22.7 us
    ppermute x1, starting transfers between devices, per_device(): other = lax.ppermute(own, 'zh', [(0, 1), (1, 0)])  16.3 us
    all_to_all x1, waiting for transfers between devices, per_device(): parts = lax.all_to_all(partial, PLANE, 0, 0, tiled=True)  12.7 us
    all_to_all x1, starting transfers between devices, per_device(): parts = lax.all_to_all(partial, PLANE, 0, 0, tiled=True)  10.9 us
    pallas_call x9, Pallas kernels, call(): pl.pallas_call(body, out_shape=outs, in_specs=[smem] * scalars + [vmem] *...  9.69 us
    all_to_all x1, waiting for transfers between devices, per_device(): rows = lax.all_to_all(summed.reshape(16, 8, 384), HEIGHT, 0, 0, tiled=True)  9.01 us
    all_to_all x1, starting transfers between devices, per_device(): slab = lax.all_to_all(slabs, LINE, 0, 0, tiled=True)  6.14 us
    ppermute x5, waiting for transfers between devices, shifted(): return lax.ppermute(block, axis, route)  5.97 us
  transfers between devices with their start and end apart: 11, of which 5 were waited for; matrix products, arithmetic and copies ran while one was open for 0% of the time, Pallas kernels for 4%

profile of v3, /device:TPU:1, one launch (start us, length us, event | category | flops | bytes accessed | tf_op | source)
XLA Modules:
  0.0 109.1 jit_solution(14867339764721079411)
XLA Ops:
  0.6 0.9 copy-done.3
  1.5 0.7 shard_map.75.after_ref
  2.3 16.3 %collective-permute-start = (bf16[2,4,64,128]{3,2,1,0:T(8,128)(2,1)S(1)}, bf16[2,4,64,128]{3,2,1,0:T(8,128)(2,1)S(1)}, u32[]{:S(2)}, u32[]{:S(2)}) collective-permute-start(bf16[2,4,64,128]{3,2,1,0:T(8,128)(2,1)S(1)} %shard_map.75.after_ref), channel_id=1, source_target_pairs={{0,16},{16,0},{1,17},{17,1},{2,18},{18,2},{3,19},{19,3},{4,20},{20... | collective-permute-start | bytes 393224 | tf_op jit(solution)/shard_map/ppermute | solution.py:244
  18.7 0.7 shard_map.77
  19.4 6.1 %all-to-all-start = ((bf16[32,8,384]{2,1,0:T(8,128)(2,1)}), bf16[32,8,384]{2,1,0:T(8,128)(2,1)S(1)}, u32[]{:S(2)}, u32[]{:S(2)}) async-start(bf16[32,8,384]{2,1,0:T(8,128)(2,1)} %shard_map.77), calls=%async_computation | async-start | bytes 393216 | tf_op jit(solution)/shard_map/all_to_all | solution.py:245
  25.6 3.2 %collective-permute-start.1 = (bf16[1,4,64,128]{3,2,1,0:T(8,128)(2,1)S(1)}, bf16[1,4,64,128]{3,2,1,0:T(8,128)(2,1)S(1)}, u32[]{:S(2)}, u32[]{:S(2)}) collective-permute-start(bf16[1,4,64,128]{3,2,1,0:T(8,128)(2,1)S(1)} %slice.56), channel_id=1, source_target_pairs={{0,32},{32,64},{64,96},{96,128},{128,160},{160,192},{192,224},{224... | collective-permute-start | bytes 196616 | tf_op jit(solution)/shard_map/ppermute | solution.py:227
  28.8 1.3 %collective-permute-done.1 = bf16[1,4,64,128]{3,2,1,0:T(8,128)(2,1)S(1)} collective-permute-done((bf16[1,4,64,128]{3,2,1,0:T(8,128)(2,1)S(1)}, bf16[1,4,64,128]{3,2,1,0:T(8,128)(2,1)S(1)}, u32[]{:S(2)}, u32[]{:S(2)}) %collective-permute-start.1) | collective-permute-done | bytes 65568 | tf_op jit(solution)/shard_map/ppermute | solution.py:227
  30.2 12.3 %collective-permute-start.2 = (bf16[5,3,64,128]{3,2,1,0:T(8,128)(2,1)S(1)}, bf16[5,3,64,128]{3,2,1,0:T(8,128)(2,1)S(1)}, u32[]{:S(2)}, u32[]{:S(2)}) collective-permute-start(bf16[5,3,64,128]{3,2,1,0:T(8,128)(2,1)S(1)} %slice.57), channel_id=1, source_target_pairs={{0,1},{1,2},{2,3},{3,4},{4,5},{5,6},{6,7},{7,8},{8,9},{9,10},{10,1... | collective-permute-start | bytes 737288 | tf_op jit(solution)/shard_map/ppermute | solution.py:227
  42.5 1.9 %collective-permute-start.3 = (bf16[5,2,64,128]{3,2,1,0:T(8,128)(2,1)S(1)}, bf16[5,2,64,128]{3,2,1,0:T(8,128)(2,1)S(1)}, u32[]{:S(2)}, u32[]{:S(2)}) collective-permute-start(bf16[5,2,64,128]{3,2,1,0:T(8,128)(2,1)S(1)} %slice.58), channel_id=1, source_target_pairs={{1,0},{2,1},{3,2},{4,3},{5,4},{6,5},{7,6},{8,7},{9,8},{10,9},{11,1... | collective-permute-start | bytes 491528 | tf_op jit(solution)/shard_map/ppermute | solution.py:227
  44.5 4.6 %collective-permute-done.3 = bf16[5,2,64,128]{3,2,1,0:T(8,128)(2,1)S(1)} collective-permute-done((bf16[5,2,64,128]{3,2,1,0:T(8,128)(2,1)S(1)}, bf16[5,2,64,128]{3,2,1,0:T(8,128)(2,1)S(1)}, u32[]{:S(2)}, u32[]{:S(2)}) %collective-permute-start.3) | collective-permute-done | bytes 163872 | tf_op jit(solution)/shard_map/ppermute | solution.py:227
  49.2 1.2 %shard_map.76 = (f32[2,4,64,128]{3,2,1,0:T(8,128)S(1)}, bf16[2,4,64,128]{3,2,1,0:T(8,128)(2,1)S(1)}) custom-call(s32[2]{0:T(128)S(1)} %pad_add_fusion.h_ref.s_ref, bf16[5,9,64,128]{3,2,1,0:T(8,128)(2,1)S(1)} %pad_maximum_fusion.v_ref, bf16[9,192,128]{2,1,0:T(8,128)(2,1)S(1)} %bitcast.19), custom_call_target="tpu_custom_call" | custom-call | tf_op jit(solution)/shard_map/pallas_call | solution.py:45
  50.7 4.0 %collective-permute-start.5 = (bf16[1,6,64,128]{3,2,1,0:T(8,128)(2,1)S(1)}, bf16[1,6,64,128]{3,2,1,0:T(8,128)(2,1)S(1)}, u32[]{:S(2)}, u32[]{:S(2)}) collective-permute-start(bf16[1,6,64,128]{3,2,1,0:T(8,128)(2,1)S(1)} %get-tuple-element.18), channel_id=1, source_target_pairs={{0,32},{32,64},{64,96},{96,128},{128,160},{160,192},{192,224},{224... | collective-permute-start | bytes 294920 | tf_op jit(solution)/shard_map/ppermute | solution.py:227
  54.7 1.3 %collective-permute-start.6 = (bf16[1,6,64,128]{3,2,1,0:T(8,128)(2,1)S(1)}, bf16[1,6,64,128]{3,2,1,0:T(8,128)(2,1)S(1)}, u32[]{:S(2)}, u32[]{:S(2)}) collective-permute-start(bf16[1,6,64,128]{3,2,1,0:T(8,128)(2,1)S(1)} %get-tuple-element.19), channel_id=1, source_target_pairs={{32,0},{64,32},{96,64},{128,96},{160,128},{192,160},{224,192},{256... | collective-permute-start | bytes 294920 | tf_op jit(solution)/shard_map/ppermute | solution.py:227
  56.1 4.0 %collective-permute-start.4 = (bf16[1,4,64,128]{3,2,1,0:T(8,128)(2,1)S(1)}, bf16[1,4,64,128]{3,2,1,0:T(8,128)(2,1)S(1)}, u32[]{:S(2)}, u32[]{:S(2)}) collective-permute-start(bf16[1,4,64,128]{3,2,1,0:T(8,128)(2,1)S(1)} %slice_select_fusion), channel_id=1, source_target_pairs={{0,32},{32,64},{64,96},{96,128},{128,160},{160,192},{192,224},{224... | collective-permute-start | bytes 196616 | tf_op jit(solution)/shard_map/ppermute | solution.py:265
  60.2 1.2 %collective-permute-done.4 = bf16[1,4,64,128]{3,2,1,0:T(8,128)(2,1)S(1)} collective-permute-done((bf16[1,4,64,128]{3,2,1,0:T(8,128)(2,1)S(1)}, bf16[1,4,64,128]{3,2,1,0:T(8,128)(2,1)S(1)}, u32[]{:S(2)}, u32[]{:S(2)}) %collective-permute-start.4) | collective-permute-done | bytes 65568 | tf_op jit(solution)/shard_map/ppermute | solution.py:265
  61.4 3.9 %shard_map.79 = (bf16[2,3,64,128]{3,2,1,0:T(8,128)(2,1)S(1)}, bf16[16,16,1408]{2,1,0:T(8,128)(2,1)}) custom-call(s32[2]{0:T(128)S(1)} %pad_add_fusion.h_ref.s_ref, bf16[4,6,64,128]{3,2,1,0:T(8,128)(2,1)S(1)} %pad_maximum_fusion.1.c_ref, bf16[9,384,128]{2,1,0:T(8,128)(2,1)S(1)} %bitcast.17, f32[2,4,64,128]{3,2,1,0:T(8,128)S(1)} %get-tuple-element.12.act_ref, ...), custom_call_target="tpu_custom_call" | custom-call | tf_op jit(solution)/shard_map/pallas_call | solution.py:45
  65.2 10.9 %all-to-all-start.1 = ((bf16[16,16,1408]{2,1,0:T(8,128)(2,1)}), bf16[16,16,1408]{2,1,0:T(8,128)(2,1)S(1)}, u32[]{:S(2)}, u32[]{:S(2)}) async-start(bf16[16,16,1408]{2,1,0:T(8,128)(2,1)} %get-tuple-element.13), calls=%async_computation.1 | async-start | bytes 1441792 | tf_op jit(solution)/shard_map/all_to_all | solution.py:278
  76.6 12.7 %all-to-all-done.1.got_ref = bf16[16,16,1408]{2,1,0:T(8,128)(2,1)S(1)} async-done(((bf16[16,16,1408]{2,1,0:T(8,128)(2,1)}), bf16[16,16,1408]{2,1,0:T(8,128)(2,1)S(1)}, u32[]{:S(2)}, u32[]{:S(2)}) %all-to-all-start.1) | async-done | bytes 720928 | tf_op jit(solution)/shard_map/all_to_all | solution.py:278
  89.4 0.8 shard_map.81
  90.2 4.0 %all-to-all-start.2 = ((bf16[16,8,384]{2,1,0:T(8,128)(2,1)}), bf16[16,8,384]{2,1,0:T(8,128)(2,1)S(1)}, u32[]{:S(2)}, u32[]{:S(2)}) async-start(bf16[16,8,384]{2,1,0:T(8,128)(2,1)} %bitcast.7), calls=%async_computation.2 | async-start | bytes 196608 | tf_op jit(solution)/shard_map/all_to_all | solution.py:289
  94.9 1.6 %shard_map.82 = bf16[512,128]{1,0:T(8,128)(2,1)} custom-call(bf16[2,3,64,128]{3,2,1,0:T(8,128)(2,1)S(1)} %maximum_select_fusion.1.a_ref, bf16[9,192,128]{2,1,0:T(8,128)(2,1)S(1)} %bitcast.20), custom_call_target="tpu_custom_call" | custom-call | tf_op jit(solution)/shard_map/pallas_call | solution.py:45
  96.5 9.0 %all-to-all-done.2.got_ref = bf16[16,8,384]{2,1,0:T(8,128)(2,1)S(1)} async-done(((bf16[16,8,384]{2,1,0:T(8,128)(2,1)}), bf16[16,8,384]{2,1,0:T(8,128)(2,1)S(1)}, u32[]{:S(2)}, u32[]{:S(2)}) %all-to-all-start.2) | async-done | bytes 98336 | tf_op jit(solution)/shard_map/all_to_all | solution.py:289
  106.3 0.7 slice-done
  107.7 0.7 copy.10
  (41 shorter events, 4.1 us)
Async XLA Ops:
  0.6 0.9 copy-start.3
  1.5 17.0 %copy-start.4 = (bf16[8,1,32,64]{3,2,1,0:T(8,128)(2,1)S(1)}, bf16[8,1,32,64]{3,2,1,0:T(8,128)(2,1)}, u32[]{:S(2)}) copy-start(bf16[8,1,32,64]{3,2,1,0:T(8,128)(2,1)} %param.7) | copy-start | bytes 98308
  2.3 23.3 %collective-permute-start = (bf16[2,4,64,128]{3,2,1,0:T(8,128)(2,1)S(1)}, bf16[2,4,64,128]{3,2,1,0:T(8,128)(2,1)S(1)}, u32[]{:S(2)}, u32[]{:S(2)}) collective-permute-start(bf16[2,4,64,128]{3,2,1,0:T(8,128)(2,1)S(1)} %shard_map.75.after_ref), channel_id=1, source_target_pairs={{0,16},{16,0},{1,17},{17,1},{2,18},{18,2},{3,19},{19,3},{4,20},{20... | collective-permute-start | bytes 393224 | tf_op jit(solution)/shard_map/ppermute | solution.py:244
  19.4 31.0 %all-to-all-start = ((bf16[32,8,384]{2,1,0:T(8,128)(2,1)}), bf16[32,8,384]{2,1,0:T(8,128)(2,1)S(1)}, u32[]{:S(2)}, u32[]{:S(2)}) async-start(bf16[32,8,384]{2,1,0:T(8,128)(2,1)} %shard_map.77), calls=%async_computation | async-start | bytes 393216 | tf_op jit(solution)/shard_map/all_to_all | solution.py:245
  25.6 4.5 %collective-permute-start.1 = (bf16[1,4,64,128]{3,2,1,0:T(8,128)(2,1)S(1)}, bf16[1,4,64,128]{3,2,1,0:T(8,128)(2,1)S(1)}, u32[]{:S(2)}, u32[]{:S(2)}) collective-permute-start(bf16[1,4,64,128]{3,2,1,0:T(8,128)(2,1)S(1)} %slice.56), channel_id=1, source_target_pairs={{0,32},{32,64},{64,96},{96,128},{128,160},{160,192},{192,224},{224... | collective-permute-start | bytes 196616 | tf_op jit(solution)/shard_map/ppermute | solution.py:227
  30.2 18.9 %collective-permute-start.2 = (bf16[5,3,64,128]{3,2,1,0:T(8,128)(2,1)S(1)}, bf16[5,3,64,128]{3,2,1,0:T(8,128)(2,1)S(1)}, u32[]{:S(2)}, u32[]{:S(2)}) collective-permute-start(bf16[5,3,64,128]{3,2,1,0:T(8,128)(2,1)S(1)} %slice.57), channel_id=1, source_target_pairs={{0,1},{1,2},{2,3},{3,4},{4,5},{5,6},{6,7},{7,8},{8,9},{9,10},{10,1... | collective-permute-start | bytes 737288 | tf_op jit(solution)/shard_map/ppermute | solution.py:227
  42.5 6.6 %collective-permute-start.3 = (bf16[5,2,64,128]{3,2,1,0:T(8,128)(2,1)S(1)}, bf16[5,2,64,128]{3,2,1,0:T(8,128)(2,1)S(1)}, u32[]{:S(2)}, u32[]{:S(2)}) collective-permute-start(bf16[5,2,64,128]{3,2,1,0:T(8,128)(2,1)S(1)} %slice.58), channel_id=1, source_target_pairs={{1,0},{2,1},{3,2},{4,3},{5,4},{6,5},{7,6},{8,7},{9,8},{10,9},{11,1... | collective-permute-start | bytes 491528 | tf_op jit(solution)/shard_map/ppermute | solution.py:227
  44.5 4.7 %copy-start.1 = (bf16[3,3,3,64,128]{4,3,2,1,0:T(8,128)(2,1)S(1)}, bf16[3,3,3,64,128]{4,3,2,1,0:T(8,128)(2,1)}, u32[]{:S(2)}) copy-start(bf16[3,3,3,64,128]{4,3,2,1,0:T(8,128)(2,1)} %param.5) | copy-start | bytes 1327108
  50.5 10.9 %copy-start = (bf16[3,3,3,128,128]{4,3,2,1,0:T(8,128)(2,1)S(1)}, bf16[3,3,3,128,128]{4,3,2,1,0:T(8,128)(2,1)}, u32[]{:S(2)}) copy-start(bf16[3,3,3,128,128]{4,3,2,1,0:T(8,128)(2,1)} %param.6) | copy-start | bytes 2654212
  50.7 9.3 %collective-permute-start.5 = (bf16[1,6,64,128]{3,2,1,0:T(8,128)(2,1)S(1)}, bf16[1,6,64,128]{3,2,1,0:T(8,128)(2,1)S(1)}, u32[]{:S(2)}, u32[]{:S(2)}) collective-permute-start(bf16[1,6,64,128]{3,2,1,0:T(8,128)(2,1)S(1)} %get-tuple-element.18), channel_id=1, source_target_pairs={{0,32},{32,64},{64,96},{96,128},{128,160},{160,192},{192,224},{224... | collective-permute-start | bytes 294920 | tf_op jit(solution)/shard_map/ppermute | solution.py:227
  54.7 5.4 %collective-permute-start.6 = (bf16[1,6,64,128]{3,2,1,0:T(8,128)(2,1)S(1)}, bf16[1,6,64,128]{3,2,1,0:T(8,128)(2,1)S(1)}, u32[]{:S(2)}, u32[]{:S(2)}) collective-permute-start(bf16[1,6,64,128]{3,2,1,0:T(8,128)(2,1)S(1)} %get-tuple-element.19), channel_id=1, source_target_pairs={{32,0},{64,32},{96,64},{128,96},{160,128},{192,160},{224,192},{256... | collective-permute-start | bytes 294920 | tf_op jit(solution)/shard_map/ppermute | solution.py:227
  56.1 5.3 %collective-permute-start.4 = (bf16[1,4,64,128]{3,2,1,0:T(8,128)(2,1)S(1)}, bf16[1,4,64,128]{3,2,1,0:T(8,128)(2,1)S(1)}, u32[]{:S(2)}, u32[]{:S(2)}) collective-permute-start(bf16[1,4,64,128]{3,2,1,0:T(8,128)(2,1)S(1)} %slice_select_fusion), channel_id=1, source_target_pairs={{0,32},{32,64},{64,96},{96,128},{128,160},{160,192},{192,224},{224... | collective-permute-start | bytes 196616 | tf_op jit(solution)/shard_map/ppermute | solution.py:265
  65.2 24.1 %all-to-all-start.1 = ((bf16[16,16,1408]{2,1,0:T(8,128)(2,1)}), bf16[16,16,1408]{2,1,0:T(8,128)(2,1)S(1)}, u32[]{:S(2)}, u32[]{:S(2)}) async-start(bf16[16,16,1408]{2,1,0:T(8,128)(2,1)} %get-tuple-element.13), calls=%async_computation.1 | async-start | bytes 1441792 | tf_op jit(solution)/shard_map/all_to_all | solution.py:278
  90.2 15.3 %all-to-all-start.2 = ((bf16[16,8,384]{2,1,0:T(8,128)(2,1)}), bf16[16,8,384]{2,1,0:T(8,128)(2,1)S(1)}, u32[]{:S(2)}, u32[]{:S(2)}) async-start(bf16[16,8,384]{2,1,0:T(8,128)(2,1)} %bitcast.7), calls=%async_computation.2 | async-start | bytes 196608 | tf_op jit(solution)/shard_map/all_to_all | solution.py:289
  94.2 0.7 collective-permute-start.7
  105.6 0.6 copy-start.2
  106.3 0.7 slice-start

commit v4 on v3

--- a/solution.py
+++ b/solution.py
@@ -38,7 +38,7 @@
     return jnp.where(iota(x.shape, 0) % 64 == 63, 0.0, pltpu.roll(x, x.shape[0] - 1, 0))
 
 
-def call(body, outs, *args, scalars=0):
+def call(body, outs, *args, scalars=0, flops=0):
     smem = pl.BlockSpec(memory_space=pltpu.SMEM)
     vmem = pl.BlockSpec(memory_space=pltpu.VMEM)
     many = isinstance(outs, list)
@@ -48,6 +48,7 @@
         in_specs=[smem] * scalars + [vmem] * (len(args) - scalars),
         out_specs=[vmem] * len(outs) if many else vmem,
         compiler_params=pltpu.CompilerParams(vmem_limit_bytes=48 * 1024 * 1024),
+        cost_estimate=pl.CostEstimate(flops=flops, bytes_accessed=0, transcendentals=0) if flops else None,
     )(*args)
 
 
@@ -77,6 +78,13 @@
                 piece = jnp.zeros((8, 128), BF)
             slab_ref[i, :, 128 * j : 128 * j + 128] = piece
             slab_ref[16 + i, :, 128 * j : 128 * j + 128] = piece
+
+
+def order_body(s_ref, own_ref, other_ref, out_ref):
+    first = s_ref[1]
+    for i in range(2):
+        out_ref[2 * first + i] = own_ref[i]
+        out_ref[2 - 2 * first + i] = other_ref[i]
 
 
 def turn_body(got_ref, out_ref):
@@ -110,8 +118,8 @@
             hid_ref[q, r] = hidden[at : at + 64]
 
 
-def grads_body(s_ref, c_ref, k_ref, act_ref, hid_ref, v_ref, ag_ref, out_ref):
-    h, zh = s_ref[0], s_ref[1]
+def hidden_grad_body(s_ref, c_ref, k_ref, act_ref, ag_ref):
+    h = s_ref[0]
     cells, weights = [], []
     for a, b in PAIRS:
         rows = [c_ref[q + a, r + 1 + b] for q in range(2) for r in range(3)]
@@ -129,8 +137,11 @@
         for r in range(3):
             at = 64 * (3 * q + r)
             ag_ref[q, r] = ag[at : at + 64]
-    own_ag = jnp.concatenate([ag[:128], ag[192:320]], axis=0)
-
+
+
+def kernel_grads_body(s_ref, c_ref, ag_ref, hid_ref, v_ref, out_ref):
+    zh = s_ref[1]
+    own_ag = jnp.concatenate([ag_ref[q, r] for q in range(2) for r in range(2)], axis=0)
     slot_row = iota((256, 128), 0)
     source = iota((256, 128), 1)
     device, slot = slot_row // 16, slot_row % 16
@@ -243,14 +254,16 @@
     slabs = call(slabs_body, shape((32, 8, 384)), cotangent.reshape(8, 2048), own)
     other = lax.ppermute(own, "zh", [(0, 1), (1, 0)])
     slab = lax.all_to_all(slabs, LINE, 0, 0, tiled=True)
-    low = jnp.where(zh == 0, own, other)
-    high = jnp.where(zh == 0, other, own)
-    deep = jnp.concatenate([shifted(high[1:], PLANE, 1), low, high], axis=0)
-    vol = jnp.concatenate(
-        [shifted(deep[:, 1:], HEIGHT, 1), deep, shifted(deep[:, :2], HEIGHT, -1)], axis=1
+    planes4 = call(
+        order_body, shape((4, 4, 64, 128)), here, own, other, scalars=1, flops=40 * 10**9
+    )
+    deep = jnp.concatenate(
+        [shifted(planes4[:, 1:], HEIGHT, 1), planes4, shifted(planes4[:, :2], HEIGHT, -1)], axis=1
     )
     cot = call(turn_body, shape((2, 6, 64, 128)), slab.reshape(256, 384))
-    cot = jnp.concatenate([shifted(cot[1:], PLANE, 1), cot, shifted(cot[:1], PLANE, -1)], axis=0)
+    lower = shifted(jnp.concatenate([deep[3], cot[1]], axis=0), PLANE, 1)
+    vol = jnp.concatenate([lower[None, :9], deep], axis=0)
+    cot = jnp.concatenate([lower[None, 9:], cot, shifted(cot[:1], PLANE, -1)], axis=0)
 
     act, hidden = call(
         conv_one_body,
@@ -262,28 +275,24 @@
     )
     up = [(2 * k, 2 * k + 2) for k in range(planes - 1)]
     down = [(2 * k + 1, 2 * k - 1) for k in range(1, planes)]
-    edge = lax.ppermute(jnp.where(zh == 0, hidden[1:], hidden[:1]), DEPTH, up + down)
-    edge, cot = lax.optimization_barrier((edge, cot))
-    ag, partial = call(
-        grads_body,
-        [shape((2, 3, 64, 128)), shape((16, 16, 1408))],
-        here,
-        cot,
-        two,
-        act,
-        hidden,
-        vol,
-        scalars=1,
+    ag = call(
+        hidden_grad_body, shape((2, 3, 64, 128)), here, cot, two, act, scalars=1
+    )
+    edge = jnp.concatenate([jnp.where(zh == 0, hidden[1], hidden[0]), ag[0]], axis=0)
+    edge = lax.ppermute(edge, DEPTH, up + down)
+    partial = call(
+        kernel_grads_body, shape((16, 16, 1408)), here, cot, ag, hidden, vol, scalars=1
     )
     parts = lax.all_to_all(partial, PLANE, 0, 0, tiled=True)
+
+    side = edge[None, :4]
     three = jnp.where(
-        zh == 0, jnp.concatenate([edge, hidden], axis=0), jnp.concatenate([hidden, edge], axis=0)
+        zh == 0, jnp.concatenate([side, hidden], axis=0), jnp.concatenate([hidden, side], axis=0)
     )
     next_own = call(conv_two_body, shape((128, 128)), three, kernel_two.reshape(3456, 128))
-
-    after = lax.ppermute(ag[:1], DEPTH, down)
-    pair = jnp.where(zh == 0, ag, jnp.concatenate([ag[1:], after], axis=0))
+    pair = jnp.where(zh == 0, ag, jnp.concatenate([ag[1:], edge[None, 4:]], axis=0))
     volume_grad = call(volume_grad_body, shape((512, 128)), pair, one).reshape(volume.shape)
+    parts, volume_grad = lax.optimization_barrier((parts, volume_grad))
 
     summed = call(plane_sum_body, shape((128, 384)), parts, next_own)
     rows = lax.all_to_all(summed.reshape(16, 8, 384), HEIGHT, 0, 0, tiled=True)

time: 110 us -> 105 us (0.955)
  blocking collectives: 0 us -> 18.9 us
  starting transfers between devices: 64.7 us -> 52.3 us
  waiting for transfers between devices: 28.9 us -> 17.9 us
    all_to_all x0 -> x1, blocking collectives: none -> 18.9 us  [per_device(): rows = lax.all_to_all(summed.reshape(16, 8, 384), HEIGHT, 0, 0, tiled=True)]
    all_to_all x1 -> x0, waiting for transfers between devices: 9.01 us -> none  [per_device(): rows = lax.all_to_all(summed.reshape(16, 8, 384), HEIGHT, 0, 0, tiled=True)]
    ppermute x5 -> x4, starting transfers between devices: 22.7 us -> 17.7 us  [shifted(): return lax.ppermute(block, axis, route)]
    all_to_all x1 -> x0, starting transfers between devices: 4.04 us -> none  [per_device(): rows = lax.all_to_all(summed.reshape(16, 8, 384), HEIGHT, 0, 0, tiled=True)]
    all_to_all x1, waiting for transfers between devices: 12.7 us -> 9.32 us  [per_device(): parts = lax.all_to_all(partial, PLANE, 0, 0, tiled=True)]
    all_to_all x1, starting transfers between devices: 10.9 us -> 7.97 us  [per_device(): parts = lax.all_to_all(partial, PLANE, 0, 0, tiled=True)]
    ppermute x5 -> x4, waiting for transfers between devices: 5.97 us -> 8.15 us  [shifted(): return lax.ppermute(block, axis, route)]
    ppermute x2 -> x1, waiting for transfers between devices: 1.22 us -> 0.01 us  [per_device(): edge = lax.ppermute(edge, DEPTH, up + down)]
  transfers between devices with their start and end apart: 11 -> 8, of which waited for: 5 -> 4; matrix products, arithmetic and copies ran while one was open for 0% -> 0% of each run, Pallas kernels for 4% -> 7%
where the time goes in v4:
time: 105 us
  starting transfers between devices  52.3 us (50%)
  blocking collectives  18.9 us (18%)
  waiting for transfers between devices  17.9 us (17%)
  Pallas kernels  10.4 us (10%)
  local copies, waits for them, and re-layouts  3.45 us (3%)
    all_to_all x1, blocking collectives, per_device(): rows = lax.all_to_all(summed.reshape(16, 8, 384), HEIGHT, 0, 0, tiled=True)  18.9 us
    ppermute x4, starting transfers between devices, shifted(): return lax.ppermute(block, axis, route)  17.7 us
    ppermute x1, starting transfers between devices, per_device(): other = lax.ppermute(own, 'zh', [(0, 1), (1, 0)])  16.3 us
    pallas_call x11, Pallas kernels, call(): pl.pallas_call(body, out_shape=outs, in_specs=[smem] * scalars + [vmem] *...  10.4 us
    all_to_all x1, waiting for transfers between devices, per_device(): parts = lax.all_to_all(partial, PLANE, 0, 0, tiled=True)  9.32 us
    ppermute x4, waiting for transfers between devices, shifted(): return lax.ppermute(block, axis, route)  8.15 us
    all_to_all x1, starting transfers between devices, per_device(): parts = lax.all_to_all(partial, PLANE, 0, 0, tiled=True)  7.97 us
    all_to_all x1, starting transfers between devices, per_device(): slab = lax.all_to_all(slabs, LINE, 0, 0, tiled=True)  6.14 us
  transfers between devices with their start and end apart: 8, of which 4 were waited for; matrix products, arithmetic and copies ran while one was open for 0% of the time, Pallas kernels for 7%

profile of v4, /device:TPU:1, one launch (start us, length us, event | category | flops | bytes accessed | tf_op | source)
XLA Modules:
  0.0 104.7 jit_solution(5724906438034014276)
XLA Ops:
  0.6 0.9 copy-done.2
  1.5 0.7 shard_map.75.own_ref.after_ref
  2.3 16.3 %collective-permute-start = (bf16[2,4,64,128]{3,2,1,0:T(8,128)(2,1)S(1)}, bf16[2,4,64,128]{3,2,1,0:T(8,128)(2,1)S(1)}, u32[]{:S(2)}, u32[]{:S(2)}) collective-permute-start(bf16[2,4,64,128]{3,2,1,0:T(8,128)(2,1)S(1)} %shard_map.75.own_ref.after_ref), channel_id=1, source_target_pairs={{0,16},{16,0},{1,17},{17,1},{2,18},{18,2},{3,19},{19,3},{4,20},{20... | collective-permute-start | bytes 393224 | tf_op jit(solution)/shard_map/ppermute | solution.py:255
  18.7 0.7 shard_map.77
  19.4 6.1 %all-to-all-start = ((bf16[32,8,384]{2,1,0:T(8,128)(2,1)}), bf16[32,8,384]{2,1,0:T(8,128)(2,1)S(1)}, u32[]{:S(2)}, u32[]{:S(2)}) async-start(bf16[32,8,384]{2,1,0:T(8,128)(2,1)} %shard_map.77), calls=%async_computation | async-start | bytes 393216 | tf_op jit(solution)/shard_map/all_to_all | solution.py:256
  25.6 0.6 shard_map.76
  26.2 11.3 %collective-permute-start.1 = (bf16[4,3,64,128]{3,2,1,0:T(8,128)(2,1)S(1)}, bf16[4,3,64,128]{3,2,1,0:T(8,128)(2,1)S(1)}, u32[]{:S(2)}, u32[]{:S(2)}) collective-permute-start(bf16[4,3,64,128]{3,2,1,0:T(8,128)(2,1)S(1)} %slice.72), channel_id=1, source_target_pairs={{0,1},{1,2},{2,3},{3,4},{4,5},{5,6},{6,7},{7,8},{8,9},{9,10},{10,1... | collective-permute-start | bytes 589832 | tf_op jit(solution)/shard_map/ppermute | solution.py:238
  37.6 1.9 %collective-permute-start.2 = (bf16[4,2,64,128]{3,2,1,0:T(8,128)(2,1)S(1)}, bf16[4,2,64,128]{3,2,1,0:T(8,128)(2,1)S(1)}, u32[]{:S(2)}, u32[]{:S(2)}) collective-permute-start(bf16[4,2,64,128]{3,2,1,0:T(8,128)(2,1)S(1)} %slice.73), channel_id=1, source_target_pairs={{1,0},{2,1},{3,2},{4,3},{5,4},{6,5},{7,6},{8,7},{9,8},{10,9},{11,1... | collective-permute-start | bytes 393224 | tf_op jit(solution)/shard_map/ppermute | solution.py:238
  39.5 4.7 %collective-permute-done.2 = bf16[4,2,64,128]{3,2,1,0:T(8,128)(2,1)S(1)} collective-permute-done((bf16[4,2,64,128]{3,2,1,0:T(8,128)(2,1)S(1)}, bf16[4,2,64,128]{3,2,1,0:T(8,128)(2,1)S(1)}, u32[]{:S(2)}, u32[]{:S(2)}) %collective-permute-start.2) | collective-permute-done | bytes 131104 | tf_op jit(solution)/shard_map/ppermute | solution.py:238
  44.9 3.2 %collective-permute-start.3 = (bf16[15,64,128]{2,1,0:T(8,128)(2,1)S(1)}, bf16[15,64,128]{2,1,0:T(8,128)(2,1)S(1)}, u32[]{:S(2)}, u32[]{:S(2)}) collective-permute-start(bf16[15,64,128]{2,1,0:T(8,128)(2,1)S(1)} %pad_maximum_fusion.1), channel_id=1, source_target_pairs={{0,32},{32,64},{64,96},{96,128},{128,160},{160,192},{192,224},{224... | collective-permute-start | bytes 737288 | tf_op jit(solution)/shard_map/ppermute | solution.py:238
  48.1 1.3 %collective-permute-start.4 = (bf16[1,6,64,128]{3,2,1,0:T(8,128)(2,1)S(1)}, bf16[1,6,64,128]{3,2,1,0:T(8,128)(2,1)S(1)}, u32[]{:S(2)}, u32[]{:S(2)}) collective-permute-start(bf16[1,6,64,128]{3,2,1,0:T(8,128)(2,1)S(1)} %get-tuple-element.13), channel_id=1, source_target_pairs={{32,0},{64,32},{96,64},{128,96},{160,128},{192,160},{224,192},{256... | collective-permute-start | bytes 294920 | tf_op jit(solution)/shard_map/ppermute | solution.py:238
  49.4 3.5 %collective-permute-done.3 = bf16[15,64,128]{2,1,0:T(8,128)(2,1)S(1)} collective-permute-done((bf16[15,64,128]{2,1,0:T(8,128)(2,1)S(1)}, bf16[15,64,128]{2,1,0:T(8,128)(2,1)S(1)}, u32[]{:S(2)}, u32[]{:S(2)}) %collective-permute-start.3) | collective-permute-done | bytes 245792 | tf_op jit(solution)/shard_map/ppermute | solution.py:238
  53.1 0.9 copy-done.1
  54.0 1.2 %shard_map.79 = (f32[2,4,64,128]{3,2,1,0:T(8,128)S(1)}, bf16[2,4,64,128]{3,2,1,0:T(8,128)(2,1)S(1)}) custom-call(s32[2]{0:T(128)S(1)} %pad_add_fusion.s_ref.h_ref, bf16[5,9,64,128]{3,2,1,0:T(8,128)(2,1)S(1)} %maximum_maximum_fusion.v_ref, bf16[9,192,128]{2,1,0:T(8,128)(2,1)S(1)} %bitcast.35), custom_call_target="tpu_custom_call" | custom-call | tf_op jit(solution)/shard_map/pallas_call | solution.py:45
  55.3 1.3 %shard_map.80.ag_ref = bf16[2,3,64,128]{3,2,1,0:T(8,128)(2,1)S(1)} custom-call(s32[2]{0:T(128)S(1)} %pad_add_fusion.s_ref.h_ref, bf16[4,6,64,128]{3,2,1,0:T(8,128)(2,1)S(1)} %pad_maximum_fusion.c_ref, bf16[9,384,128]{2,1,0:T(8,128)(2,1)S(1)} %bitcast.33, f32[2,4,64,128]{3,2,1,0:T(8,128)S(1)} %get-tuple-element.8.act_ref), custom_call_target="tpu_custom_call" | custom-call | tf_op jit(solution)/shard_map/pallas_call | solution.py:45
  56.6 4.1 %collective-permute-start.5 = (bf16[7,64,128]{2,1,0:T(8,128)(2,1)S(1)}, bf16[7,64,128]{2,1,0:T(8,128)(2,1)S(1)}, u32[]{:S(2)}, u32[]{:S(2)}) collective-permute-start(bf16[7,64,128]{2,1,0:T(8,128)(2,1)S(1)} %pad_maximum_fusion.4), channel_id=1, source_target_pairs={{0,32},{32,64},{64,96},{96,128},{128,160},{160,192},{192,224},{224... | collective-permute-start | bytes 344072 | tf_op jit(solution)/shard_map/ppermute | solution.py:282
  60.8 3.3 %shard_map.81 = bf16[16,16,1408]{2,1,0:T(8,128)(2,1)} custom-call(s32[2]{0:T(128)S(1)} %pad_add_fusion.s_ref.h_ref, bf16[4,6,64,128]{3,2,1,0:T(8,128)(2,1)S(1)} %pad_maximum_fusion.c_ref, bf16[2,3,64,128]{3,2,1,0:T(8,128)(2,1)S(1)} %shard_map.80.ag_ref, bf16[2,4,64,128]{3,2,1,0:T(8,128)(2,1)S(1)} %get-tuple-element.9.hid_ref, ...), custom_call_target="tpu_custom_call" | custom-call | tf_op jit(solution)/shard_map/pallas_call | solution.py:45
  64.0 8.0 %all-to-all-start.1 = ((bf16[16,16,1408]{2,1,0:T(8,128)(2,1)}), bf16[16,16,1408]{2,1,0:T(8,128)(2,1)S(1)}, u32[]{:S(2)}, u32[]{:S(2)}) async-start(bf16[16,16,1408]{2,1,0:T(8,128)(2,1)} %shard_map.81), calls=%async_computation.1 | async-start | bytes 1441792 | tf_op jit(solution)/shard_map/all_to_all | solution.py:286
  72.1 1.6 %shard_map.82 = bf16[512,128]{1,0:T(8,128)(2,1)} custom-call(bf16[2,3,64,128]{3,2,1,0:T(8,128)(2,1)S(1)} %maximum_select_fusion.1.a_ref, bf16[9,192,128]{2,1,0:T(8,128)(2,1)S(1)} %bitcast.36), custom_call_target="tpu_custom_call" | custom-call | tf_op jit(solution)/shard_map/pallas_call | solution.py:45
  74.1 9.3 %all-to-all-done.1.got_ref = bf16[16,16,1408]{2,1,0:T(8,128)(2,1)S(1)} async-done(((bf16[16,16,1408]{2,1,0:T(8,128)(2,1)}), bf16[16,16,1408]{2,1,0:T(8,128)(2,1)S(1)}, u32[]{:S(2)}, u32[]{:S(2)}) %all-to-all-start.1) | async-done | bytes 720928 | tf_op jit(solution)/shard_map/all_to_all | solution.py:286
  83.6 18.9 %all_to_all.15.got_ref = bf16[16,8,384]{2,1,0:T(8,128)(2,1)S(1)} all-to-all(bf16[16,8,384]{2,1,0:T(8,128)(2,1)S(1)} %bitcast.38), channel_id=1, replica_groups=mesh['x'=4,'y'=4,'zh'=2,'zl'=8,'core'=2] {'zl','core'}, dimensions={0} | all-to-all | bytes 196608 | tf_op jit(solution)/shard_map/all_to_all | solution.py:298
  102.8 0.7 copy.10
  103.5 0.6 reshape.64
  104.1 0.6 pad_maximum_fusion.5
  (39 shorter events, 2.1 us)
Async XLA Ops:
  0.6 0.9 copy-start.2
  1.5 17.0 %copy-start.3 = (bf16[8,1,32,64]{3,2,1,0:T(8,128)(2,1)S(1)}, bf16[8,1,32,64]{3,2,1,0:T(8,128)(2,1)}, u32[]{:S(2)}) copy-start(bf16[8,1,32,64]{3,2,1,0:T(8,128)(2,1)} %param.7) | copy-start | bytes 98308
  2.3 23.4 %collective-permute-start = (bf16[2,4,64,128]{3,2,1,0:T(8,128)(2,1)S(1)}, bf16[2,4,64,128]{3,2,1,0:T(8,128)(2,1)S(1)}, u32[]{:S(2)}, u32[]{:S(2)}) collective-permute-start(bf16[2,4,64,128]{3,2,1,0:T(8,128)(2,1)S(1)} %shard_map.75.own_ref.after_ref), channel_id=1, source_target_pairs={{0,16},{16,0},{1,17},{17,1},{2,18},{18,2},{3,19},{19,3},{4,20},{20... | collective-permute-start | bytes 393224 | tf_op jit(solution)/shard_map/ppermute | solution.py:255
  19.4 25.2 %all-to-all-start = ((bf16[32,8,384]{2,1,0:T(8,128)(2,1)}), bf16[32,8,384]{2,1,0:T(8,128)(2,1)S(1)}, u32[]{:S(2)}, u32[]{:S(2)}) async-start(bf16[32,8,384]{2,1,0:T(8,128)(2,1)} %shard_map.77), calls=%async_computation | async-start | bytes 393216 | tf_op jit(solution)/shard_map/all_to_all | solution.py:256
  26.2 17.9 %collective-permute-start.1 = (bf16[4,3,64,128]{3,2,1,0:T(8,128)(2,1)S(1)}, bf16[4,3,64,128]{3,2,1,0:T(8,128)(2,1)S(1)}, u32[]{:S(2)}, u32[]{:S(2)}) collective-permute-start(bf16[4,3,64,128]{3,2,1,0:T(8,128)(2,1)S(1)} %slice.72), channel_id=1, source_target_pairs={{0,1},{1,2},{2,3},{3,4},{4,5},{5,6},{6,7},{7,8},{8,9},{9,10},{10,1... | collective-permute-start | bytes 589832 | tf_op jit(solution)/shard_map/ppermute | solution.py:238
  37.6 6.6 %collective-permute-start.2 = (bf16[4,2,64,128]{3,2,1,0:T(8,128)(2,1)S(1)}, bf16[4,2,64,128]{3,2,1,0:T(8,128)(2,1)S(1)}, u32[]{:S(2)}, u32[]{:S(2)}) collective-permute-start(bf16[4,2,64,128]{3,2,1,0:T(8,128)(2,1)S(1)} %slice.73), channel_id=1, source_target_pairs={{1,0},{2,1},{3,2},{4,3},{5,4},{6,5},{7,6},{8,7},{9,8},{10,9},{11,1... | collective-permute-start | bytes 393224 | tf_op jit(solution)/shard_map/ppermute | solution.py:238
  44.9 8.0 %collective-permute-start.3 = (bf16[15,64,128]{2,1,0:T(8,128)(2,1)S(1)}, bf16[15,64,128]{2,1,0:T(8,128)(2,1)S(1)}, u32[]{:S(2)}, u32[]{:S(2)}) collective-permute-start(bf16[15,64,128]{2,1,0:T(8,128)(2,1)S(1)} %pad_maximum_fusion.1), channel_id=1, source_target_pairs={{0,32},{32,64},{64,96},{96,128},{128,160},{160,192},{192,224},{224... | collective-permute-start | bytes 737288 | tf_op jit(solution)/shard_map/ppermute | solution.py:238
  48.1 7.0 %collective-permute-start.4 = (bf16[1,6,64,128]{3,2,1,0:T(8,128)(2,1)S(1)}, bf16[1,6,64,128]{3,2,1,0:T(8,128)(2,1)S(1)}, u32[]{:S(2)}, u32[]{:S(2)}) collective-permute-start(bf16[1,6,64,128]{3,2,1,0:T(8,128)(2,1)S(1)} %get-tuple-element.13), channel_id=1, source_target_pairs={{32,0},{64,32},{96,64},{128,96},{160,128},{192,160},{224,192},{256... | collective-permute-start | bytes 294920 | tf_op jit(solution)/shard_map/ppermute | solution.py:238
  53.0 1.0 copy-start.1
  54.0 1.3 %copy-start = (bf16[3,3,3,128,128]{4,3,2,1,0:T(8,128)(2,1)S(1)}, bf16[3,3,3,128,128]{4,3,2,1,0:T(8,128)(2,1)}, u32[]{:S(2)}) copy-start(bf16[3,3,3,128,128]{4,3,2,1,0:T(8,128)(2,1)} %param.6) | copy-start | bytes 2654212
  56.6 15.4 %collective-permute-start.5 = (bf16[7,64,128]{2,1,0:T(8,128)(2,1)S(1)}, bf16[7,64,128]{2,1,0:T(8,128)(2,1)S(1)}, u32[]{:S(2)}, u32[]{:S(2)}) collective-permute-start(bf16[7,64,128]{2,1,0:T(8,128)(2,1)S(1)} %pad_maximum_fusion.4), channel_id=1, source_target_pairs={{0,32},{32,64},{64,96},{96,128},{128,160},{160,192},{192,224},{224... | collective-permute-start | bytes 344072 | tf_op jit(solution)/shard_map/ppermute | solution.py:282
  64.0 19.4 %all-to-all-start.1 = ((bf16[16,16,1408]{2,1,0:T(8,128)(2,1)}), bf16[16,16,1408]{2,1,0:T(8,128)(2,1)S(1)}, u32[]{:S(2)}, u32[]{:S(2)}) async-start(bf16[16,16,1408]{2,1,0:T(8,128)(2,1)} %shard_map.81), calls=%async_computation.1 | async-start | bytes 1441792 | tf_op jit(solution)/shard_map/all_to_all | solution.py:286

commit v5 on v4

v5 whole, which is shorter than its diff:
```python
import functools
import math

import jax
import jax.numpy as jnp
from jax import lax
from jax.experimental import pallas as pl
from jax.experimental.pallas import tpu as pltpu
from jax.sharding import Mesh, PartitionSpec as P

SLOPE = 0.2
DEPTH = ("x", "y", "zh")
HEIGHT = ("zl", "core")
PLANE = ("x", "y")
LINE = ("zh", "zl", "core")
BF = jnp.bfloat16
F32 = jnp.float32
PAIRS = tuple((a, b) for a in range(3) for b in range(3))


def dot(a, b, ca=1, cb=0):
    return lax.dot_general(a, b, (((ca,), (cb,)), ((), ())), preferred_element_type=F32)


def iota(shape, dim):
    return lax.broadcasted_iota(jnp.int32, shape, dim)


def one_hot(mask):
    return jnp.where(mask, 1.0, 0.0).astype(BF)


def earlier(x):
    return jnp.where(iota(x.shape, 0) % 64 == 0, 0.0, pltpu.roll(x, 1, 0))


def later(x):
    return jnp.where(iota(x.shape, 0) % 64 == 63, 0.0, pltpu.roll(x, x.shape[0] - 1, 0))


def call(body, outs, *args, scalars=0, flops=0, far=0, far_out=False, scratch=()):
    smem = pl.BlockSpec(memory_space=pltpu.SMEM)
    vmem = pl.BlockSpec(memory_space=pltpu.VMEM)
    hbm = pl.BlockSpec(memory_space=pl.ANY)
    out = hbm if far_out else vmem
    many = isinstance(outs, list)
    return pl.pallas_call(
        body,
        out_shape=outs,
        in_specs=[smem] * scalars + [vmem] * (len(args) - scalars - far) + [hbm] * far,
        out_specs=[out] * len(outs) if many else out,
        scratch_shapes=scratch,
        compiler_params=pltpu.CompilerParams(vmem_limit_bytes=16 * 1024 * 1024),
        cost_estimate=pl.CostEstimate(flops=flops, bytes_accessed=0, transcendentals=0) if flops else None,
    )(*args)


def columns(vol):
    shape = (512, 512)
    to, of = iota(shape, 0), iota(shape, 1)
    rows = dot(one_hot(of == (to % 64) * 8 + to // 64), vol).astype(BF)
    half = (64, 128)
    even = one_hot(iota(half, 1) == 2 * iota(half, 0))
    odd = one_hot(iota(half, 1) == 2 * iota(half, 0) + 1)
    zero = jnp.zeros((64, 128), BF)
    blocks = []
    for i in range(8):
        block = rows[64 * i : 64 * i + 64]
        left = jnp.concatenate([block, zero], axis=0)
        right = jnp.concatenate([zero, block], axis=0)
        blocks.append((dot(even, left, 1, 1) + dot(odd, right, 1, 1)).astype(BF))
    return blocks


def columns_body(vol_ref, out_ref):
    for i, block in enumerate(columns(vol_ref[...])):
        out_ref[i // 4, i % 4] = block


def pair_body(s_ref, own_ref, other_ref, out_ref):
    zh = s_ref[1]
    for i, block in enumerate(columns(other_ref[...])):
        out_ref[2 - 2 * zh + i // 4, i % 4] = block
    for i in range(2):
        out_ref[2 * zh + i] = own_ref[i]


def slabs_body(cot_ref, slab_ref):
    for i in range(16):
        for j in range(3):
            pair = i + j - 1
            if 0 <= pair < 16:
                piece = cot_ref[:, 128 * pair : 128 * pair + 128]
            else:
                piece = jnp.zeros((8, 128), BF)
            slab_ref[i, :, 128 * j : 128 * j + 128] = piece
            slab_ref[16 + i, :, 128 * j : 128 * j + 128] = piece


def weights_body(one_far, two_far, w_one_ref, w_two_ref, one_ref, two_ref, sems):
    fetch_one = pltpu.make_async_copy(one_far, one_ref, sems.at[0])
    fetch_two = pltpu.make_async_copy(two_far, two_ref, sems.at[1])
    fetch_one.start()
    fetch_two.start()
    fetch_one.wait()
    fetch_two.wait()
    w_one_ref[...] = one_ref[...]
    for i, (a, b) in enumerate(PAIRS):
        w_two_ref[:, 128 * i : 128 * i + 128] = two_ref[3 * (2 - a) + 2 - b]


def turn_body(got_ref, out_ref):
    eye = one_hot(iota((128, 128), 0) == iota((128, 128), 1))
    for q in range(2):
        for j in range(3):
            block = got_ref[128 * q : 128 * q + 128, 128 * j : 128 * j + 128]
            turned = dot(eye, block, 1, 1).astype(BF)
            out_ref[q, 2 * j] = turned[:64]
            out_ref[q, 2 * j + 1] = turned[64:]


def vol_row(deep_ref, low_ref, plane, row):
    return low_ref[row] if plane == 0 else deep_ref[plane - 1, row]


def cot_row(cot_ref, low_ref, up_ref, plane, row):
    if plane == 0:
        return low_ref[8 + row]
    return up_ref[row - 1] if plane == 3 else cot_ref[plane - 1, row]


def front_body(s_ref, deep_ref, low_ref, cot_ref, up_ref, w_one_ref, w_two_ref, hid_ref, ag_ref):
    h = s_ref[0]
    cells = [
        jnp.concatenate(
            [
                vol_row(deep_ref, low_ref, 2 * q + a, 2 * r + b)
                for q in range(2)
                for r in range(4)
            ],
            axis=0,
        )
        for a, b in PAIRS
    ]
    zero = jnp.zeros((64, 128), BF)
    left = [w_one_ref[i, 64:] for i in range(9)]
    right = [part for i in range(9) for part in (zero, w_one_ref[i, :64])]
    weights = [jnp.concatenate(parts, axis=0) for parts in (left, right)]
    acc = dot(jnp.concatenate(cells, axis=1), jnp.concatenate(weights, axis=1))
    act = acc[:, :128] + earlier(acc[:, 128:])
    small = jnp.exp(-jnp.abs(act))
    hidden = SLOPE * act + (1.0 - SLOPE) * (jnp.maximum(act, 0.0) + jnp.log1p(small))
    row = iota((512, 128), 0) // 64 % 4 + 2 * h - 1
    hidden = jnp.where((row >= 0) & (row < 32), hidden, 0.0).astype(BF)
    sigmoid = jnp.where(act >= 0.0, 1.0, small) / (1.0 + small)
    factor = SLOPE + (1.0 - SLOPE) * sigmoid
    factor = jnp.concatenate([factor[64:256], factor[320:]], axis=0)
    for q in range(2):
        for r in range(4):
            at = 64 * (4 * q + r)
            hid_ref[q, r] = hidden[at : at + 64]
    cells = [
        jnp.concatenate(
            [
                cot_row(cot_ref, low_ref, up_ref, q + a, r + 1 + b)
                for q in range(2)
                for r in range(3)
            ],
            axis=0,
        )
        for a, b in PAIRS
    ]
    acc = dot(jnp.concatenate(cells, axis=1), w_two_ref[...], 1, 1)
    grad = acc[:, 128:256] + earlier(acc[:, 256:]) + later(acc[:, :128])
    row = iota((384, 128), 0) // 64 % 3 + 2 * h
    ag = jnp.where(row < 32, grad * factor, 0.0).astype(BF)
    for q in range(2):
        for r in range(3):
            at = 64 * (3 * q + r)
            ag_ref[q, r] = ag[at : at + 64]


def kernel_grads_body(
    s_ref, deep_ref, low_ref, cot_ref, up_ref, ag_ref, hid_ref, out_far, out_ref, sems
):
    zh = s_ref[1]
    copies = []

    def put(i, value):
        out_ref[i] = value.astype(BF).reshape(16, 16, 128)
        place = out_far.at[:, :, 128 * i : 128 * i + 128]
        copies.append(pltpu.make_async_copy(out_ref.at[i], place, sems.at[i]))
        copies[-1].start()

    own_ag = jnp.concatenate([ag_ref[q, r] for q in range(2) for r in range(2)], axis=0)
    slot_row = iota((256, 128), 0)
    source = iota((256, 128), 1)
    device, slot = slot_row // 16, slot_row % 16
    pick_two = one_hot((slot < 12) & (source == device * 8 + zh * 4 + slot % 4))
    own_hid = jnp.concatenate([hid_ref[q, r + 1] for q in range(2) for r in range(2)], axis=0)
    flat = dot(pick_two, own_hid, 1, 1)
    tap = iota((256, 256), 0) % 16 // 4
    column = iota((256, 256), 1) % 64
    before = jnp.where(column == 0, 0.0, pltpu.roll(flat, 1, 1))
    after = jnp.where(column == 63, 0.0, pltpu.roll(flat, 255, 1))
    hid_rows = jnp.where(tap == 0, before, jnp.where(tap == 1, flat, after)).astype(BF)
    cots = [
        jnp.concatenate(
            [
                cot_row(cot_ref, low_ref, up_ref, q + 2 - a, r + 3 - b)
                for q in range(2)
                for r in range(2)
            ],
            axis=0,
        )
        for a, b in PAIRS
    ]
    first = dot(hid_rows, jnp.concatenate(cots, axis=1))
    channel = device * 4 + zh * 2 + slot % 2
    pick_one = one_hot((slot >= 12) & (source == (slot - 12) // 2 * 64 + channel))
    vols, picks = [], []
    for i, (a, b) in enumerate(PAIRS):
        x = jnp.concatenate(
            [
                vol_row(deep_ref, low_ref, 2 * q + a, 2 * r + 2 + b)
                for q in range(2)
                for r in range(2)
            ],
            axis=0,
        )
        vol_rows = dot(pick_one, x, 1, 1).astype(BF)
        both = first[:, 128 * i : 128 * i + 128] + dot(vol_rows, own_ag)
        put(i, both)
        vols.append(x)
        picks.append(one_hot((slot // 2 == i % 8) & (source == 64 + channel)))
    groups = (
        (9, jnp.concatenate(picks[:8], axis=1), jnp.concatenate(vols[:8], axis=1)),
        (10, picks[8], vols[8]),
    )
    for i, pick, x in groups:
        rows = dot(pick, x, 1, 1)
        rows = jnp.where(column == 0, 0.0, pltpu.roll(rows, 1, 1)).astype(BF)
        put(i, dot(rows, own_ag))
    for copy in copies:
        copy.wait()


def conv_two_body(h_ref, w_two_ref, out_ref):
    acc = jnp.zeros((128, 128), F32)
    for i, (a, b) in enumerate(PAIRS):
        x = jnp.concatenate([h_ref[a, b], h_ref[a, b + 1]], axis=0)
        wide = x.astype(F32)
        taps = jnp.concatenate([earlier(wide).astype(BF), x, later(wide).astype(BF)], axis=1)
        acc += dot(taps, w_two_ref[:, 128 * (8 - i) : 128 * (9 - i)])
    out_ref[...] = acc.T.astype(BF)


def volume_grad_body(a_ref, k_ref, out_ref):
    zero = jnp.zeros((64, 128), BF)
    half = (64, 256)
    spread = one_hot(iota(half, 1) % 128 == 2 * iota(half, 0) + iota(half, 1) // 128)
    offsets = (((1, 0),), ((0, 1), (2, 0)))
    blocks = [None] * 8
    for pi in range(2):
        for pj in range(2):
            acc = jnp.zeros((128, 256), F32)
            for a, plane in offsets[pi]:
                for b, row in offsets[pj]:
                    x = jnp.concatenate([a_ref[plane, row], a_ref[plane, row + 1]], axis=0)
                    taps = k_ref[3 * a + b]
                    weights = jnp.concatenate([taps[64:], zero, taps[:64]], axis=0)
                    acc += dot(x, weights, 1, 1)
            cells = (acc[:, :128] + later(acc[:, 128:])).astype(BF)
            for r in range(2):
                wide = dot(cells[64 * r : 64 * r + 64], spread, 0, 0)
                blocks[4 * pi + 2 * r + pj] = (wide[:64, :128] + wide[64:, 128:]).astype(BF)
    shape = (512, 512)
    to, of = iota(shape, 0), iota(shape, 1)
    turn = one_hot(of == (to % 8) * 64 + to // 8)
    out_ref[...] = dot(turn, jnp.concatenate(blocks, axis=0)).astype(BF)


def plane_sum_body(got_ref, next_ref, out_ref):
    total = got_ref[0].astype(F32)
    for i in range(1, 16):
        total += got_ref[i].astype(F32)
    pieces = [total[:, 128 * j : 128 * j + 128] for j in range(11)]
    rows = jnp.concatenate(pieces + [jnp.zeros((80, 128), F32)], axis=0)
    out_ref[:, :128] = next_ref[...]
    out_ref[:, 128:] = rows.T.astype(BF)


def finish_body(scale, got_ref, next_ref, one_ref, two_ref):
    total = got_ref[0][:, 128:].astype(F32)
    for i in range(1, 16):
        total += got_ref[i][:, 128:].astype(F32)
    table = (total * scale).T
    for i in range(9):
        one_ref[3 * i] = table[144 + 2 * i : 146 + 2 * i]
        one_ref[3 * i + 1] = table[16 * i + 12 : 16 * i + 14]
        one_ref[3 * i + 2] = table[16 * i + 14 : 16 * i + 16]
        for e in range(3):
            two_ref[3 * i + e] = table[16 * i + 4 * e : 16 * i + 4 * e + 4]
    cells = jnp.concatenate([got_ref[i][:, :128].astype(F32) for i in range(16)], axis=0).astype(BF)
    to, of = iota((256, 128), 0), iota((256, 128), 1)
    source = to % 32 // 2 * 8 + to // 32
    left = dot(one_hot((of == source) & (to % 2 == 0)), cells)
    right = dot(one_hot((of == source) & (to % 2 == 1)), cells)
    rows = left[:, :64] + right[:, 64:]
    next_ref[...] = rows.reshape(8, 32, 64).astype(BF)


def shifted(block, axis, distance):
    size = lax.axis_size(axis)
    route = [(i, i + distance) for i in range(size) if 0 <= i + distance < size]
    return lax.ppermute(block, axis, route)


def shape(dims, kind=BF):
    return jax.ShapeDtypeStruct(dims, kind)


def per_device(volume, kernel_one, kernel_two, cotangent):
    zh = lax.axis_index("zh")
    h = lax.axis_index(HEIGHT)
    here = jnp.stack([h, zh]).astype(jnp.int32)
    one = kernel_one.reshape(9, 192, 128)
    two = kernel_two.reshape(9, 384, 128)
    planes = lax.axis_size(PLANE)

    other = lax.ppermute(volume, "zh", [(0, 1), (1, 0)])
    slabs = call(slabs_body, shape((32, 8, 384)), cotangent.reshape(8, 2048))
    slab = lax.all_to_all(slabs, LINE, 0, 0, tiled=True)
    own = call(columns_body, shape((2, 4, 64, 128)), volume.reshape(512, 128))
    weights = call(
        weights_body,
        [shape((9, 192, 128)), shape((384, 1152))],
        one,
        two,
        far=2,
        scratch=(
            pltpu.VMEM((9, 192, 128), BF),
            pltpu.VMEM((9, 384, 128), BF),
            pltpu.SemaphoreType.DMA((2,)),
        ),
    )
    other, own, *weights = lax.optimization_barrier((other, own, *weights))
    deep = call(
        pair_body,
        shape((4, 4, 64, 128)),
        here,
        own,
        other.reshape(512, 128),
        scalars=1,
        flops=40 * 10**9,
    )
    deep = jnp.concatenate(
        [shifted(deep[:, 1:], HEIGHT, 1), deep, shifted(deep[:, :2], HEIGHT, -1)], axis=1
    )
    cot = call(turn_body, shape((2, 6, 64, 128)), slab.reshape(256, 384))
    lower = shifted(jnp.concatenate([deep[3], cot[1, 1:]], axis=0), PLANE, 1)
    upper = shifted(cot[0, 1:], PLANE, -1)

    hidden, ag = call(
        front_body,
        [shape((2, 4, 64, 128)), shape((2, 3, 64, 128))],
        here,
        deep,
        lower,
        cot,
        upper,
        *weights,
        scalars=1,
    )
    up = [(2 * k, 2 * k + 2) for k in range(planes - 1)]
    down = [(2 * k + 1, 2 * k - 1) for k in range(1, planes)]
    edge = jnp.concatenate([jnp.where(zh == 0, hidden[1], hidden[0]), ag[0]], axis=0)
    edge = lax.ppermute(edge, DEPTH, up + down)
    partial = call(
        kernel_grads_body,
        shape((16, 16, 1408)),
        here,
        deep,
        lower,
        cot,
        upper,
        ag,
        hidden,
        scalars=1,
        far_out=True,
        scratch=(pltpu.VMEM((11, 16, 16, 128), BF), pltpu.SemaphoreType.DMA((11,))),
    )
    parts = lax.all_to_all(partial, PLANE, 0, 0, tiled=True)

    side = edge[None, :4]
    three = jnp.where(
        zh == 0, jnp.concatenate([side, hidden], axis=0), jnp.concatenate([hidden, side], axis=0)
    )
    next_own = call(conv_two_body, shape((128, 128)), three, weights[1])
    pair = jnp.where(zh == 0, ag, jnp.concatenate([ag[1:], edge[None, 4:]], axis=0))
    volume_grad = call(volume_grad_body, shape((512, 128)), pair, weights[0]).reshape(volume.shape)
    parts, volume_grad = lax.optimization_barrier((parts, volume_grad))

    summed = call(plane_sum_body, shape((128, 384)), parts, next_own)
    rows = lax.all_to_all(summed.reshape(16, 8, 384), HEIGHT, 0, 0, tiled=True)
    next_acts, one_grad, two_grad = call(
        functools.partial(finish_body, 1.0 / math.sqrt(65536)),
        [shape((8, 32, 64)), shape((27, 2, 8), F32), shape((27, 4, 8), F32)],
        rows,
    )
    return (
        next_acts.reshape(cotangent.shape),
        volume_grad,
        one_grad.reshape(3, 3, 3, 2, 8),
        two_grad.reshape(3, 3, 3, 4, 8),
    )


def solution(mesh):
    fine = Mesh(mesh.devices.reshape(4, 4, 2, 8, 2), DEPTH + HEIGHT)
    placed = (P(None, DEPTH, HEIGHT, None), P(), P(), P(HEIGHT, DEPTH, None, None))
    return jax.shard_map(
        per_device,
        mesh=fine,
        in_specs=placed,
        out_specs=(
            P(HEIGHT, DEPTH, None, None),
            P(None, DEPTH, HEIGHT, None),
            P(None, None, None, DEPTH, HEIGHT),
            P(None, None, None, DEPTH, HEIGHT),
        ),
        check_vma=False,
    )
```

time: 105 us -> 102 us (0.971)
  starting transfers between devices: 52.3 us -> 48.2 us
  Pallas kernels: 10.4 us -> 11.5 us
    ppermute x4, starting transfers between devices: 17.7 us -> 14.1 us  [shifted(): return lax.ppermute(block, axis, route)]
    pallas_call x11, Pallas kernels: 10.4 us -> 11.5 us  [call(): pl.pallas_call(body, out_shape=outs, in_specs=[smem] * scalars + [vmem] *...]
  transfers between devices with their start and end apart: 8 -> 8, of which waited for: 4 -> 3; matrix products, arithmetic and copies ran while one was open for 0% -> 1% of each run, Pallas kernels for 7% -> 8%
where the time goes in v5:
time: 102 us; the launch traced here: 101 us
  starting transfers between devices  48.2 us (47%)
  blocking collectives  19.5 us (19%)
  waiting for transfers between devices  17.8 us (17%)
  Pallas kernels  11.5 us (11%)
  local copies, waits for them, and re-layouts  2.96 us (3%)
    all_to_all x1, blocking collectives, per_device(): rows = lax.all_to_all(summed.reshape(16, 8, 384), HEIGHT, 0, 0, tiled=True)  19.5 us
    ppermute x1, starting transfers between devices, per_device(): other = lax.ppermute(volume, 'zh', [(0, 1), (1, 0)])  16.4 us
    ppermute x4, starting transfers between devices, shifted(): return lax.ppermute(block, axis, route)  14.1 us
    pallas_call x11, Pallas kernels, call(): pl.pallas_call(body, out_shape=outs, in_specs=[smem] * scalars + [vmem] *...  11.5 us
    all_to_all x1, waiting for transfers between devices, per_device(): parts = lax.all_to_all(partial, PLANE, 0, 0, tiled=True)  9.34 us
    ppermute x4, waiting for transfers between devices, shifted(): return lax.ppermute(block, axis, route)  8.48 us
    all_to_all x1, starting transfers between devices, per_device(): parts = lax.all_to_all(partial, PLANE, 0, 0, tiled=True)  7.97 us
    all_to_all x1, starting transfers between devices, per_device(): slab = lax.all_to_all(slabs, LINE, 0, 0, tiled=True)  6.13 us
  transfers between devices with their start and end apart: 8, of which 3 were waited for; matrix products, arithmetic and copies ran while one was open for 1% of the time, Pallas kernels for 8%

profile of v5, /device:TPU:1, one launch (start us, length us, event | category | flops | bytes accessed | tf_op | source)
XLA Modules:
  0.0 101.1 jit_solution(3961846309569624207)
XLA Ops:
  0.6 16.4 %collective-permute-start = (bf16[64,2,4,128]{3,2,1,0:T(4,128)(2,1)}, bf16[64,2,4,128]{3,2,1,0:T(4,128)(2,1)S(1)}, u32[]{:S(2)}, u32[]{:S(2)}) collective-permute-start(bf16[64,2,4,128]{3,2,1,0:T(4,128)(2,1)} %param.4), channel_id=1, source_target_pairs={{0,16},{16,0},{1,17},{17,1},{2,18},{18,2},{3,19},{19,3},{4,20},{20... | collective-permute-start | bytes 393224 | tf_op jit(solution)/shard_map/ppermute | solution.py:331
  17.1 1.0 reshape.47.cot_ref
  18.0 0.7 shard_map.78
  18.7 6.1 %all-to-all-start = ((bf16[32,8,384]{2,1,0:T(8,128)(2,1)}), bf16[32,8,384]{2,1,0:T(8,128)(2,1)S(1)}, u32[]{:S(2)}, u32[]{:S(2)}) async-start(bf16[32,8,384]{2,1,0:T(8,128)(2,1)} %shard_map.78), calls=%async_computation | async-start | bytes 393216 | tf_op jit(solution)/shard_map/all_to_all | solution.py:333
  24.9 0.9 copy-done.2
  25.8 0.7 shard_map.75.own_ref
  26.5 1.0 copy-done.1
  27.5 0.6 shard_map.76
  28.3 1.3 %shard_map.77 = bf16[4,4,64,128]{3,2,1,0:T(8,128)(2,1)S(1)} custom-call(s32[2]{0:T(128)S(1)} %pad_add_fusion.s_ref, bf16[2,4,64,128]{3,2,1,0:T(8,128)(2,1)S(1)} %shard_map.75.own_ref, bf16[512,128]{1,0:T(8,128)(2,1)S(1)} %bitcast.35), custom_call_target="tpu_custom_call" | custom-call | flops 40000000000 | tf_op jit(solution)/shard_map/pallas_call | solution.py:47
  29.6 7.7 %collective-permute-start.1 = (bf16[4,3,64,128]{3,2,1,0:T(8,128)(2,1)S(1)}, bf16[4,3,64,128]{3,2,1,0:T(8,128)(2,1)S(1)}, u32[]{:S(2)}, u32[]{:S(2)}) collective-permute-start(bf16[4,3,64,128]{3,2,1,0:T(8,128)(2,1)S(1)} %slice.44), channel_id=1, source_target_pairs={{0,1},{1,2},{2,3},{3,4},{4,5},{5,6},{6,7},{7,8},{8,9},{9,10},{10,1... | collective-permute-start | bytes 589832 | tf_op jit(solution)/shard_map/ppermute | solution.py:316
  37.3 1.9 %collective-permute-start.2 = (bf16[4,2,64,128]{3,2,1,0:T(8,128)(2,1)S(1)}, bf16[4,2,64,128]{3,2,1,0:T(8,128)(2,1)S(1)}, u32[]{:S(2)}, u32[]{:S(2)}) collective-permute-start(bf16[4,2,64,128]{3,2,1,0:T(8,128)(2,1)S(1)} %slice.45), channel_id=1, source_target_pairs={{1,0},{2,1},{3,2},{4,3},{5,4},{6,5},{7,6},{8,7},{9,8},{10,9},{11,1... | collective-permute-start | bytes 393224 | tf_op jit(solution)/shard_map/ppermute | solution.py:316
  39.2 4.6 %collective-permute-done.2 = bf16[4,2,64,128]{3,2,1,0:T(8,128)(2,1)S(1)} collective-permute-done((bf16[4,2,64,128]{3,2,1,0:T(8,128)(2,1)S(1)}, bf16[4,2,64,128]{3,2,1,0:T(8,128)(2,1)S(1)}, u32[]{:S(2)}, u32[]{:S(2)}) %collective-permute-start.2) | collective-permute-done | bytes 131104 | tf_op jit(solution)/shard_map/ppermute | solution.py:316
  44.2 3.2 %collective-permute-start.3 = (bf16[14,64,128]{2,1,0:T(8,128)(2,1)S(1)}, bf16[14,64,128]{2,1,0:T(8,128)(2,1)S(1)}, u32[]{:S(2)}, u32[]{:S(2)}) collective-permute-start(bf16[14,64,128]{2,1,0:T(8,128)(2,1)S(1)} %pad_maximum_fusion.1), channel_id=1, source_target_pairs={{0,32},{32,64},{64,96},{96,128},{128,160},{160,192},{192,224},{224... | collective-permute-start | bytes 688136 | tf_op jit(solution)/shard_map/ppermute | solution.py:316
  47.4 1.3 %collective-permute-start.4 = (bf16[5,64,128]{2,1,0:T(8,128)(2,1)S(1)}, bf16[5,64,128]{2,1,0:T(8,128)(2,1)S(1)}, u32[]{:S(2)}, u32[]{:S(2)}) collective-permute-start(bf16[5,64,128]{2,1,0:T(8,128)(2,1)S(1)} %get-tuple-element.34), channel_id=1, source_target_pairs={{32,0},{64,32},{96,64},{128,96},{160,128},{192,160},{224,192},{256... | collective-permute-start | bytes 245768 | tf_op jit(solution)/shard_map/ppermute | solution.py:316
  48.7 3.9 %collective-permute-done.4.up_ref = bf16[5,64,128]{2,1,0:T(8,128)(2,1)S(1)} collective-permute-done((bf16[5,64,128]{2,1,0:T(8,128)(2,1)S(1)}, bf16[5,64,128]{2,1,0:T(8,128)(2,1)S(1)}, u32[]{:S(2)}, u32[]{:S(2)}) %collective-permute-start.4) | collective-permute-done | bytes 81952 | tf_op jit(solution)/shard_map/ppermute | solution.py:316
  52.6 1.7 %shard_map.80 = (bf16[2,4,64,128]{3,2,1,0:T(8,128)(2,1)S(1)}, bf16[2,3,64,128]{3,2,1,0:T(8,128)(2,1)S(1)}) custom-call(s32[2]{0:T(128)S(1)} %pad_add_fusion.s_ref, bf16[4,9,64,128]{3,2,1,0:T(8,128)(2,1)S(1)} %pad_maximum_fusion.deep_ref, bf16[14,64,128]{2,1,0:T(8,128)(2,1)S(1)} %collective-permute-done.3.low_ref, ...), custom_call_target="tpu_custom_call" | custom-call | tf_op jit(solution)/shard_map/pallas_call | solution.py:47
  54.4 3.6 %collective-permute-start.5 = (bf16[7,64,128]{2,1,0:T(8,128)(2,1)S(1)}, bf16[7,64,128]{2,1,0:T(8,128)(2,1)S(1)}, u32[]{:S(2)}, u32[]{:S(2)}) collective-permute-start(bf16[7,64,128]{2,1,0:T(8,128)(2,1)S(1)} %pad_maximum_fusion.2), channel_id=1, source_target_pairs={{0,32},{32,64},{64,96},{96,128},{128,160},{160,192},{192,224},{224... | collective-permute-start | bytes 344072 | tf_op jit(solution)/shard_map/ppermute | solution.py:378
  58.0 3.1 %shard_map.81 = bf16[16,16,1408]{2,1,0:T(8,128)(2,1)} custom-call(s32[2]{0:T(128)S(1)} %pad_add_fusion.s_ref, bf16[4,9,64,128]{3,2,1,0:T(8,128)(2,1)S(1)} %pad_maximum_fusion.deep_ref, bf16[14,64,128]{2,1,0:T(8,128)(2,1)S(1)} %collective-permute-done.3.low_ref, bf16[2,6,64,128]{3,2,1,0:T(8,128)(2,1)S(1)} %shard_map.79.cot_ref, ...), custom_call_target="tpu_custom_call" | custom-call | tf_op jit(solution)/shard_map/pallas_call | solution.py:47
  61.1 8.0 %all-to-all-start.1 = ((bf16[16,16,1408]{2,1,0:T(8,128)(2,1)}), bf16[16,16,1408]{2,1,0:T(8,128)(2,1)S(1)}, u32[]{:S(2)}, u32[]{:S(2)}) async-start(bf16[16,16,1408]{2,1,0:T(8,128)(2,1)} %shard_map.81), calls=%async_computation.1 | async-start | bytes 1441792 | tf_op jit(solution)/shard_map/all_to_all | solution.py:393
  69.2 0.5 shard_map.83.next_ref
  69.7 1.6 %shard_map.82 = bf16[512,128]{1,0:T(8,128)(2,1)} custom-call(bf16[2,3,64,128]{3,2,1,0:T(8,128)(2,1)S(1)} %maximum_select_fusion.1.a_ref, bf16[9,192,128]{2,1,0:T(8,128)(2,1)S(1)} %get-tuple-element.21.w_one_ref.k_ref), custom_call_target="tpu_custom_call" | custom-call | tf_op jit(solution)/shard_map/pallas_call | solution.py:47
  71.2 9.3 %all-to-all-done.1.got_ref = bf16[16,16,1408]{2,1,0:T(8,128)(2,1)S(1)} async-done(((bf16[16,16,1408]{2,1,0:T(8,128)(2,1)}), bf16[16,16,1408]{2,1,0:T(8,128)(2,1)S(1)}, u32[]{:S(2)}, u32[]{:S(2)}) %all-to-all-start.1) | async-done | bytes 720928 | tf_op jit(solution)/shard_map/all_to_all | solution.py:393
  80.7 19.5 %all_to_all.15.got_ref = bf16[16,8,384]{2,1,0:T(8,128)(2,1)S(1)} all-to-all(bf16[16,8,384]{2,1,0:T(8,128)(2,1)S(1)} %bitcast.33), channel_id=1, replica_groups=mesh['x'=4,'y'=4,'zh'=2,'zl'=8,'core'=2] {'zl','core'}, dimensions={0} | all-to-all | bytes 196608 | tf_op jit(solution)/shard_map/all_to_all | solution.py:405
  100.2 0.9 shard_map.85
  (25 shorter events, 0.8 us)
Async XLA Ops:
  0.6 25.9 %copy-start = (bf16[3,3,3,128,128]{4,3,2,1,0:T(8,128)(2,1)S(1)}, bf16[3,3,3,128,128]{4,3,2,1,0:T(8,128)(2,1)}, u32[]{:S(2)}) copy-start(bf16[3,3,3,128,128]{4,3,2,1,0:T(8,128)(2,1)} %param.6) | copy-start | bytes 2654212
  0.6 27.6 %collective-permute-start = (bf16[64,2,4,128]{3,2,1,0:T(4,128)(2,1)}, bf16[64,2,4,128]{3,2,1,0:T(4,128)(2,1)S(1)}, u32[]{:S(2)}, u32[]{:S(2)}) collective-permute-start(bf16[64,2,4,128]{3,2,1,0:T(4,128)(2,1)} %param.4), channel_id=1, source_target_pairs={{0,16},{16,0},{1,17},{17,1},{2,18},{18,2},{3,19},{19,3},{4,20},{20... | collective-permute-start | bytes 393224 | tf_op jit(solution)/shard_map/ppermute | solution.py:331
  18.7 25.2 %all-to-all-start = ((bf16[32,8,384]{2,1,0:T(8,128)(2,1)}), bf16[32,8,384]{2,1,0:T(8,128)(2,1)S(1)}, u32[]{:S(2)}, u32[]{:S(2)}) async-start(bf16[32,8,384]{2,1,0:T(8,128)(2,1)} %shard_map.78), calls=%async_computation | async-start | bytes 393216 | tf_op jit(solution)/shard_map/all_to_all | solution.py:333
  24.9 0.9 copy-start.2
  26.5 1.0 %copy-start.1 = (bf16[3,3,3,64,128]{4,3,2,1,0:T(8,128)(2,1)S(1)}, bf16[3,3,3,64,128]{4,3,2,1,0:T(8,128)(2,1)}, u32[]{:S(2)}) copy-start(bf16[3,3,3,64,128]{4,3,2,1,0:T(8,128)(2,1)} %param.5) | copy-start | bytes 1327108
  29.6 14.2 %collective-permute-start.1 = (bf16[4,3,64,128]{3,2,1,0:T(8,128)(2,1)S(1)}, bf16[4,3,64,128]{3,2,1,0:T(8,128)(2,1)S(1)}, u32[]{:S(2)}, u32[]{:S(2)}) collective-permute-start(bf16[4,3,64,128]{3,2,1,0:T(8,128)(2,1)S(1)} %slice.44), channel_id=1, source_target_pairs={{0,1},{1,2},{2,3},{3,4},{4,5},{5,6},{6,7},{7,8},{8,9},{9,10},{10,1... | collective-permute-start | bytes 589832 | tf_op jit(solution)/shard_map/ppermute | solution.py:316
  37.3 6.5 %collective-permute-start.2 = (bf16[4,2,64,128]{3,2,1,0:T(8,128)(2,1)S(1)}, bf16[4,2,64,128]{3,2,1,0:T(8,128)(2,1)S(1)}, u32[]{:S(2)}, u32[]{:S(2)}) collective-permute-start(bf16[4,2,64,128]{3,2,1,0:T(8,128)(2,1)S(1)} %slice.45), channel_id=1, source_target_pairs={{1,0},{2,1},{3,2},{4,3},{5,4},{6,5},{7,6},{8,7},{9,8},{10,9},{11,1... | collective-permute-start | bytes 393224 | tf_op jit(solution)/shard_map/ppermute | solution.py:316
  44.2 8.4 %collective-permute-start.3 = (bf16[14,64,128]{2,1,0:T(8,128)(2,1)S(1)}, bf16[14,64,128]{2,1,0:T(8,128)(2,1)S(1)}, u32[]{:S(2)}, u32[]{:S(2)}) collective-permute-start(bf16[14,64,128]{2,1,0:T(8,128)(2,1)S(1)} %pad_maximum_fusion.1), channel_id=1, source_target_pairs={{0,32},{32,64},{64,96},{96,128},{128,160},{160,192},{192,224},{224... | collective-permute-start | bytes 688136 | tf_op jit(solution)/shard_map/ppermute | solution.py:316
  47.4 5.2 %collective-permute-start.4 = (bf16[5,64,128]{2,1,0:T(8,128)(2,1)S(1)}, bf16[5,64,128]{2,1,0:T(8,128)(2,1)S(1)}, u32[]{:S(2)}, u32[]{:S(2)}) collective-permute-start(bf16[5,64,128]{2,1,0:T(8,128)(2,1)S(1)} %get-tuple-element.34), channel_id=1, source_target_pairs={{32,0},{64,32},{96,64},{128,96},{160,128},{192,160},{224,192},{256... | collective-permute-start | bytes 245768 | tf_op jit(solution)/shard_map/ppermute | solution.py:316
  54.4 14.7 %collective-permute-start.5 = (bf16[7,64,128]{2,1,0:T(8,128)(2,1)S(1)}, bf16[7,64,128]{2,1,0:T(8,128)(2,1)S(1)}, u32[]{:S(2)}, u32[]{:S(2)}) collective-permute-start(bf16[7,64,128]{2,1,0:T(8,128)(2,1)S(1)} %pad_maximum_fusion.2), channel_id=1, source_target_pairs={{0,32},{32,64},{64,96},{96,128},{128,160},{160,192},{192,224},{224... | collective-permute-start | bytes 344072 | tf_op jit(solution)/shard_map/ppermute | solution.py:378
  61.1 19.4 %all-to-all-start.1 = ((bf16[16,16,1408]{2,1,0:T(8,128)(2,1)}), bf16[16,16,1408]{2,1,0:T(8,128)(2,1)S(1)}, u32[]{:S(2)}, u32[]{:S(2)}) async-start(bf16[16,16,1408]{2,1,0:T(8,128)(2,1)} %shard_map.81), calls=%async_computation.1 | async-start | bytes 1441792 | tf_op jit(solution)/shard_map/all_to_all | solution.py:393

commit v6 on v5

--- a/solution.py
+++ b/solution.py
@@ -72,17 +72,12 @@
     return blocks
 
 
-def columns_body(vol_ref, out_ref):
-    for i, block in enumerate(columns(vol_ref[...])):
-        out_ref[i // 4, i % 4] = block
-
-
 def pair_body(s_ref, own_ref, other_ref, out_ref):
     zh = s_ref[1]
+    for i, block in enumerate(columns(own_ref[...])):
+        out_ref[2 * zh + i // 4, i % 4] = block
     for i, block in enumerate(columns(other_ref[...])):
         out_ref[2 - 2 * zh + i // 4, i % 4] = block
-    for i in range(2):
-        out_ref[2 * zh + i] = own_ref[i]
 
 
 def slabs_body(cot_ref, slab_ref):
@@ -331,7 +326,18 @@
     other = lax.ppermute(volume, "zh", [(0, 1), (1, 0)])
     slabs = call(slabs_body, shape((32, 8, 384)), cotangent.reshape(8, 2048))
     slab = lax.all_to_all(slabs, LINE, 0, 0, tiled=True)
-    own = call(columns_body, shape((2, 4, 64, 128)), volume.reshape(512, 128))
+    deep = call(
+        pair_body,
+        shape((4, 4, 64, 128)),
+        here,
+        volume.reshape(512, 128),
+        other.reshape(512, 128),
+        scalars=1,
+        flops=40 * 10**9,
+    )
+    deep = jnp.concatenate(
+        [shifted(deep[:, 1:], HEIGHT, 1), deep, shifted(deep[:, :2], HEIGHT, -1)], axis=1
+    )
     weights = call(
         weights_body,
         [shape((9, 192, 128)), shape((384, 1152))],
@@ -344,19 +350,7 @@
             pltpu.SemaphoreType.DMA((2,)),
         ),
     )
-    other, own, *weights = lax.optimization_barrier((other, own, *weights))
-    deep = call(
-        pair_body,
-        shape((4, 4, 64, 128)),
-        here,
-        own,
-        other.reshape(512, 128),
-        scalars=1,
-        flops=40 * 10**9,
-    )
-    deep = jnp.concatenate(
-        [shifted(deep[:, 1:], HEIGHT, 1), deep, shifted(deep[:, :2], HEIGHT, -1)], axis=1
-    )
+    deep, *weights = lax.optimization_barrier((deep, *weights))
     cot = call(turn_body, shape((2, 6, 64, 128)), slab.reshape(256, 384))
     lower = shifted(jnp.concatenate([deep[3], cot[1, 1:]], axis=0), PLANE, 1)
     upper = shifted(cot[0, 1:], PLANE, -1)

time: 102 us -> 101 us (level)
  starting transfers between devices: 48.2 us -> 51.5 us
  local copies, waits for them, and re-layouts: 2.96 us -> 1.06 us
  blocking collectives: 19.5 us -> 17.9 us
    ppermute x4, starting transfers between devices: 14.1 us -> 17.5 us  [shifted(): return lax.ppermute(block, axis, route)]
    unnamed x6, local copies, waits for them, and re-layouts: 1.93 us -> 0.02 us
    all_to_all x1, blocking collectives: 19.5 us -> 17.9 us  [per_device(): rows = lax.all_to_all(summed.reshape(16, 8, 384), HEIGHT, 0, 0, tiled=True)]
    pallas_call x11 -> x10, Pallas kernels: 11.5 us -> 11.2 us  [call(): pl.pallas_call(body, out_shape=outs, in_specs=[smem] * scalars + [vmem] *...]
where the time goes in v6:
time: 101 us
  starting transfers between devices  51.5 us (51%)
  waiting for transfers between devices  18.1 us (18%)
  blocking collectives  17.9 us (18%)
  Pallas kernels  11.2 us (11%)
  local copies, waits for them, and re-layouts  1.06 us (1%)
    all_to_all x1, blocking collectives, per_device(): rows = lax.all_to_all(summed.reshape(16, 8, 384), HEIGHT, 0, 0, tiled=True)  17.9 us
    ppermute x4, starting transfers between devices, shifted(): return lax.ppermute(block, axis, route)  17.5 us
    ppermute x1, starting transfers between devices, per_device(): other = lax.ppermute(volume, 'zh', [(0, 1), (1, 0)])  16.3 us
    pallas_call x10, Pallas kernels, call(): pl.pallas_call(body, out_shape=outs, in_specs=[smem] * scalars + [vmem] *...  11.2 us
    all_to_all x1, waiting for transfers between devices, per_device(): parts = lax.all_to_all(partial, PLANE, 0, 0, tiled=True)  10.1 us
    ppermute x4, waiting for transfers between devices, shifted(): return lax.ppermute(block, axis, route)  8 us
    all_to_all x1, starting transfers between devices, per_device(): parts = lax.all_to_all(partial, PLANE, 0, 0, tiled=True)  7.97 us
    all_to_all x1, starting transfers between devices, per_device(): slab = lax.all_to_all(slabs, LINE, 0, 0, tiled=True)  6.26 us
  transfers between devices with their start and end apart: 8, of which 3 were waited for; matrix products, arithmetic and copies ran while one was open for 1% of the time, Pallas kernels for 8%

profile of v6, /device:TPU:1, one launch (start us, length us, event | category | flops | bytes accessed | tf_op | source)
XLA Modules:
  0.0 100.9 jit_solution(2991091948074014261)
XLA Ops:
  0.6 16.3 %collective-permute-start = (bf16[64,2,4,128]{3,2,1,0:T(4,128)(2,1)}, bf16[64,2,4,128]{3,2,1,0:T(4,128)(2,1)S(1)}, u32[]{:S(2)}, u32[]{:S(2)}) collective-permute-start(bf16[64,2,4,128]{3,2,1,0:T(4,128)(2,1)} %param.4), channel_id=1, source_target_pairs={{0,16},{16,0},{1,17},{17,1},{2,18},{18,2},{3,19},{19,3},{4,20},{20... | collective-permute-start | bytes 393224 | tf_op jit(solution)/shard_map/ppermute | solution.py:326
  16.9 1.0 reshape.47.cot_ref
  17.9 0.7 shard_map.77
  18.6 6.3 %all-to-all-start = ((bf16[32,8,384]{2,1,0:T(8,128)(2,1)}), bf16[32,8,384]{2,1,0:T(8,128)(2,1)S(1)}, u32[]{:S(2)}, u32[]{:S(2)}) async-start(bf16[32,8,384]{2,1,0:T(8,128)(2,1)} %shard_map.77), calls=%async_computation | async-start | bytes 393216 | tf_op jit(solution)/shard_map/all_to_all | solution.py:328
  24.9 0.1 pad_add_fusion.s_ref
  24.9 1.6 %shard_map.75 = bf16[4,4,64,128]{3,2,1,0:T(8,128)(2,1)S(1)} custom-call(s32[2]{0:T(128)S(1)} %pad_add_fusion.s_ref, bf16[512,128]{1,0:T(8,128)(2,1)S(1)} %bitcast.34, bf16[512,128]{1,0:T(8,128)(2,1)S(1)} %bitcast.35), custom_call_target="tpu_custom_call" | custom-call | flops 40000000000 | tf_op jit(solution)/shard_map/pallas_call | solution.py:47
  26.6 11.1 %collective-permute-start.1 = (bf16[4,3,64,128]{3,2,1,0:T(8,128)(2,1)S(1)}, bf16[4,3,64,128]{3,2,1,0:T(8,128)(2,1)S(1)}, u32[]{:S(2)}, u32[]{:S(2)}) collective-permute-start(bf16[4,3,64,128]{3,2,1,0:T(8,128)(2,1)S(1)} %slice.44), channel_id=1, source_target_pairs={{0,1},{1,2},{2,3},{3,4},{4,5},{5,6},{6,7},{7,8},{8,9},{9,10},{10,1... | collective-permute-start | bytes 589832 | tf_op jit(solution)/shard_map/ppermute | solution.py:311
  37.8 1.9 %collective-permute-start.2 = (bf16[4,2,64,128]{3,2,1,0:T(8,128)(2,1)S(1)}, bf16[4,2,64,128]{3,2,1,0:T(8,128)(2,1)S(1)}, u32[]{:S(2)}, u32[]{:S(2)}) collective-permute-start(bf16[4,2,64,128]{3,2,1,0:T(8,128)(2,1)S(1)} %slice.45), channel_id=1, source_target_pairs={{1,0},{2,1},{3,2},{4,3},{5,4},{6,5},{7,6},{8,7},{9,8},{10,9},{11,1... | collective-permute-start | bytes 393224 | tf_op jit(solution)/shard_map/ppermute | solution.py:311
  39.7 0.6 shard_map.76
  40.4 3.7 %collective-permute-done.2 = bf16[4,2,64,128]{3,2,1,0:T(8,128)(2,1)S(1)} collective-permute-done((bf16[4,2,64,128]{3,2,1,0:T(8,128)(2,1)S(1)}, bf16[4,2,64,128]{3,2,1,0:T(8,128)(2,1)S(1)}, u32[]{:S(2)}, u32[]{:S(2)}) %collective-permute-start.2) | collective-permute-done | bytes 131104 | tf_op jit(solution)/shard_map/ppermute | solution.py:311
  44.2 0.2 shard_map.78.cot_ref
  44.5 3.2 %collective-permute-start.3 = (bf16[14,64,128]{2,1,0:T(8,128)(2,1)S(1)}, bf16[14,64,128]{2,1,0:T(8,128)(2,1)S(1)}, u32[]{:S(2)}, u32[]{:S(2)}) collective-permute-start(bf16[14,64,128]{2,1,0:T(8,128)(2,1)S(1)} %pad_maximum_fusion.1), channel_id=1, source_target_pairs={{0,32},{32,64},{64,96},{96,128},{128,160},{160,192},{192,224},{224... | collective-permute-start | bytes 688136 | tf_op jit(solution)/shard_map/ppermute | solution.py:311
  47.7 1.3 %collective-permute-start.4 = (bf16[5,64,128]{2,1,0:T(8,128)(2,1)S(1)}, bf16[5,64,128]{2,1,0:T(8,128)(2,1)S(1)}, u32[]{:S(2)}, u32[]{:S(2)}) collective-permute-start(bf16[5,64,128]{2,1,0:T(8,128)(2,1)S(1)} %get-tuple-element.32), channel_id=1, source_target_pairs={{32,0},{64,32},{96,64},{128,96},{160,128},{192,160},{224,192},{256... | collective-permute-start | bytes 245768 | tf_op jit(solution)/shard_map/ppermute | solution.py:311
  49.0 4.3 %collective-permute-done.4.up_ref = bf16[5,64,128]{2,1,0:T(8,128)(2,1)S(1)} collective-permute-done((bf16[5,64,128]{2,1,0:T(8,128)(2,1)S(1)}, bf16[5,64,128]{2,1,0:T(8,128)(2,1)S(1)}, u32[]{:S(2)}, u32[]{:S(2)}) %collective-permute-start.4) | collective-permute-done | bytes 81952 | tf_op jit(solution)/shard_map/ppermute | solution.py:311
  53.3 1.7 %shard_map.79 = (bf16[2,4,64,128]{3,2,1,0:T(8,128)(2,1)S(1)}, bf16[2,3,64,128]{3,2,1,0:T(8,128)(2,1)S(1)}) custom-call(s32[2]{0:T(128)S(1)} %pad_add_fusion.s_ref, bf16[4,9,64,128]{3,2,1,0:T(8,128)(2,1)S(1)} %pad_maximum_fusion.deep_ref, bf16[14,64,128]{2,1,0:T(8,128)(2,1)S(1)} %collective-permute-done.3.low_ref, ...), custom_call_target="tpu_custom_call" | custom-call | tf_op jit(solution)/shard_map/pallas_call | solution.py:47
  55.1 3.5 %collective-permute-start.5 = (bf16[7,64,128]{2,1,0:T(8,128)(2,1)S(1)}, bf16[7,64,128]{2,1,0:T(8,128)(2,1)S(1)}, u32[]{:S(2)}, u32[]{:S(2)}) collective-permute-start(bf16[7,64,128]{2,1,0:T(8,128)(2,1)S(1)} %pad_maximum_fusion.2), channel_id=1, source_target_pairs={{0,32},{32,64},{64,96},{96,128},{128,160},{160,192},{192,224},{224... | collective-permute-start | bytes 344072 | tf_op jit(solution)/shard_map/ppermute | solution.py:372
  58.5 3.1 %shard_map.80 = bf16[16,16,1408]{2,1,0:T(8,128)(2,1)} custom-call(s32[2]{0:T(128)S(1)} %pad_add_fusion.s_ref, bf16[4,9,64,128]{3,2,1,0:T(8,128)(2,1)S(1)} %pad_maximum_fusion.deep_ref, bf16[14,64,128]{2,1,0:T(8,128)(2,1)S(1)} %collective-permute-done.3.low_ref, bf16[2,6,64,128]{3,2,1,0:T(8,128)(2,1)S(1)} %shard_map.78.cot_ref, ...), custom_call_target="tpu_custom_call" | custom-call | tf_op jit(solution)/shard_map/pallas_call | solution.py:47
  61.7 8.0 %all-to-all-start.1 = ((bf16[16,16,1408]{2,1,0:T(8,128)(2,1)}), bf16[16,16,1408]{2,1,0:T(8,128)(2,1)S(1)}, u32[]{:S(2)}, u32[]{:S(2)}) async-start(bf16[16,16,1408]{2,1,0:T(8,128)(2,1)} %shard_map.80), calls=%async_computation.1 | async-start | bytes 1441792 | tf_op jit(solution)/shard_map/all_to_all | solution.py:387
  69.7 0.5 shard_map.82.next_ref
  70.2 1.6 %shard_map.81 = bf16[512,128]{1,0:T(8,128)(2,1)} custom-call(bf16[2,3,64,128]{3,2,1,0:T(8,128)(2,1)S(1)} %maximum_select_fusion.1.a_ref, bf16[9,192,128]{2,1,0:T(8,128)(2,1)S(1)} %get-tuple-element.19.w_one_ref.k_ref), custom_call_target="tpu_custom_call" | custom-call | tf_op jit(solution)/shard_map/pallas_call | solution.py:47
  71.8 10.1 %all-to-all-done.1.got_ref = bf16[16,16,1408]{2,1,0:T(8,128)(2,1)S(1)} async-done(((bf16[16,16,1408]{2,1,0:T(8,128)(2,1)}), bf16[16,16,1408]{2,1,0:T(8,128)(2,1)S(1)}, u32[]{:S(2)}, u32[]{:S(2)}) %all-to-all-start.1) | async-done | bytes 720928 | tf_op jit(solution)/shard_map/all_to_all | solution.py:387
  81.9 0.2 shard_map.83
  82.1 17.9 %all_to_all.15.got_ref = bf16[16,8,384]{2,1,0:T(8,128)(2,1)S(1)} all-to-all(bf16[16,8,384]{2,1,0:T(8,128)(2,1)S(1)} %bitcast.33), channel_id=1, replica_groups=mesh['x'=4,'y'=4,'zh'=2,'zl'=8,'core'=2] {'zl','core'}, dimensions={0} | all-to-all | bytes 196608 | tf_op jit(solution)/shard_map/all_to_all | solution.py:399
  100.0 0.9 shard_map.84
  (24 shorter events, 0.3 us)
Async XLA Ops:
  0.6 24.3 %collective-permute-start = (bf16[64,2,4,128]{3,2,1,0:T(4,128)(2,1)}, bf16[64,2,4,128]{3,2,1,0:T(4,128)(2,1)S(1)}, u32[]{:S(2)}, u32[]{:S(2)}) collective-permute-start(bf16[64,2,4,128]{3,2,1,0:T(4,128)(2,1)} %param.4), channel_id=1, source_target_pairs={{0,16},{16,0},{1,17},{17,1},{2,18},{18,2},{3,19},{19,3},{4,20},{20... | collective-permute-start | bytes 393224 | tf_op jit(solution)/shard_map/ppermute | solution.py:326
  18.6 6.4 %copy-start.2 = (bf16[64,2,4,128]{3,2,1,0:T(4,128)(2,1)S(1)}, bf16[64,2,4,128]{3,2,1,0:T(4,128)(2,1)}, u32[]{:S(2)}) copy-start(bf16[64,2,4,128]{3,2,1,0:T(4,128)(2,1)} %param.4) | copy-start | bytes 393220
  18.6 25.6 %all-to-all-start = ((bf16[32,8,384]{2,1,0:T(8,128)(2,1)}), bf16[32,8,384]{2,1,0:T(8,128)(2,1)S(1)}, u32[]{:S(2)}, u32[]{:S(2)}) async-start(bf16[32,8,384]{2,1,0:T(8,128)(2,1)} %shard_map.77), calls=%async_computation | async-start | bytes 393216 | tf_op jit(solution)/shard_map/all_to_all | solution.py:328
  24.9 14.8 %copy-start = (bf16[3,3,3,128,128]{4,3,2,1,0:T(8,128)(2,1)S(1)}, bf16[3,3,3,128,128]{4,3,2,1,0:T(8,128)(2,1)}, u32[]{:S(2)}) copy-start(bf16[3,3,3,128,128]{4,3,2,1,0:T(8,128)(2,1)} %param.6) | copy-start | bytes 2654212
  26.6 13.1 %copy-start.1 = (bf16[3,3,3,64,128]{4,3,2,1,0:T(8,128)(2,1)S(1)}, bf16[3,3,3,64,128]{4,3,2,1,0:T(8,128)(2,1)}, u32[]{:S(2)}) copy-start(bf16[3,3,3,64,128]{4,3,2,1,0:T(8,128)(2,1)} %param.5) | copy-start | bytes 1327108
  26.6 17.4 %collective-permute-start.1 = (bf16[4,3,64,128]{3,2,1,0:T(8,128)(2,1)S(1)}, bf16[4,3,64,128]{3,2,1,0:T(8,128)(2,1)S(1)}, u32[]{:S(2)}, u32[]{:S(2)}) collective-permute-start(bf16[4,3,64,128]{3,2,1,0:T(8,128)(2,1)S(1)} %slice.44), channel_id=1, source_target_pairs={{0,1},{1,2},{2,3},{3,4},{4,5},{5,6},{6,7},{7,8},{8,9},{9,10},{10,1... | collective-permute-start | bytes 589832 | tf_op jit(solution)/shard_map/ppermute | solution.py:311
  37.8 6.3 %collective-permute-start.2 = (bf16[4,2,64,128]{3,2,1,0:T(8,128)(2,1)S(1)}, bf16[4,2,64,128]{3,2,1,0:T(8,128)(2,1)S(1)}, u32[]{:S(2)}, u32[]{:S(2)}) collective-permute-start(bf16[4,2,64,128]{3,2,1,0:T(8,128)(2,1)S(1)} %slice.45), channel_id=1, source_target_pairs={{1,0},{2,1},{3,2},{4,3},{5,4},{6,5},{7,6},{8,7},{9,8},{10,9},{11,1... | collective-permute-start | bytes 393224 | tf_op jit(solution)/shard_map/ppermute | solution.py:311
  44.5 8.8 %collective-permute-start.3 = (bf16[14,64,128]{2,1,0:T(8,128)(2,1)S(1)}, bf16[14,64,128]{2,1,0:T(8,128)(2,1)S(1)}, u32[]{:S(2)}, u32[]{:S(2)}) collective-permute-start(bf16[14,64,128]{2,1,0:T(8,128)(2,1)S(1)} %pad_maximum_fusion.1), channel_id=1, source_target_pairs={{0,32},{32,64},{64,96},{96,128},{128,160},{160,192},{192,224},{224... | collective-permute-start | bytes 688136 | tf_op jit(solution)/shard_map/ppermute | solution.py:311
  47.7 5.6 %collective-permute-start.4 = (bf16[5,64,128]{2,1,0:T(8,128)(2,1)S(1)}, bf16[5,64,128]{2,1,0:T(8,128)(2,1)S(1)}, u32[]{:S(2)}, u32[]{:S(2)}) collective-permute-start(bf16[5,64,128]{2,1,0:T(8,128)(2,1)S(1)} %get-tuple-element.32), channel_id=1, source_target_pairs={{32,0},{64,32},{96,64},{128,96},{160,128},{192,160},{224,192},{256... | collective-permute-start | bytes 245768 | tf_op jit(solution)/shard_map/ppermute | solution.py:311
  55.1 14.6 %collective-permute-start.5 = (bf16[7,64,128]{2,1,0:T(8,128)(2,1)S(1)}, bf16[7,64,128]{2,1,0:T(8,128)(2,1)S(1)}, u32[]{:S(2)}, u32[]{:S(2)}) collective-permute-start(bf16[7,64,128]{2,1,0:T(8,128)(2,1)S(1)} %pad_maximum_fusion.2), channel_id=1, source_target_pairs={{0,32},{32,64},{64,96},{96,128},{128,160},{160,192},{192,224},{224... | collective-permute-start | bytes 344072 | tf_op jit(solution)/shard_map/ppermute | solution.py:372
  61.7 20.2 %all-to-all-start.1 = ((bf16[16,16,1408]{2,1,0:T(8,128)(2,1)}), bf16[16,16,1408]{2,1,0:T(8,128)(2,1)S(1)}, u32[]{:S(2)}, u32[]{:S(2)}) async-start(bf16[16,16,1408]{2,1,0:T(8,128)(2,1)} %shard_map.80), calls=%async_computation.1 | async-start | bytes 1441792 | tf_op jit(solution)/shard_map/all_to_all | solution.py:387

commit v7 on v6

--- a/solution.py
+++ b/solution.py
@@ -368,8 +368,7 @@
     )
     up = [(2 * k, 2 * k + 2) for k in range(planes - 1)]
     down = [(2 * k + 1, 2 * k - 1) for k in range(1, planes)]
-    edge = jnp.concatenate([jnp.where(zh == 0, hidden[1], hidden[0]), ag[0]], axis=0)
-    edge = lax.ppermute(edge, DEPTH, up + down)
+    side = lax.ppermute(jnp.where(zh == 0, hidden[1:], hidden[:1]), DEPTH, up + down)
     partial = call(
         kernel_grads_body,
         shape((16, 16, 1408)),
@@ -386,14 +385,13 @@
     )
     parts = lax.all_to_all(partial, PLANE, 0, 0, tiled=True)
 
-    side = edge[None, :4]
     three = jnp.where(
         zh == 0, jnp.concatenate([side, hidden], axis=0), jnp.concatenate([hidden, side], axis=0)
     )
     next_own = call(conv_two_body, shape((128, 128)), three, weights[1])
-    pair = jnp.where(zh == 0, ag, jnp.concatenate([ag[1:], edge[None, 4:]], axis=0))
+    after = lax.ppermute(ag[:1], DEPTH, down)
+    pair = jnp.where(zh == 0, ag, jnp.concatenate([ag[1:], after], axis=0))
     volume_grad = call(volume_grad_body, shape((512, 128)), pair, weights[0]).reshape(volume.shape)
-    parts, volume_grad = lax.optimization_barrier((parts, volume_grad))
 
     summed = call(plane_sum_body, shape((128, 384)), parts, next_own)
     rows = lax.all_to_all(summed.reshape(16, 8, 384), HEIGHT, 0, 0, tiled=True)

time: 101 us -> 99.1 us (0.981)
  blocking collectives: 17.9 us -> 0 us
  starting transfers between devices: 51.5 us -> 59 us
  waiting for transfers between devices: 18.1 us -> 25.5 us
    all_to_all x1 -> x0, blocking collectives: 17.9 us -> none  [per_device(): rows = lax.all_to_all(summed.reshape(16, 8, 384), HEIGHT, 0, 0, tiled=True)]
    all_to_all x0 -> x1, waiting for transfers between devices: none -> 9.01 us  [per_device(): rows = lax.all_to_all(summed.reshape(16, 8, 384), HEIGHT, 0, 0, tiled=True)]
    all_to_all x0 -> x1, starting transfers between devices: none -> 7.02 us  [per_device(): rows = lax.all_to_all(summed.reshape(16, 8, 384), HEIGHT, 0, 0, tiled=True)]
    all_to_all x1, waiting for transfers between devices: 10.1 us -> 5.81 us  [per_device(): parts = lax.all_to_all(partial, PLANE, 0, 0, tiled=True)]
    ppermute x1 -> x2, waiting for transfers between devices: 0.01 us -> 2.66 us  [the longest x1 2.66 us: per_device(): lax.ppermute(jnp.where(zh == 0, hidden[1:], hidden[:1]), DEPTH, up + down)]
    ppermute x1 -> x2, starting transfers between devices: 3.46 us -> 3.93 us  [the longest x1 3.26 us: per_device(): lax.ppermute(jnp.where(zh == 0, hidden[1:], hidden[:1]), DEPTH, up + down)]
  transfers between devices with their start and end apart: 8 -> 10, of which waited for: 3 -> 5; matrix products, arithmetic and copies ran while one was open for 1% -> 1% of each run, Pallas kernels for 8% -> 5%
where the time goes in v7:
time: 99.1 us; the launch traced here: 98.5 us
  starting transfers between devices  59 us (60%)
  waiting for transfers between devices  25.5 us (26%)
  Pallas kernels  11.9 us (12%)
  local copies, waits for them, and re-layouts  1.04 us (1%)
    ppermute x4, starting transfers between devices, shifted(): return lax.ppermute(block, axis, route)  17.5 us
    ppermute x1, starting transfers between devices, per_device(): other = lax.ppermute(volume, 'zh', [(0, 1), (1, 0)])  16.3 us
    pallas_call x10, Pallas kernels, call(): pl.pallas_call(body, out_shape=outs, in_specs=[smem] * scalars + [vmem] *...  11.9 us
    all_to_all x1, waiting for transfers between devices, per_device(): rows = lax.all_to_all(summed.reshape(16, 8, 384), HEIGHT, 0, 0, tiled=True)  9.01 us
    ppermute x4, waiting for transfers between devices, shifted(): return lax.ppermute(block, axis, route)  8.02 us
    all_to_all x1, starting transfers between devices, per_device(): parts = lax.all_to_all(partial, PLANE, 0, 0, tiled=True)  7.97 us
    all_to_all x1, starting transfers between devices, per_device(): rows = lax.all_to_all(summed.reshape(16, 8, 384), HEIGHT, 0, 0, tiled=True)  7.02 us
    all_to_all x1, starting transfers between devices, per_device(): slab = lax.all_to_all(slabs, LINE, 0, 0, tiled=True)  6.26 us
  transfers between devices with their start and end apart: 10, of which 5 were waited for; matrix products, arithmetic and copies ran while one was open for 1% of the time, Pallas kernels for 5%

profile of v7, /device:TPU:1, one launch (start us, length us, event | category | flops | bytes accessed | tf_op | source)
XLA Modules:
  0.0 98.5 jit_solution(11980085106039286026)
XLA Ops:
  0.6 16.3 %collective-permute-start = (bf16[64,2,4,128]{3,2,1,0:T(4,128)(2,1)}, bf16[64,2,4,128]{3,2,1,0:T(4,128)(2,1)S(1)}, u32[]{:S(2)}, u32[]{:S(2)}) collective-permute-start(bf16[64,2,4,128]{3,2,1,0:T(4,128)(2,1)} %param.4), channel_id=1, source_target_pairs={{0,16},{16,0},{1,17},{17,1},{2,18},{18,2},{3,19},{19,3},{4,20},{20... | collective-permute-start | bytes 393224 | tf_op jit(solution)/shard_map/ppermute | solution.py:326
  16.9 1.0 reshape.45.cot_ref
  17.9 0.7 shard_map.77
  18.6 6.3 %all-to-all-start = ((bf16[32,8,384]{2,1,0:T(8,128)(2,1)}), bf16[32,8,384]{2,1,0:T(8,128)(2,1)S(1)}, u32[]{:S(2)}, u32[]{:S(2)}) async-start(bf16[32,8,384]{2,1,0:T(8,128)(2,1)} %shard_map.77), calls=%async_computation | async-start | bytes 393216 | tf_op jit(solution)/shard_map/all_to_all | solution.py:328
  24.9 1.6 %shard_map.75 = bf16[4,4,64,128]{3,2,1,0:T(8,128)(2,1)S(1)} custom-call(s32[2]{0:T(128)S(1)} %pad_add_fusion.s_ref, bf16[512,128]{1,0:T(8,128)(2,1)S(1)} %bitcast.25, bf16[512,128]{1,0:T(8,128)(2,1)S(1)} %bitcast.26), custom_call_target="tpu_custom_call" | custom-call | flops 40000000000 | tf_op jit(solution)/shard_map/pallas_call | solution.py:47
  26.6 11.1 %collective-permute-start.1 = (bf16[4,3,64,128]{3,2,1,0:T(8,128)(2,1)S(1)}, bf16[4,3,64,128]{3,2,1,0:T(8,128)(2,1)S(1)}, u32[]{:S(2)}, u32[]{:S(2)}) collective-permute-start(bf16[4,3,64,128]{3,2,1,0:T(8,128)(2,1)S(1)} %slice.36), channel_id=1, source_target_pairs={{0,1},{1,2},{2,3},{3,4},{4,5},{5,6},{6,7},{7,8},{8,9},{9,10},{10,1... | collective-permute-start | bytes 589832 | tf_op jit(solution)/shard_map/ppermute | solution.py:311
  37.8 1.9 %collective-permute-start.2 = (bf16[4,2,64,128]{3,2,1,0:T(8,128)(2,1)S(1)}, bf16[4,2,64,128]{3,2,1,0:T(8,128)(2,1)S(1)}, u32[]{:S(2)}, u32[]{:S(2)}) collective-permute-start(bf16[4,2,64,128]{3,2,1,0:T(8,128)(2,1)S(1)} %slice.37), channel_id=1, source_target_pairs={{1,0},{2,1},{3,2},{4,3},{5,4},{6,5},{7,6},{8,7},{9,8},{10,9},{11,1... | collective-permute-start | bytes 393224 | tf_op jit(solution)/shard_map/ppermute | solution.py:311
  39.7 0.6 shard_map.76
  40.3 3.7 %collective-permute-done.2 = bf16[4,2,64,128]{3,2,1,0:T(8,128)(2,1)S(1)} collective-permute-done((bf16[4,2,64,128]{3,2,1,0:T(8,128)(2,1)S(1)}, bf16[4,2,64,128]{3,2,1,0:T(8,128)(2,1)S(1)}, u32[]{:S(2)}, u32[]{:S(2)}) %collective-permute-start.2) | collective-permute-done | bytes 131104 | tf_op jit(solution)/shard_map/ppermute | solution.py:311
  44.5 3.2 %collective-permute-start.3 = (bf16[14,64,128]{2,1,0:T(8,128)(2,1)S(1)}, bf16[14,64,128]{2,1,0:T(8,128)(2,1)S(1)}, u32[]{:S(2)}, u32[]{:S(2)}) collective-permute-start(bf16[14,64,128]{2,1,0:T(8,128)(2,1)S(1)} %pad_maximum_fusion.1), channel_id=1, source_target_pairs={{0,32},{32,64},{64,96},{96,128},{128,160},{160,192},{192,224},{224... | collective-permute-start | bytes 688136 | tf_op jit(solution)/shard_map/ppermute | solution.py:311
  47.7 1.3 %collective-permute-start.4 = (bf16[5,64,128]{2,1,0:T(8,128)(2,1)S(1)}, bf16[5,64,128]{2,1,0:T(8,128)(2,1)S(1)}, u32[]{:S(2)}, u32[]{:S(2)}) collective-permute-start(bf16[5,64,128]{2,1,0:T(8,128)(2,1)S(1)} %get-tuple-element.28), channel_id=1, source_target_pairs={{32,0},{64,32},{96,64},{128,96},{160,128},{192,160},{224,192},{256... | collective-permute-start | bytes 245768 | tf_op jit(solution)/shard_map/ppermute | solution.py:311
  49.0 4.3 %collective-permute-done.4.up_ref = bf16[5,64,128]{2,1,0:T(8,128)(2,1)S(1)} collective-permute-done((bf16[5,64,128]{2,1,0:T(8,128)(2,1)S(1)}, bf16[5,64,128]{2,1,0:T(8,128)(2,1)S(1)}, u32[]{:S(2)}, u32[]{:S(2)}) %collective-permute-start.4) | collective-permute-done | bytes 81952 | tf_op jit(solution)/shard_map/ppermute | solution.py:311
  53.3 1.7 %shard_map.79 = (bf16[2,4,64,128]{3,2,1,0:T(8,128)(2,1)S(1)}, bf16[2,3,64,128]{3,2,1,0:T(8,128)(2,1)S(1)}) custom-call(s32[2]{0:T(128)S(1)} %pad_add_fusion.s_ref, bf16[4,9,64,128]{3,2,1,0:T(8,128)(2,1)S(1)} %pad_maximum_fusion.deep_ref, bf16[14,64,128]{2,1,0:T(8,128)(2,1)S(1)} %collective-permute-done.3.low_ref, ...), custom_call_target="tpu_custom_call" | custom-call | tf_op jit(solution)/shard_map/pallas_call | solution.py:47
  55.0 3.2 %shard_map.80 = bf16[16,16,1408]{2,1,0:T(8,128)(2,1)} custom-call(s32[2]{0:T(128)S(1)} %pad_add_fusion.s_ref, bf16[4,9,64,128]{3,2,1,0:T(8,128)(2,1)S(1)} %pad_maximum_fusion.deep_ref, bf16[14,64,128]{2,1,0:T(8,128)(2,1)S(1)} %collective-permute-done.3.low_ref, bf16[2,6,64,128]{3,2,1,0:T(8,128)(2,1)S(1)} %shard_map.78.cot_ref, ...), custom_call_target="tpu_custom_call" | custom-call | tf_op jit(solution)/shard_map/pallas_call | solution.py:47
  58.2 8.0 %all-to-all-start.1 = ((bf16[16,16,1408]{2,1,0:T(8,128)(2,1)}), bf16[16,16,1408]{2,1,0:T(8,128)(2,1)S(1)}, u32[]{:S(2)}, u32[]{:S(2)}) async-start(bf16[16,16,1408]{2,1,0:T(8,128)(2,1)} %shard_map.80), calls=%async_computation.1 | async-start | bytes 1441792 | tf_op jit(solution)/shard_map/all_to_all | solution.py:386
  66.2 3.3 %collective-permute-start.5 = (bf16[1,4,64,128]{3,2,1,0:T(8,128)(2,1)S(1)}, bf16[1,4,64,128]{3,2,1,0:T(8,128)(2,1)S(1)}, u32[]{:S(2)}, u32[]{:S(2)}) collective-permute-start(bf16[1,4,64,128]{3,2,1,0:T(8,128)(2,1)S(1)} %slice_select_fusion), channel_id=1, source_target_pairs={{0,32},{32,64},{64,96},{96,128},{128,160},{160,192},{192,224},{224... | collective-permute-start | bytes 196616 | tf_op jit(solution)/shard_map/ppermute | solution.py:371
  69.5 2.7 %collective-permute-done.5 = bf16[1,4,64,128]{3,2,1,0:T(8,128)(2,1)S(1)} collective-permute-done((bf16[1,4,64,128]{3,2,1,0:T(8,128)(2,1)S(1)}, bf16[1,4,64,128]{3,2,1,0:T(8,128)(2,1)S(1)}, u32[]{:S(2)}, u32[]{:S(2)}) %collective-permute-start.5) | collective-permute-done | bytes 65568 | tf_op jit(solution)/shard_map/ppermute | solution.py:371
  72.7 5.8 %all-to-all-done.1.got_ref = bf16[16,16,1408]{2,1,0:T(8,128)(2,1)S(1)} async-done(((bf16[16,16,1408]{2,1,0:T(8,128)(2,1)}), bf16[16,16,1408]{2,1,0:T(8,128)(2,1)S(1)}, u32[]{:S(2)}, u32[]{:S(2)}) %all-to-all-start.1) | async-done | bytes 720928 | tf_op jit(solution)/shard_map/all_to_all | solution.py:386
  78.5 0.8 shard_map.82
  79.3 7.0 %all-to-all-start.2 = ((bf16[16,8,384]{2,1,0:T(8,128)(2,1)}), bf16[16,8,384]{2,1,0:T(8,128)(2,1)S(1)}, u32[]{:S(2)}, u32[]{:S(2)}) async-start(bf16[16,8,384]{2,1,0:T(8,128)(2,1)} %bitcast.10), calls=%async_computation.2 | async-start | bytes 196608 | tf_op jit(solution)/shard_map/all_to_all | solution.py:397
  86.3 0.7 collective-permute-start.6
  87.0 1.6 %shard_map.84 = bf16[512,128]{1,0:T(8,128)(2,1)} custom-call(bf16[2,3,64,128]{3,2,1,0:T(8,128)(2,1)S(1)} %maximum_select_fusion.1.a_ref, bf16[9,192,128]{2,1,0:T(8,128)(2,1)S(1)} %get-tuple-element.17.w_one_ref.k_ref), custom_call_target="tpu_custom_call" | custom-call | tf_op jit(solution)/shard_map/pallas_call | solution.py:47
  88.6 9.0 %all-to-all-done.2.got_ref = bf16[16,8,384]{2,1,0:T(8,128)(2,1)S(1)} async-done(((bf16[16,8,384]{2,1,0:T(8,128)(2,1)}), bf16[16,8,384]{2,1,0:T(8,128)(2,1)S(1)}, u32[]{:S(2)}, u32[]{:S(2)}) %all-to-all-start.2) | async-done | bytes 98336 | tf_op jit(solution)/shard_map/all_to_all | solution.py:397
  97.6 0.9 shard_map.83
  (24 shorter events, 1.0 us)
Async XLA Ops:
  0.6 24.3 %collective-permute-start = (bf16[64,2,4,128]{3,2,1,0:T(4,128)(2,1)}, bf16[64,2,4,128]{3,2,1,0:T(4,128)(2,1)S(1)}, u32[]{:S(2)}, u32[]{:S(2)}) collective-permute-start(bf16[64,2,4,128]{3,2,1,0:T(4,128)(2,1)} %param.4), channel_id=1, source_target_pairs={{0,16},{16,0},{1,17},{17,1},{2,18},{18,2},{3,19},{19,3},{4,20},{20... | collective-permute-start | bytes 393224 | tf_op jit(solution)/shard_map/ppermute | solution.py:326
  18.6 6.4 %copy-start.2 = (bf16[64,2,4,128]{3,2,1,0:T(4,128)(2,1)S(1)}, bf16[64,2,4,128]{3,2,1,0:T(4,128)(2,1)}, u32[]{:S(2)}) copy-start(bf16[64,2,4,128]{3,2,1,0:T(4,128)(2,1)} %param.4) | copy-start | bytes 393220
  18.6 25.6 %all-to-all-start = ((bf16[32,8,384]{2,1,0:T(8,128)(2,1)}), bf16[32,8,384]{2,1,0:T(8,128)(2,1)S(1)}, u32[]{:S(2)}, u32[]{:S(2)}) async-start(bf16[32,8,384]{2,1,0:T(8,128)(2,1)} %shard_map.77), calls=%async_computation | async-start | bytes 393216 | tf_op jit(solution)/shard_map/all_to_all | solution.py:328
  24.9 14.8 %copy-start = (bf16[3,3,3,128,128]{4,3,2,1,0:T(8,128)(2,1)S(1)}, bf16[3,3,3,128,128]{4,3,2,1,0:T(8,128)(2,1)}, u32[]{:S(2)}) copy-start(bf16[3,3,3,128,128]{4,3,2,1,0:T(8,128)(2,1)} %param.6) | copy-start | bytes 2654212
  26.6 13.1 %copy-start.1 = (bf16[3,3,3,64,128]{4,3,2,1,0:T(8,128)(2,1)S(1)}, bf16[3,3,3,64,128]{4,3,2,1,0:T(8,128)(2,1)}, u32[]{:S(2)}) copy-start(bf16[3,3,3,64,128]{4,3,2,1,0:T(8,128)(2,1)} %param.5) | copy-start | bytes 1327108
  26.6 17.4 %collective-permute-start.1 = (bf16[4,3,64,128]{3,2,1,0:T(8,128)(2,1)S(1)}, bf16[4,3,64,128]{3,2,1,0:T(8,128)(2,1)S(1)}, u32[]{:S(2)}, u32[]{:S(2)}) collective-permute-start(bf16[4,3,64,128]{3,2,1,0:T(8,128)(2,1)S(1)} %slice.36), channel_id=1, source_target_pairs={{0,1},{1,2},{2,3},{3,4},{4,5},{5,6},{6,7},{7,8},{8,9},{9,10},{10,1... | collective-permute-start | bytes 589832 | tf_op jit(solution)/shard_map/ppermute | solution.py:311
  37.8 6.3 %collective-permute-start.2 = (bf16[4,2,64,128]{3,2,1,0:T(8,128)(2,1)S(1)}, bf16[4,2,64,128]{3,2,1,0:T(8,128)(2,1)S(1)}, u32[]{:S(2)}, u32[]{:S(2)}) collective-permute-start(bf16[4,2,64,128]{3,2,1,0:T(8,128)(2,1)S(1)} %slice.37), channel_id=1, source_target_pairs={{1,0},{2,1},{3,2},{4,3},{5,4},{6,5},{7,6},{8,7},{9,8},{10,9},{11,1... | collective-permute-start | bytes 393224 | tf_op jit(solution)/shard_map/ppermute | solution.py:311
  44.5 8.8 %collective-permute-start.3 = (bf16[14,64,128]{2,1,0:T(8,128)(2,1)S(1)}, bf16[14,64,128]{2,1,0:T(8,128)(2,1)S(1)}, u32[]{:S(2)}, u32[]{:S(2)}) collective-permute-start(bf16[14,64,128]{2,1,0:T(8,128)(2,1)S(1)} %pad_maximum_fusion.1), channel_id=1, source_target_pairs={{0,32},{32,64},{64,96},{96,128},{128,160},{160,192},{192,224},{224... | collective-permute-start | bytes 688136 | tf_op jit(solution)/shard_map/ppermute | solution.py:311
  47.7 5.6 %collective-permute-start.4 = (bf16[5,64,128]{2,1,0:T(8,128)(2,1)S(1)}, bf16[5,64,128]{2,1,0:T(8,128)(2,1)S(1)}, u32[]{:S(2)}, u32[]{:S(2)}) collective-permute-start(bf16[5,64,128]{2,1,0:T(8,128)(2,1)S(1)} %get-tuple-element.28), channel_id=1, source_target_pairs={{32,0},{64,32},{96,64},{128,96},{160,128},{192,160},{224,192},{256... | collective-permute-start | bytes 245768 | tf_op jit(solution)/shard_map/ppermute | solution.py:311
  58.2 20.3 %all-to-all-start.1 = ((bf16[16,16,1408]{2,1,0:T(8,128)(2,1)}), bf16[16,16,1408]{2,1,0:T(8,128)(2,1)S(1)}, u32[]{:S(2)}, u32[]{:S(2)}) async-start(bf16[16,16,1408]{2,1,0:T(8,128)(2,1)} %shard_map.80), calls=%async_computation.1 | async-start | bytes 1441792 | tf_op jit(solution)/shard_map/all_to_all | solution.py:386
  66.2 5.9 %collective-permute-start.5 = (bf16[1,4,64,128]{3,2,1,0:T(8,128)(2,1)S(1)}, bf16[1,4,64,128]{3,2,1,0:T(8,128)(2,1)S(1)}, u32[]{:S(2)}, u32[]{:S(2)}) collective-permute-start(bf16[1,4,64,128]{3,2,1,0:T(8,128)(2,1)S(1)} %slice_select_fusion), channel_id=1, source_target_pairs={{0,32},{32,64},{64,96},{96,128},{128,160},{160,192},{192,224},{224... | collective-permute-start | bytes 196616 | tf_op jit(solution)/shard_map/ppermute | solution.py:371
  79.3 18.3 %all-to-all-start.2 = ((bf16[16,8,384]{2,1,0:T(8,128)(2,1)}), bf16[16,8,384]{2,1,0:T(8,128)(2,1)S(1)}, u32[]{:S(2)}, u32[]{:S(2)}) async-start(bf16[16,8,384]{2,1,0:T(8,128)(2,1)} %bitcast.10), calls=%async_computation.2 | async-start | bytes 196608 | tf_op jit(solution)/shard_map/all_to_all | solution.py:397
  86.3 0.7 collective-permute-start.6

commit v8 on v7

--- a/solution.py
+++ b/solution.py
@@ -182,7 +182,7 @@
     copies = []
 
     def put(i, value):
-        out_ref[i] = value.astype(BF).reshape(16, 16, 128)
+        out_ref[i] = value.reshape(16, 16, 128).astype(BF)
         place = out_far.at[:, :, 128 * i : 128 * i + 128]
         copies.append(pltpu.make_async_copy(out_ref.at[i], place, sems.at[i]))
         copies[-1].start()
@@ -212,7 +212,9 @@
     ]
     first = dot(hid_rows, jnp.concatenate(cots, axis=1))
     channel = device * 4 + zh * 2 + slot % 2
-    pick_one = one_hot((slot >= 12) & (source == (slot - 12) // 2 * 64 + channel))
+    row, of = iota((128, 128), 0), iota((128, 128), 1)
+    wanted = (row % 8 - 4) // 2 * 64 + row // 8 * 4 + zh * 2 + row % 2
+    pick_one = one_hot((row % 8 >= 4) & (of == wanted))
     vols, picks = [], []
     for i, (a, b) in enumerate(PAIRS):
         x = jnp.concatenate(
@@ -224,8 +226,9 @@
             axis=0,
         )
         vol_rows = dot(pick_one, x, 1, 1).astype(BF)
-        both = first[:, 128 * i : 128 * i + 128] + dot(vol_rows, own_ag)
-        put(i, both)
+        upper = dot(vol_rows, own_ag).reshape(16, 8, 128)
+        both = first[:, 128 * i : 128 * i + 128].reshape(16, 16, 128)
+        put(i, jnp.concatenate([both[:, :8], both[:, 8:] + upper], axis=1))
         vols.append(x)
         picks.append(one_hot((slot // 2 == i % 8) & (source == 64 + channel)))
     groups = (

time: 99.1 us -> 98.8 us (level)
  no operation moved by 1% of the time
where the time goes in v8:
time: 98.8 us; the launch traced here: 98.2 us
  starting transfers between devices  59 us (60%)
  waiting for transfers between devices  25.5 us (26%)
  Pallas kernels  11.6 us (12%)
  local copies, waits for them, and re-layouts  1.04 us (1%)
    ppermute x4, starting transfers between devices, shifted(): return lax.ppermute(block, axis, route)  17.5 us
    ppermute x1, starting transfers between devices, per_device(): other = lax.ppermute(volume, 'zh', [(0, 1), (1, 0)])  16.3 us
    pallas_call x10, Pallas kernels, call(): pl.pallas_call(body, out_shape=outs, in_specs=[smem] * scalars + [vmem] *...  11.6 us
    all_to_all x1, waiting for transfers between devices, per_device(): rows = lax.all_to_all(summed.reshape(16, 8, 384), HEIGHT, 0, 0, tiled=True)  9.01 us
    ppermute x4, waiting for transfers between devices, shifted(): return lax.ppermute(block, axis, route)  8.02 us
    all_to_all x1, starting transfers between devices, per_device(): parts = lax.all_to_all(partial, PLANE, 0, 0, tiled=True)  7.97 us
    all_to_all x1, starting transfers between devices, per_device(): rows = lax.all_to_all(summed.reshape(16, 8, 384), HEIGHT, 0, 0, tiled=True)  7.02 us
    all_to_all x1, starting transfers between devices, per_device(): slab = lax.all_to_all(slabs, LINE, 0, 0, tiled=True)  6.26 us
  transfers between devices with their start and end apart: 10, of which 5 were waited for; matrix products, arithmetic and copies ran while one was open for 1% of the time, Pallas kernels for 5%

profile of v8, /device:TPU:1, one launch (start us, length us, event | category | flops | bytes accessed | tf_op | source)
XLA Modules:
  0.0 98.2 jit_solution(9040973982661540156)
XLA Ops:
  0.6 16.3 %collective-permute-start = (bf16[64,2,4,128]{3,2,1,0:T(4,128)(2,1)}, bf16[64,2,4,128]{3,2,1,0:T(4,128)(2,1)S(1)}, u32[]{:S(2)}, u32[]{:S(2)}) collective-permute-start(bf16[64,2,4,128]{3,2,1,0:T(4,128)(2,1)} %param.4), channel_id=1, source_target_pairs={{0,16},{16,0},{1,17},{17,1},{2,18},{18,2},{3,19},{19,3},{4,20},{20... | collective-permute-start | bytes 393224 | tf_op jit(solution)/shard_map/ppermute | solution.py:329
  16.9 1.0 reshape.45.cot_ref
  17.9 0.7 shard_map.77
  18.6 6.3 %all-to-all-start = ((bf16[32,8,384]{2,1,0:T(8,128)(2,1)}), bf16[32,8,384]{2,1,0:T(8,128)(2,1)S(1)}, u32[]{:S(2)}, u32[]{:S(2)}) async-start(bf16[32,8,384]{2,1,0:T(8,128)(2,1)} %shard_map.77), calls=%async_computation | async-start | bytes 393216 | tf_op jit(solution)/shard_map/all_to_all | solution.py:331
  24.9 1.6 %shard_map.75 = bf16[4,4,64,128]{3,2,1,0:T(8,128)(2,1)S(1)} custom-call(s32[2]{0:T(128)S(1)} %pad_add_fusion.s_ref, bf16[512,128]{1,0:T(8,128)(2,1)S(1)} %bitcast.25, bf16[512,128]{1,0:T(8,128)(2,1)S(1)} %bitcast.26), custom_call_target="tpu_custom_call" | custom-call | flops 40000000000 | tf_op jit(solution)/shard_map/pallas_call | solution.py:47
  26.6 11.1 %collective-permute-start.1 = (bf16[4,3,64,128]{3,2,1,0:T(8,128)(2,1)S(1)}, bf16[4,3,64,128]{3,2,1,0:T(8,128)(2,1)S(1)}, u32[]{:S(2)}, u32[]{:S(2)}) collective-permute-start(bf16[4,3,64,128]{3,2,1,0:T(8,128)(2,1)S(1)} %slice.36), channel_id=1, source_target_pairs={{0,1},{1,2},{2,3},{3,4},{4,5},{5,6},{6,7},{7,8},{8,9},{9,10},{10,1... | collective-permute-start | bytes 589832 | tf_op jit(solution)/shard_map/ppermute | solution.py:314
  37.8 1.9 %collective-permute-start.2 = (bf16[4,2,64,128]{3,2,1,0:T(8,128)(2,1)S(1)}, bf16[4,2,64,128]{3,2,1,0:T(8,128)(2,1)S(1)}, u32[]{:S(2)}, u32[]{:S(2)}) collective-permute-start(bf16[4,2,64,128]{3,2,1,0:T(8,128)(2,1)S(1)} %slice.37), channel_id=1, source_target_pairs={{1,0},{2,1},{3,2},{4,3},{5,4},{6,5},{7,6},{8,7},{9,8},{10,9},{11,1... | collective-permute-start | bytes 393224 | tf_op jit(solution)/shard_map/ppermute | solution.py:314
  39.7 0.6 shard_map.76
  40.3 3.7 %collective-permute-done.2 = bf16[4,2,64,128]{3,2,1,0:T(8,128)(2,1)S(1)} collective-permute-done((bf16[4,2,64,128]{3,2,1,0:T(8,128)(2,1)S(1)}, bf16[4,2,64,128]{3,2,1,0:T(8,128)(2,1)S(1)}, u32[]{:S(2)}, u32[]{:S(2)}) %collective-permute-start.2) | collective-permute-done | bytes 131104 | tf_op jit(solution)/shard_map/ppermute | solution.py:314
  44.5 3.2 %collective-permute-start.3 = (bf16[14,64,128]{2,1,0:T(8,128)(2,1)S(1)}, bf16[14,64,128]{2,1,0:T(8,128)(2,1)S(1)}, u32[]{:S(2)}, u32[]{:S(2)}) collective-permute-start(bf16[14,64,128]{2,1,0:T(8,128)(2,1)S(1)} %pad_maximum_fusion.1), channel_id=1, source_target_pairs={{0,32},{32,64},{64,96},{96,128},{128,160},{160,192},{192,224},{224... | collective-permute-start | bytes 688136 | tf_op jit(solution)/shard_map/ppermute | solution.py:314
  47.7 1.3 %collective-permute-start.4 = (bf16[5,64,128]{2,1,0:T(8,128)(2,1)S(1)}, bf16[5,64,128]{2,1,0:T(8,128)(2,1)S(1)}, u32[]{:S(2)}, u32[]{:S(2)}) collective-permute-start(bf16[5,64,128]{2,1,0:T(8,128)(2,1)S(1)} %get-tuple-element.28), channel_id=1, source_target_pairs={{32,0},{64,32},{96,64},{128,96},{160,128},{192,160},{224,192},{256... | collective-permute-start | bytes 245768 | tf_op jit(solution)/shard_map/ppermute | solution.py:314
  49.0 4.3 %collective-permute-done.4.up_ref = bf16[5,64,128]{2,1,0:T(8,128)(2,1)S(1)} collective-permute-done((bf16[5,64,128]{2,1,0:T(8,128)(2,1)S(1)}, bf16[5,64,128]{2,1,0:T(8,128)(2,1)S(1)}, u32[]{:S(2)}, u32[]{:S(2)}) %collective-permute-start.4) | collective-permute-done | bytes 81952 | tf_op jit(solution)/shard_map/ppermute | solution.py:314
  53.3 1.7 %shard_map.79 = (bf16[2,4,64,128]{3,2,1,0:T(8,128)(2,1)S(1)}, bf16[2,3,64,128]{3,2,1,0:T(8,128)(2,1)S(1)}) custom-call(s32[2]{0:T(128)S(1)} %pad_add_fusion.s_ref, bf16[4,9,64,128]{3,2,1,0:T(8,128)(2,1)S(1)} %pad_maximum_fusion.deep_ref, bf16[14,64,128]{2,1,0:T(8,128)(2,1)S(1)} %collective-permute-done.3.low_ref, ...), custom_call_target="tpu_custom_call" | custom-call | tf_op jit(solution)/shard_map/pallas_call | solution.py:47
  55.0 2.9 %shard_map.80 = bf16[16,16,1408]{2,1,0:T(8,128)(2,1)} custom-call(s32[2]{0:T(128)S(1)} %pad_add_fusion.s_ref, bf16[4,9,64,128]{3,2,1,0:T(8,128)(2,1)S(1)} %pad_maximum_fusion.deep_ref, bf16[14,64,128]{2,1,0:T(8,128)(2,1)S(1)} %collective-permute-done.3.low_ref, bf16[2,6,64,128]{3,2,1,0:T(8,128)(2,1)S(1)} %shard_map.78.cot_ref, ...), custom_call_target="tpu_custom_call" | custom-call | tf_op jit(solution)/shard_map/pallas_call | solution.py:47
  58.0 8.0 %all-to-all-start.1 = ((bf16[16,16,1408]{2,1,0:T(8,128)(2,1)}), bf16[16,16,1408]{2,1,0:T(8,128)(2,1)S(1)}, u32[]{:S(2)}, u32[]{:S(2)}) async-start(bf16[16,16,1408]{2,1,0:T(8,128)(2,1)} %shard_map.80), calls=%async_computation.1 | async-start | bytes 1441792 | tf_op jit(solution)/shard_map/all_to_all | solution.py:389
  66.0 3.3 %collective-permute-start.5 = (bf16[1,4,64,128]{3,2,1,0:T(8,128)(2,1)S(1)}, bf16[1,4,64,128]{3,2,1,0:T(8,128)(2,1)S(1)}, u32[]{:S(2)}, u32[]{:S(2)}) collective-permute-start(bf16[1,4,64,128]{3,2,1,0:T(8,128)(2,1)S(1)} %slice_select_fusion), channel_id=1, source_target_pairs={{0,32},{32,64},{64,96},{96,128},{128,160},{160,192},{192,224},{224... | collective-permute-start | bytes 196616 | tf_op jit(solution)/shard_map/ppermute | solution.py:374
  69.3 2.7 %collective-permute-done.5 = bf16[1,4,64,128]{3,2,1,0:T(8,128)(2,1)S(1)} collective-permute-done((bf16[1,4,64,128]{3,2,1,0:T(8,128)(2,1)S(1)}, bf16[1,4,64,128]{3,2,1,0:T(8,128)(2,1)S(1)}, u32[]{:S(2)}, u32[]{:S(2)}) %collective-permute-start.5) | collective-permute-done | bytes 65568 | tf_op jit(solution)/shard_map/ppermute | solution.py:374
  72.4 5.8 %all-to-all-done.1.got_ref = bf16[16,16,1408]{2,1,0:T(8,128)(2,1)S(1)} async-done(((bf16[16,16,1408]{2,1,0:T(8,128)(2,1)}), bf16[16,16,1408]{2,1,0:T(8,128)(2,1)S(1)}, u32[]{:S(2)}, u32[]{:S(2)}) %all-to-all-start.1) | async-done | bytes 720928 | tf_op jit(solution)/shard_map/all_to_all | solution.py:389
  78.2 0.8 shard_map.82
  79.0 7.0 %all-to-all-start.2 = ((bf16[16,8,384]{2,1,0:T(8,128)(2,1)}), bf16[16,8,384]{2,1,0:T(8,128)(2,1)S(1)}, u32[]{:S(2)}, u32[]{:S(2)}) async-start(bf16[16,8,384]{2,1,0:T(8,128)(2,1)} %bitcast.10), calls=%async_computation.2 | async-start | bytes 196608 | tf_op jit(solution)/shard_map/all_to_all | solution.py:400
  86.1 0.7 collective-permute-start.6
  86.8 1.6 %shard_map.84 = bf16[512,128]{1,0:T(8,128)(2,1)} custom-call(bf16[2,3,64,128]{3,2,1,0:T(8,128)(2,1)S(1)} %maximum_select_fusion.1.a_ref, bf16[9,192,128]{2,1,0:T(8,128)(2,1)S(1)} %get-tuple-element.17.w_one_ref.k_ref), custom_call_target="tpu_custom_call" | custom-call | tf_op jit(solution)/shard_map/pallas_call | solution.py:47
  88.3 9.0 %all-to-all-done.2.got_ref = bf16[16,8,384]{2,1,0:T(8,128)(2,1)S(1)} async-done(((bf16[16,8,384]{2,1,0:T(8,128)(2,1)}), bf16[16,8,384]{2,1,0:T(8,128)(2,1)S(1)}, u32[]{:S(2)}, u32[]{:S(2)}) %all-to-all-start.2) | async-done | bytes 98336 | tf_op jit(solution)/shard_map/all_to_all | solution.py:400
  97.3 0.9 shard_map.83
  (24 shorter events, 1.0 us)
Async XLA Ops:
  0.6 24.3 %collective-permute-start = (bf16[64,2,4,128]{3,2,1,0:T(4,128)(2,1)}, bf16[64,2,4,128]{3,2,1,0:T(4,128)(2,1)S(1)}, u32[]{:S(2)}, u32[]{:S(2)}) collective-permute-start(bf16[64,2,4,128]{3,2,1,0:T(4,128)(2,1)} %param.4), channel_id=1, source_target_pairs={{0,16},{16,0},{1,17},{17,1},{2,18},{18,2},{3,19},{19,3},{4,20},{20... | collective-permute-start | bytes 393224 | tf_op jit(solution)/shard_map/ppermute | solution.py:329
  18.6 6.4 %copy-start.2 = (bf16[64,2,4,128]{3,2,1,0:T(4,128)(2,1)S(1)}, bf16[64,2,4,128]{3,2,1,0:T(4,128)(2,1)}, u32[]{:S(2)}) copy-start(bf16[64,2,4,128]{3,2,1,0:T(4,128)(2,1)} %param.4) | copy-start | bytes 393220
  18.6 25.6 %all-to-all-start = ((bf16[32,8,384]{2,1,0:T(8,128)(2,1)}), bf16[32,8,384]{2,1,0:T(8,128)(2,1)S(1)}, u32[]{:S(2)}, u32[]{:S(2)}) async-start(bf16[32,8,384]{2,1,0:T(8,128)(2,1)} %shard_map.77), calls=%async_computation | async-start | bytes 393216 | tf_op jit(solution)/shard_map/all_to_all | solution.py:331
  24.9 14.8 %copy-start = (bf16[3,3,3,128,128]{4,3,2,1,0:T(8,128)(2,1)S(1)}, bf16[3,3,3,128,128]{4,3,2,1,0:T(8,128)(2,1)}, u32[]{:S(2)}) copy-start(bf16[3,3,3,128,128]{4,3,2,1,0:T(8,128)(2,1)} %param.6) | copy-start | bytes 2654212
  26.6 13.1 %copy-start.1 = (bf16[3,3,3,64,128]{4,3,2,1,0:T(8,128)(2,1)S(1)}, bf16[3,3,3,64,128]{4,3,2,1,0:T(8,128)(2,1)}, u32[]{:S(2)}) copy-start(bf16[3,3,3,64,128]{4,3,2,1,0:T(8,128)(2,1)} %param.5) | copy-start | bytes 1327108
  26.6 17.4 %collective-permute-start.1 = (bf16[4,3,64,128]{3,2,1,0:T(8,128)(2,1)S(1)}, bf16[4,3,64,128]{3,2,1,0:T(8,128)(2,1)S(1)}, u32[]{:S(2)}, u32[]{:S(2)}) collective-permute-start(bf16[4,3,64,128]{3,2,1,0:T(8,128)(2,1)S(1)} %slice.36), channel_id=1, source_target_pairs={{0,1},{1,2},{2,3},{3,4},{4,5},{5,6},{6,7},{7,8},{8,9},{9,10},{10,1... | collective-permute-start | bytes 589832 | tf_op jit(solution)/shard_map/ppermute | solution.py:314
  37.8 6.3 %collective-permute-start.2 = (bf16[4,2,64,128]{3,2,1,0:T(8,128)(2,1)S(1)}, bf16[4,2,64,128]{3,2,1,0:T(8,128)(2,1)S(1)}, u32[]{:S(2)}, u32[]{:S(2)}) collective-permute-start(bf16[4,2,64,128]{3,2,1,0:T(8,128)(2,1)S(1)} %slice.37), channel_id=1, source_target_pairs={{1,0},{2,1},{3,2},{4,3},{5,4},{6,5},{7,6},{8,7},{9,8},{10,9},{11,1... | collective-permute-start | bytes 393224 | tf_op jit(solution)/shard_map/ppermute | solution.py:314
  44.5 8.8 %collective-permute-start.3 = (bf16[14,64,128]{2,1,0:T(8,128)(2,1)S(1)}, bf16[14,64,128]{2,1,0:T(8,128)(2,1)S(1)}, u32[]{:S(2)}, u32[]{:S(2)}) collective-permute-start(bf16[14,64,128]{2,1,0:T(8,128)(2,1)S(1)} %pad_maximum_fusion.1), channel_id=1, source_target_pairs={{0,32},{32,64},{64,96},{96,128},{128,160},{160,192},{192,224},{224... | collective-permute-start | bytes 688136 | tf_op jit(solution)/shard_map/ppermute | solution.py:314
  47.7 5.6 %collective-permute-start.4 = (bf16[5,64,128]{2,1,0:T(8,128)(2,1)S(1)}, bf16[5,64,128]{2,1,0:T(8,128)(2,1)S(1)}, u32[]{:S(2)}, u32[]{:S(2)}) collective-permute-start(bf16[5,64,128]{2,1,0:T(8,128)(2,1)S(1)} %get-tuple-element.28), channel_id=1, source_target_pairs={{32,0},{64,32},{96,64},{128,96},{160,128},{192,160},{224,192},{256... | collective-permute-start | bytes 245768 | tf_op jit(solution)/shard_map/ppermute | solution.py:314
  58.0 20.2 %all-to-all-start.1 = ((bf16[16,16,1408]{2,1,0:T(8,128)(2,1)}), bf16[16,16,1408]{2,1,0:T(8,128)(2,1)S(1)}, u32[]{:S(2)}, u32[]{:S(2)}) async-start(bf16[16,16,1408]{2,1,0:T(8,128)(2,1)} %shard_map.80), calls=%async_computation.1 | async-start | bytes 1441792 | tf_op jit(solution)/shard_map/all_to_all | solution.py:389
  66.0 5.9 %collective-permute-start.5 = (bf16[1,4,64,128]{3,2,1,0:T(8,128)(2,1)S(1)}, bf16[1,4,64,128]{3,2,1,0:T(8,128)(2,1)S(1)}, u32[]{:S(2)}, u32[]{:S(2)}) collective-permute-start(bf16[1,4,64,128]{3,2,1,0:T(8,128)(2,1)S(1)} %slice_select_fusion), channel_id=1, source_target_pairs={{0,32},{32,64},{64,96},{96,128},{128,160},{160,192},{192,224},{224... | collective-permute-start | bytes 196616 | tf_op jit(solution)/shard_map/ppermute | solution.py:374
  79.0 18.3 %all-to-all-start.2 = ((bf16[16,8,384]{2,1,0:T(8,128)(2,1)}), bf16[16,8,384]{2,1,0:T(8,128)(2,1)S(1)}, u32[]{:S(2)}, u32[]{:S(2)}) async-start(bf16[16,8,384]{2,1,0:T(8,128)(2,1)} %bitcast.10), calls=%async_computation.2 | async-start | bytes 196608 | tf_op jit(solution)/shard_map/all_to_all | solution.py:400
  86.1 0.7 collective-permute-start.6

commit v9 on v8

--- a/solution.py
+++ b/solution.py
@@ -38,17 +38,17 @@
     return jnp.where(iota(x.shape, 0) % 64 == 63, 0.0, pltpu.roll(x, x.shape[0] - 1, 0))
 
 
-def call(body, outs, *args, scalars=0, flops=0, far=0, far_out=False, scratch=()):
+def call(body, outs, *args, scalars=0, flops=0, far=0, far_outs=0, scratch=()):
     smem = pl.BlockSpec(memory_space=pltpu.SMEM)
     vmem = pl.BlockSpec(memory_space=pltpu.VMEM)
     hbm = pl.BlockSpec(memory_space=pl.ANY)
-    out = hbm if far_out else vmem
     many = isinstance(outs, list)
+    near = len(outs) - far_outs if many else 1
     return pl.pallas_call(
         body,
         out_shape=outs,
         in_specs=[smem] * scalars + [vmem] * (len(args) - scalars - far) + [hbm] * far,
-        out_specs=[out] * len(outs) if many else out,
+        out_specs=[vmem] * near + [hbm] * far_outs if many else vmem,
         scratch_shapes=scratch,
         compiler_params=pltpu.CompilerParams(vmem_limit_bytes=16 * 1024 * 1024),
         cost_estimate=pl.CostEstimate(flops=flops, bytes_accessed=0, transcendentals=0) if flops else None,
@@ -124,7 +124,7 @@
     return up_ref[row - 1] if plane == 3 else cot_ref[plane - 1, row]
 
 
-def front_body(s_ref, deep_ref, low_ref, cot_ref, up_ref, w_one_ref, w_two_ref, hid_ref, ag_ref):
+def front(s_ref, deep_ref, low_ref, cot_ref, up_ref, w_one_ref, w_two_ref, hid_ref, ag_ref):
     h = s_ref[0]
     cells = [
         jnp.concatenate(
@@ -175,9 +175,7 @@
             ag_ref[q, r] = ag[at : at + 64]
 
 
-def kernel_grads_body(
-    s_ref, deep_ref, low_ref, cot_ref, up_ref, ag_ref, hid_ref, out_far, out_ref, sems
-):
+def kernel_grads(s_ref, deep_ref, low_ref, cot_ref, up_ref, ag_ref, hid_ref, out_far, out_ref, sems):
     zh = s_ref[1]
     copies = []
 
@@ -243,6 +241,25 @@
         copy.wait()
 
 
+def front_and_grads_body(
+    s_ref,
+    deep_ref,
+    low_ref,
+    cot_ref,
+    up_ref,
+    w_one_ref,
+    w_two_ref,
+    hid_ref,
+    ag_ref,
+    out_far,
+    out_ref,
+    sems,
+):
+    received = (deep_ref, low_ref, cot_ref, up_ref)
+    front(s_ref, *received, w_one_ref, w_two_ref, hid_ref, ag_ref)
+    kernel_grads(s_ref, *received, ag_ref, hid_ref, out_far, out_ref, sems)
+
+
 def conv_two_body(h_ref, w_two_ref, out_ref):
     acc = jnp.zeros((128, 128), F32)
     for i, (a, b) in enumerate(PAIRS):
@@ -358,9 +375,9 @@
     lower = shifted(jnp.concatenate([deep[3], cot[1, 1:]], axis=0), PLANE, 1)
     upper = shifted(cot[0, 1:], PLANE, -1)
 
-    hidden, ag = call(
-        front_body,
-        [shape((2, 4, 64, 128)), shape((2, 3, 64, 128))],
+    hidden, ag, partial = call(
+        front_and_grads_body,
+        [shape((2, 4, 64, 128)), shape((2, 3, 64, 128)), shape((16, 16, 1408))],
         here,
         deep,
         lower,
@@ -368,24 +385,12 @@
         upper,
         *weights,
         scalars=1,
+        far_outs=1,
+        scratch=(pltpu.VMEM((11, 16, 16, 128), BF), pltpu.SemaphoreType.DMA((11,))),
     )
     up = [(2 * k, 2 * k + 2) for k in range(planes - 1)]
     down = [(2 * k + 1, 2 * k - 1) for k in range(1, planes)]
     side = lax.ppermute(jnp.where(zh == 0, hidden[1:], hidden[:1]), DEPTH, up + down)
-    partial = call(
-        kernel_grads_body,
-        shape((16, 16, 1408)),
-        here,
-        deep,
-        lower,
-        cot,
-        upper,
-        ag,
-        hidden,
-        scalars=1,
-        far_out=True,
-        scratch=(pltpu.VMEM((11, 16, 16, 128), BF), pltpu.SemaphoreType.DMA((11,))),
-    )
     parts = lax.all_to_all(partial, PLANE, 0, 0, tiled=True)
 
     three = jnp.where(

time: 98.8 us -> 98.1 us (level)
    pallas_call x10 -> x9, Pallas kernels: 11.6 us -> 10.9 us  [call(): pl.pallas_call(body, out_shape=outs, in_specs=[smem] * scalars + [vmem] *...]
where the time goes in v9:
time: 98.1 us; the launch traced here: 97.5 us
  starting transfers between devices  59 us (60%)
  waiting for transfers between devices  25.5 us (26%)
  Pallas kernels  10.9 us (11%)
  local copies, waits for them, and re-layouts  1.04 us (1%)
    ppermute x4, starting transfers between devices, shifted(): return lax.ppermute(block, axis, route)  17.5 us
    ppermute x1, starting transfers between devices, per_device(): other = lax.ppermute(volume, 'zh', [(0, 1), (1, 0)])  16.3 us
    pallas_call x9, Pallas kernels, call(): pl.pallas_call(body, out_shape=outs, in_specs=[smem] * scalars + [vmem] *...  10.9 us
    all_to_all x1, waiting for transfers between devices, per_device(): rows = lax.all_to_all(summed.reshape(16, 8, 384), HEIGHT, 0, 0, tiled=True)  9.01 us
    ppermute x4, waiting for transfers between devices, shifted(): return lax.ppermute(block, axis, route)  8.02 us
    all_to_all x1, starting transfers between devices, per_device(): parts = lax.all_to_all(partial, PLANE, 0, 0, tiled=True)  7.96 us
    all_to_all x1, starting transfers between devices, per_device(): rows = lax.all_to_all(summed.reshape(16, 8, 384), HEIGHT, 0, 0, tiled=True)  7.02 us
    all_to_all x1, starting transfers between devices, per_device(): slab = lax.all_to_all(slabs, LINE, 0, 0, tiled=True)  6.26 us
  transfers between devices with their start and end apart: 10, of which 5 were waited for; matrix products, arithmetic and copies ran while one was open for 1% of the time, Pallas kernels for 5%

profile of v9, /device:TPU:1, one launch (start us, length us, event | category | flops | bytes accessed | tf_op | source)
XLA Modules:
  0.0 97.5 jit_solution(12855412591253970517)
XLA Ops:
  0.6 16.3 %collective-permute-start = (bf16[64,2,4,128]{3,2,1,0:T(4,128)(2,1)}, bf16[64,2,4,128]{3,2,1,0:T(4,128)(2,1)S(1)}, u32[]{:S(2)}, u32[]{:S(2)}) collective-permute-start(bf16[64,2,4,128]{3,2,1,0:T(4,128)(2,1)} %param.4), channel_id=1, source_target_pairs={{0,16},{16,0},{1,17},{17,1},{2,18},{18,2},{3,19},{19,3},{4,20},{20... | collective-permute-start | bytes 393224 | tf_op jit(solution)/shard_map/ppermute | solution.py:346
  16.9 1.0 reshape.45.cot_ref
  17.9 0.7 shard_map.77
  18.6 6.3 %all-to-all-start = ((bf16[32,8,384]{2,1,0:T(8,128)(2,1)}), bf16[32,8,384]{2,1,0:T(8,128)(2,1)S(1)}, u32[]{:S(2)}, u32[]{:S(2)}) async-start(bf16[32,8,384]{2,1,0:T(8,128)(2,1)} %shard_map.77), calls=%async_computation | async-start | bytes 393216 | tf_op jit(solution)/shard_map/all_to_all | solution.py:348
  24.9 1.6 %shard_map.75 = bf16[4,4,64,128]{3,2,1,0:T(8,128)(2,1)S(1)} custom-call(s32[2]{0:T(128)S(1)} %pad_add_fusion.s_ref, bf16[512,128]{1,0:T(8,128)(2,1)S(1)} %bitcast.25, bf16[512,128]{1,0:T(8,128)(2,1)S(1)} %bitcast.26), custom_call_target="tpu_custom_call" | custom-call | flops 40000000000 | tf_op jit(solution)/shard_map/pallas_call | solution.py:47
  26.6 11.1 %collective-permute-start.1 = (bf16[4,3,64,128]{3,2,1,0:T(8,128)(2,1)S(1)}, bf16[4,3,64,128]{3,2,1,0:T(8,128)(2,1)S(1)}, u32[]{:S(2)}, u32[]{:S(2)}) collective-permute-start(bf16[4,3,64,128]{3,2,1,0:T(8,128)(2,1)S(1)} %slice.36), channel_id=1, source_target_pairs={{0,1},{1,2},{2,3},{3,4},{4,5},{5,6},{6,7},{7,8},{8,9},{9,10},{10,1... | collective-permute-start | bytes 589832 | tf_op jit(solution)/shard_map/ppermute | solution.py:331
  37.8 1.9 %collective-permute-start.2 = (bf16[4,2,64,128]{3,2,1,0:T(8,128)(2,1)S(1)}, bf16[4,2,64,128]{3,2,1,0:T(8,128)(2,1)S(1)}, u32[]{:S(2)}, u32[]{:S(2)}) collective-permute-start(bf16[4,2,64,128]{3,2,1,0:T(8,128)(2,1)S(1)} %slice.37), channel_id=1, source_target_pairs={{1,0},{2,1},{3,2},{4,3},{5,4},{6,5},{7,6},{8,7},{9,8},{10,9},{11,1... | collective-permute-start | bytes 393224 | tf_op jit(solution)/shard_map/ppermute | solution.py:331
  39.7 0.6 shard_map.76
  40.3 3.7 %collective-permute-done.2 = bf16[4,2,64,128]{3,2,1,0:T(8,128)(2,1)S(1)} collective-permute-done((bf16[4,2,64,128]{3,2,1,0:T(8,128)(2,1)S(1)}, bf16[4,2,64,128]{3,2,1,0:T(8,128)(2,1)S(1)}, u32[]{:S(2)}, u32[]{:S(2)}) %collective-permute-start.2) | collective-permute-done | bytes 131104 | tf_op jit(solution)/shard_map/ppermute | solution.py:331
  44.5 3.2 %collective-permute-start.3 = (bf16[14,64,128]{2,1,0:T(8,128)(2,1)S(1)}, bf16[14,64,128]{2,1,0:T(8,128)(2,1)S(1)}, u32[]{:S(2)}, u32[]{:S(2)}) collective-permute-start(bf16[14,64,128]{2,1,0:T(8,128)(2,1)S(1)} %pad_maximum_fusion.1), channel_id=1, source_target_pairs={{0,32},{32,64},{64,96},{96,128},{128,160},{160,192},{192,224},{224... | collective-permute-start | bytes 688136 | tf_op jit(solution)/shard_map/ppermute | solution.py:331
  47.7 1.3 %collective-permute-start.4 = (bf16[5,64,128]{2,1,0:T(8,128)(2,1)S(1)}, bf16[5,64,128]{2,1,0:T(8,128)(2,1)S(1)}, u32[]{:S(2)}, u32[]{:S(2)}) collective-permute-start(bf16[5,64,128]{2,1,0:T(8,128)(2,1)S(1)} %get-tuple-element.30), channel_id=1, source_target_pairs={{32,0},{64,32},{96,64},{128,96},{160,128},{192,160},{224,192},{256... | collective-permute-start | bytes 245768 | tf_op jit(solution)/shard_map/ppermute | solution.py:331
  49.0 4.3 %collective-permute-done.4.up_ref = bf16[5,64,128]{2,1,0:T(8,128)(2,1)S(1)} collective-permute-done((bf16[5,64,128]{2,1,0:T(8,128)(2,1)S(1)}, bf16[5,64,128]{2,1,0:T(8,128)(2,1)S(1)}, u32[]{:S(2)}, u32[]{:S(2)}) %collective-permute-start.4) | collective-permute-done | bytes 81952 | tf_op jit(solution)/shard_map/ppermute | solution.py:331
  53.3 4.0 %shard_map.79 = (bf16[2,4,64,128]{3,2,1,0:T(8,128)(2,1)S(1)}, bf16[2,3,64,128]{3,2,1,0:T(8,128)(2,1)S(1)}, bf16[16,16,1408]{2,1,0:T(8,128)(2,1)}) custom-call(s32[2]{0:T(128)S(1)} %pad_add_fusion.s_ref, bf16[4,9,64,128]{3,2,1,0:T(8,128)(2,1)S(1)} %pad_maximum_fusion.deep_ref, bf16[14,64,128]{2,1,0:T(8,128)(2,1)S(1)} %collective-permute-done.3.low_ref, ...), custom_call_target="tpu_custom_call" | custom-call | tf_op jit(solution)/shard_map/pallas_call | solution.py:47
  57.3 8.0 %all-to-all-start.1 = ((bf16[16,16,1408]{2,1,0:T(8,128)(2,1)}), bf16[16,16,1408]{2,1,0:T(8,128)(2,1)S(1)}, u32[]{:S(2)}, u32[]{:S(2)}) async-start(bf16[16,16,1408]{2,1,0:T(8,128)(2,1)} %get-tuple-element.20), calls=%async_computation.1 | async-start | bytes 1441792 | tf_op jit(solution)/shard_map/all_to_all | solution.py:394
  65.3 3.3 %collective-permute-start.5 = (bf16[1,4,64,128]{3,2,1,0:T(8,128)(2,1)S(1)}, bf16[1,4,64,128]{3,2,1,0:T(8,128)(2,1)S(1)}, u32[]{:S(2)}, u32[]{:S(2)}) collective-permute-start(bf16[1,4,64,128]{3,2,1,0:T(8,128)(2,1)S(1)} %slice_select_fusion), channel_id=1, source_target_pairs={{0,32},{32,64},{64,96},{96,128},{128,160},{160,192},{192,224},{224... | collective-permute-start | bytes 196616 | tf_op jit(solution)/shard_map/ppermute | solution.py:393
  68.5 2.7 %collective-permute-done.5 = bf16[1,4,64,128]{3,2,1,0:T(8,128)(2,1)S(1)} collective-permute-done((bf16[1,4,64,128]{3,2,1,0:T(8,128)(2,1)S(1)}, bf16[1,4,64,128]{3,2,1,0:T(8,128)(2,1)S(1)}, u32[]{:S(2)}, u32[]{:S(2)}) %collective-permute-start.5) | collective-permute-done | bytes 65568 | tf_op jit(solution)/shard_map/ppermute | solution.py:393
  71.2 0.5 shard_map.80.next_ref
  71.7 5.8 %all-to-all-done.1.got_ref = bf16[16,16,1408]{2,1,0:T(8,128)(2,1)S(1)} async-done(((bf16[16,16,1408]{2,1,0:T(8,128)(2,1)}), bf16[16,16,1408]{2,1,0:T(8,128)(2,1)S(1)}, u32[]{:S(2)}, u32[]{:S(2)}) %all-to-all-start.1) | async-done | bytes 720928 | tf_op jit(solution)/shard_map/all_to_all | solution.py:394
  77.5 0.8 shard_map.81
  78.3 7.0 %all-to-all-start.2 = ((bf16[16,8,384]{2,1,0:T(8,128)(2,1)}), bf16[16,8,384]{2,1,0:T(8,128)(2,1)S(1)}, u32[]{:S(2)}, u32[]{:S(2)}) async-start(bf16[16,8,384]{2,1,0:T(8,128)(2,1)} %bitcast.10), calls=%async_computation.2 | async-start | bytes 196608 | tf_op jit(solution)/shard_map/all_to_all | solution.py:405
  85.4 0.7 collective-permute-start.6
  86.1 1.6 %shard_map.83 = bf16[512,128]{1,0:T(8,128)(2,1)} custom-call(bf16[2,3,64,128]{3,2,1,0:T(8,128)(2,1)S(1)} %maximum_select_fusion.1.a_ref, bf16[9,192,128]{2,1,0:T(8,128)(2,1)S(1)} %get-tuple-element.18.w_one_ref.k_ref), custom_call_target="tpu_custom_call" | custom-call | tf_op jit(solution)/shard_map/pallas_call | solution.py:47
  87.6 9.0 %all-to-all-done.2.got_ref = bf16[16,8,384]{2,1,0:T(8,128)(2,1)S(1)} async-done(((bf16[16,8,384]{2,1,0:T(8,128)(2,1)}), bf16[16,8,384]{2,1,0:T(8,128)(2,1)S(1)}, u32[]{:S(2)}, u32[]{:S(2)}) %all-to-all-start.2) | async-done | bytes 98336 | tf_op jit(solution)/shard_map/all_to_all | solution.py:405
  96.6 0.9 shard_map.82
  (23 shorter events, 0.6 us)
Async XLA Ops:
  0.6 24.3 %collective-permute-start = (bf16[64,2,4,128]{3,2,1,0:T(4,128)(2,1)}, bf16[64,2,4,128]{3,2,1,0:T(4,128)(2,1)S(1)}, u32[]{:S(2)}, u32[]{:S(2)}) collective-permute-start(bf16[64,2,4,128]{3,2,1,0:T(4,128)(2,1)} %param.4), channel_id=1, source_target_pairs={{0,16},{16,0},{1,17},{17,1},{2,18},{18,2},{3,19},{19,3},{4,20},{20... | collective-permute-start | bytes 393224 | tf_op jit(solution)/shard_map/ppermute | solution.py:346
  18.6 6.4 %copy-start.2 = (bf16[64,2,4,128]{3,2,1,0:T(4,128)(2,1)S(1)}, bf16[64,2,4,128]{3,2,1,0:T(4,128)(2,1)}, u32[]{:S(2)}) copy-start(bf16[64,2,4,128]{3,2,1,0:T(4,128)(2,1)} %param.4) | copy-start | bytes 393220
  18.6 25.6 %all-to-all-start = ((bf16[32,8,384]{2,1,0:T(8,128)(2,1)}), bf16[32,8,384]{2,1,0:T(8,128)(2,1)S(1)}, u32[]{:S(2)}, u32[]{:S(2)}) async-start(bf16[32,8,384]{2,1,0:T(8,128)(2,1)} %shard_map.77), calls=%async_computation | async-start | bytes 393216 | tf_op jit(solution)/shard_map/all_to_all | solution.py:348
  24.9 14.8 %copy-start = (bf16[3,3,3,128,128]{4,3,2,1,0:T(8,128)(2,1)S(1)}, bf16[3,3,3,128,128]{4,3,2,1,0:T(8,128)(2,1)}, u32[]{:S(2)}) copy-start(bf16[3,3,3,128,128]{4,3,2,1,0:T(8,128)(2,1)} %param.6) | copy-start | bytes 2654212
  26.6 13.1 %copy-start.1 = (bf16[3,3,3,64,128]{4,3,2,1,0:T(8,128)(2,1)S(1)}, bf16[3,3,3,64,128]{4,3,2,1,0:T(8,128)(2,1)}, u32[]{:S(2)}) copy-start(bf16[3,3,3,64,128]{4,3,2,1,0:T(8,128)(2,1)} %param.5) | copy-start | bytes 1327108
  26.6 17.4 %collective-permute-start.1 = (bf16[4,3,64,128]{3,2,1,0:T(8,128)(2,1)S(1)}, bf16[4,3,64,128]{3,2,1,0:T(8,128)(2,1)S(1)}, u32[]{:S(2)}, u32[]{:S(2)}) collective-permute-start(bf16[4,3,64,128]{3,2,1,0:T(8,128)(2,1)S(1)} %slice.36), channel_id=1, source_target_pairs={{0,1},{1,2},{2,3},{3,4},{4,5},{5,6},{6,7},{7,8},{8,9},{9,10},{10,1... | collective-permute-start | bytes 589832 | tf_op jit(solution)/shard_map/ppermute | solution.py:331
  37.8 6.3 %collective-permute-start.2 = (bf16[4,2,64,128]{3,2,1,0:T(8,128)(2,1)S(1)}, bf16[4,2,64,128]{3,2,1,0:T(8,128)(2,1)S(1)}, u32[]{:S(2)}, u32[]{:S(2)}) collective-permute-start(bf16[4,2,64,128]{3,2,1,0:T(8,128)(2,1)S(1)} %slice.37), channel_id=1, source_target_pairs={{1,0},{2,1},{3,2},{4,3},{5,4},{6,5},{7,6},{8,7},{9,8},{10,9},{11,1... | collective-permute-start | bytes 393224 | tf_op jit(solution)/shard_map/ppermute | solution.py:331
  44.5 8.8 %collective-permute-start.3 = (bf16[14,64,128]{2,1,0:T(8,128)(2,1)S(1)}, bf16[14,64,128]{2,1,0:T(8,128)(2,1)S(1)}, u32[]{:S(2)}, u32[]{:S(2)}) collective-permute-start(bf16[14,64,128]{2,1,0:T(8,128)(2,1)S(1)} %pad_maximum_fusion.1), channel_id=1, source_target_pairs={{0,32},{32,64},{64,96},{96,128},{128,160},{160,192},{192,224},{224... | collective-permute-start | bytes 688136 | tf_op jit(solution)/shard_map/ppermute | solution.py:331
  47.7 5.6 %collective-permute-start.4 = (bf16[5,64,128]{2,1,0:T(8,128)(2,1)S(1)}, bf16[5,64,128]{2,1,0:T(8,128)(2,1)S(1)}, u32[]{:S(2)}, u32[]{:S(2)}) collective-permute-start(bf16[5,64,128]{2,1,0:T(8,128)(2,1)S(1)} %get-tuple-element.30), channel_id=1, source_target_pairs={{32,0},{64,32},{96,64},{128,96},{160,128},{192,160},{224,192},{256... | collective-permute-start | bytes 245768 | tf_op jit(solution)/shard_map/ppermute | solution.py:331
  57.3 20.2 %all-to-all-start.1 = ((bf16[16,16,1408]{2,1,0:T(8,128)(2,1)}), bf16[16,16,1408]{2,1,0:T(8,128)(2,1)S(1)}, u32[]{:S(2)}, u32[]{:S(2)}) async-start(bf16[16,16,1408]{2,1,0:T(8,128)(2,1)} %get-tuple-element.20), calls=%async_computation.1 | async-start | bytes 1441792 | tf_op jit(solution)/shard_map/all_to_all | solution.py:394
  65.3 5.9 %collective-permute-start.5 = (bf16[1,4,64,128]{3,2,1,0:T(8,128)(2,1)S(1)}, bf16[1,4,64,128]{3,2,1,0:T(8,128)(2,1)S(1)}, u32[]{:S(2)}, u32[]{:S(2)}) collective-permute-start(bf16[1,4,64,128]{3,2,1,0:T(8,128)(2,1)S(1)} %slice_select_fusion), channel_id=1, source_target_pairs={{0,32},{32,64},{64,96},{96,128},{128,160},{160,192},{192,224},{224... | collective-permute-start | bytes 196616 | tf_op jit(solution)/shard_map/ppermute | solution.py:393
  78.3 18.3 %all-to-all-start.2 = ((bf16[16,8,384]{2,1,0:T(8,128)(2,1)}), bf16[16,8,384]{2,1,0:T(8,128)(2,1)S(1)}, u32[]{:S(2)}, u32[]{:S(2)}) async-start(bf16[16,8,384]{2,1,0:T(8,128)(2,1)} %bitcast.10), calls=%async_computation.2 | async-start | bytes 196608 | tf_op jit(solution)/shard_map/all_to_all | solution.py:405
  85.4 0.7 collective-permute-start.6

commit v10 on v9

--- a/solution.py
+++ b/solution.py
@@ -318,10 +318,8 @@
             two_ref[3 * i + e] = table[16 * i + 4 * e : 16 * i + 4 * e + 4]
     cells = jnp.concatenate([got_ref[i][:, :128].astype(F32) for i in range(16)], axis=0).astype(BF)
     to, of = iota((256, 128), 0), iota((256, 128), 1)
-    source = to % 32 // 2 * 8 + to // 32
-    left = dot(one_hot((of == source) & (to % 2 == 0)), cells)
-    right = dot(one_hot((of == source) & (to % 2 == 1)), cells)
-    rows = left[:, :64] + right[:, 64:]
+    both = dot(one_hot(of == to % 32 // 2 * 8 + to // 32), cells)
+    rows = jnp.where(iota((256, 64), 0) % 2 == 0, both[:, :64], both[:, 64:])
     next_ref[...] = rows.reshape(8, 32, 64).astype(BF)
 
 

time: 98.1 us -> 98.1 us (level)
  no operation moved by 1% of the time
where the time goes in v10:
time: 98.1 us; the launch traced here: 97.5 us
  starting transfers between devices  59 us (60%)
  waiting for transfers between devices  25.5 us (26%)
  Pallas kernels  10.9 us (11%)
  local copies, waits for them, and re-layouts  1.04 us (1%)
    ppermute x4, starting transfers between devices, shifted(): return lax.ppermute(block, axis, route)  17.5 us
    ppermute x1, starting transfers between devices, per_device(): other = lax.ppermute(volume, 'zh', [(0, 1), (1, 0)])  16.3 us
    pallas_call x9, Pallas kernels, call(): pl.pallas_call(body, out_shape=outs, in_specs=[smem] * scalars + [vmem] *...  10.9 us
    all_to_all x1, waiting for transfers between devices, per_device(): rows = lax.all_to_all(summed.reshape(16, 8, 384), HEIGHT, 0, 0, tiled=True)  9.01 us
    ppermute x4, waiting for transfers between devices, shifted(): return lax.ppermute(block, axis, route)  8.02 us
    all_to_all x1, starting transfers between devices, per_device(): parts = lax.all_to_all(partial, PLANE, 0, 0, tiled=True)  7.96 us
    all_to_all x1, starting transfers between devices, per_device(): rows = lax.all_to_all(summed.reshape(16, 8, 384), HEIGHT, 0, 0, tiled=True)  7.02 us
    all_to_all x1, starting transfers between devices, per_device(): slab = lax.all_to_all(slabs, LINE, 0, 0, tiled=True)  6.26 us
  transfers between devices with their start and end apart: 10, of which 5 were waited for; matrix products, arithmetic and copies ran while one was open for 1% of the time, Pallas kernels for 5%

profile of v10, /device:TPU:1, one launch (start us, length us, event | category | flops | bytes accessed | tf_op | source)
XLA Modules:
  0.0 97.5 jit_solution(4946279648721985901)
XLA Ops:
  0.6 16.3 %collective-permute-start = (bf16[64,2,4,128]{3,2,1,0:T(4,128)(2,1)}, bf16[64,2,4,128]{3,2,1,0:T(4,128)(2,1)S(1)}, u32[]{:S(2)}, u32[]{:S(2)}) collective-permute-start(bf16[64,2,4,128]{3,2,1,0:T(4,128)(2,1)} %param.4), channel_id=1, source_target_pairs={{0,16},{16,0},{1,17},{17,1},{2,18},{18,2},{3,19},{19,3},{4,20},{20... | collective-permute-start | bytes 393224 | tf_op jit(solution)/shard_map/ppermute | solution.py:344
  16.9 1.0 reshape.45.cot_ref
  17.9 0.7 shard_map.77
  18.6 6.3 %all-to-all-start = ((bf16[32,8,384]{2,1,0:T(8,128)(2,1)}), bf16[32,8,384]{2,1,0:T(8,128)(2,1)S(1)}, u32[]{:S(2)}, u32[]{:S(2)}) async-start(bf16[32,8,384]{2,1,0:T(8,128)(2,1)} %shard_map.77), calls=%async_computation | async-start | bytes 393216 | tf_op jit(solution)/shard_map/all_to_all | solution.py:346
  24.9 1.6 %shard_map.75 = bf16[4,4,64,128]{3,2,1,0:T(8,128)(2,1)S(1)} custom-call(s32[2]{0:T(128)S(1)} %pad_add_fusion.s_ref, bf16[512,128]{1,0:T(8,128)(2,1)S(1)} %bitcast.25, bf16[512,128]{1,0:T(8,128)(2,1)S(1)} %bitcast.26), custom_call_target="tpu_custom_call" | custom-call | flops 40000000000 | tf_op jit(solution)/shard_map/pallas_call | solution.py:47
  26.6 11.1 %collective-permute-start.1 = (bf16[4,3,64,128]{3,2,1,0:T(8,128)(2,1)S(1)}, bf16[4,3,64,128]{3,2,1,0:T(8,128)(2,1)S(1)}, u32[]{:S(2)}, u32[]{:S(2)}) collective-permute-start(bf16[4,3,64,128]{3,2,1,0:T(8,128)(2,1)S(1)} %slice.36), channel_id=1, source_target_pairs={{0,1},{1,2},{2,3},{3,4},{4,5},{5,6},{6,7},{7,8},{8,9},{9,10},{10,1... | collective-permute-start | bytes 589832 | tf_op jit(solution)/shard_map/ppermute | solution.py:329
  37.8 1.9 %collective-permute-start.2 = (bf16[4,2,64,128]{3,2,1,0:T(8,128)(2,1)S(1)}, bf16[4,2,64,128]{3,2,1,0:T(8,128)(2,1)S(1)}, u32[]{:S(2)}, u32[]{:S(2)}) collective-permute-start(bf16[4,2,64,128]{3,2,1,0:T(8,128)(2,1)S(1)} %slice.37), channel_id=1, source_target_pairs={{1,0},{2,1},{3,2},{4,3},{5,4},{6,5},{7,6},{8,7},{9,8},{10,9},{11,1... | collective-permute-start | bytes 393224 | tf_op jit(solution)/shard_map/ppermute | solution.py:329
  39.7 0.6 shard_map.76
  40.3 3.7 %collective-permute-done.2 = bf16[4,2,64,128]{3,2,1,0:T(8,128)(2,1)S(1)} collective-permute-done((bf16[4,2,64,128]{3,2,1,0:T(8,128)(2,1)S(1)}, bf16[4,2,64,128]{3,2,1,0:T(8,128)(2,1)S(1)}, u32[]{:S(2)}, u32[]{:S(2)}) %collective-permute-start.2) | collective-permute-done | bytes 131104 | tf_op jit(solution)/shard_map/ppermute | solution.py:329
  44.5 3.2 %collective-permute-start.3 = (bf16[14,64,128]{2,1,0:T(8,128)(2,1)S(1)}, bf16[14,64,128]{2,1,0:T(8,128)(2,1)S(1)}, u32[]{:S(2)}, u32[]{:S(2)}) collective-permute-start(bf16[14,64,128]{2,1,0:T(8,128)(2,1)S(1)} %pad_maximum_fusion.1), channel_id=1, source_target_pairs={{0,32},{32,64},{64,96},{96,128},{128,160},{160,192},{192,224},{224... | collective-permute-start | bytes 688136 | tf_op jit(solution)/shard_map/ppermute | solution.py:329
  47.7 1.3 %collective-permute-start.4 = (bf16[5,64,128]{2,1,0:T(8,128)(2,1)S(1)}, bf16[5,64,128]{2,1,0:T(8,128)(2,1)S(1)}, u32[]{:S(2)}, u32[]{:S(2)}) collective-permute-start(bf16[5,64,128]{2,1,0:T(8,128)(2,1)S(1)} %get-tuple-element.30), channel_id=1, source_target_pairs={{32,0},{64,32},{96,64},{128,96},{160,128},{192,160},{224,192},{256... | collective-permute-start | bytes 245768 | tf_op jit(solution)/shard_map/ppermute | solution.py:329
  49.0 4.3 %collective-permute-done.4.up_ref = bf16[5,64,128]{2,1,0:T(8,128)(2,1)S(1)} collective-permute-done((bf16[5,64,128]{2,1,0:T(8,128)(2,1)S(1)}, bf16[5,64,128]{2,1,0:T(8,128)(2,1)S(1)}, u32[]{:S(2)}, u32[]{:S(2)}) %collective-permute-start.4) | collective-permute-done | bytes 81952 | tf_op jit(solution)/shard_map/ppermute | solution.py:329
  53.3 4.0 %shard_map.79 = (bf16[2,4,64,128]{3,2,1,0:T(8,128)(2,1)S(1)}, bf16[2,3,64,128]{3,2,1,0:T(8,128)(2,1)S(1)}, bf16[16,16,1408]{2,1,0:T(8,128)(2,1)}) custom-call(s32[2]{0:T(128)S(1)} %pad_add_fusion.s_ref, bf16[4,9,64,128]{3,2,1,0:T(8,128)(2,1)S(1)} %pad_maximum_fusion.deep_ref, bf16[14,64,128]{2,1,0:T(8,128)(2,1)S(1)} %collective-permute-done.3.low_ref, ...), custom_call_target="tpu_custom_call" | custom-call | tf_op jit(solution)/shard_map/pallas_call | solution.py:47
  57.3 8.0 %all-to-all-start.1 = ((bf16[16,16,1408]{2,1,0:T(8,128)(2,1)}), bf16[16,16,1408]{2,1,0:T(8,128)(2,1)S(1)}, u32[]{:S(2)}, u32[]{:S(2)}) async-start(bf16[16,16,1408]{2,1,0:T(8,128)(2,1)} %get-tuple-element.20), calls=%async_computation.1 | async-start | bytes 1441792 | tf_op jit(solution)/shard_map/all_to_all | solution.py:392
  65.3 3.3 %collective-permute-start.5 = (bf16[1,4,64,128]{3,2,1,0:T(8,128)(2,1)S(1)}, bf16[1,4,64,128]{3,2,1,0:T(8,128)(2,1)S(1)}, u32[]{:S(2)}, u32[]{:S(2)}) collective-permute-start(bf16[1,4,64,128]{3,2,1,0:T(8,128)(2,1)S(1)} %slice_select_fusion), channel_id=1, source_target_pairs={{0,32},{32,64},{64,96},{96,128},{128,160},{160,192},{192,224},{224... | collective-permute-start | bytes 196616 | tf_op jit(solution)/shard_map/ppermute | solution.py:391
  68.5 2.7 %collective-permute-done.5 = bf16[1,4,64,128]{3,2,1,0:T(8,128)(2,1)S(1)} collective-permute-done((bf16[1,4,64,128]{3,2,1,0:T(8,128)(2,1)S(1)}, bf16[1,4,64,128]{3,2,1,0:T(8,128)(2,1)S(1)}, u32[]{:S(2)}, u32[]{:S(2)}) %collective-permute-start.5) | collective-permute-done | bytes 65568 | tf_op jit(solution)/shard_map/ppermute | solution.py:391
  71.2 0.5 shard_map.80.next_ref
  71.7 5.8 %all-to-all-done.1.got_ref = bf16[16,16,1408]{2,1,0:T(8,128)(2,1)S(1)} async-done(((bf16[16,16,1408]{2,1,0:T(8,128)(2,1)}), bf16[16,16,1408]{2,1,0:T(8,128)(2,1)S(1)}, u32[]{:S(2)}, u32[]{:S(2)}) %all-to-all-start.1) | async-done | bytes 720928 | tf_op jit(solution)/shard_map/all_to_all | solution.py:392
  77.5 0.8 shard_map.81
  78.3 7.0 %all-to-all-start.2 = ((bf16[16,8,384]{2,1,0:T(8,128)(2,1)}), bf16[16,8,384]{2,1,0:T(8,128)(2,1)S(1)}, u32[]{:S(2)}, u32[]{:S(2)}) async-start(bf16[16,8,384]{2,1,0:T(8,128)(2,1)} %bitcast.10), calls=%async_computation.2 | async-start | bytes 196608 | tf_op jit(solution)/shard_map/all_to_all | solution.py:403
  85.4 0.7 collective-permute-start.6
  86.1 1.6 %shard_map.83 = bf16[512,128]{1,0:T(8,128)(2,1)} custom-call(bf16[2,3,64,128]{3,2,1,0:T(8,128)(2,1)S(1)} %maximum_select_fusion.1.a_ref, bf16[9,192,128]{2,1,0:T(8,128)(2,1)S(1)} %get-tuple-element.18.w_one_ref.k_ref), custom_call_target="tpu_custom_call" | custom-call | tf_op jit(solution)/shard_map/pallas_call | solution.py:47
  87.6 9.0 %all-to-all-done.2.got_ref = bf16[16,8,384]{2,1,0:T(8,128)(2,1)S(1)} async-done(((bf16[16,8,384]{2,1,0:T(8,128)(2,1)}), bf16[16,8,384]{2,1,0:T(8,128)(2,1)S(1)}, u32[]{:S(2)}, u32[]{:S(2)}) %all-to-all-start.2) | async-done | bytes 98336 | tf_op jit(solution)/shard_map/all_to_all | solution.py:403
  96.6 0.9 shard_map.82
  (23 shorter events, 0.6 us)
Async XLA Ops:
  0.6 24.3 %collective-permute-start = (bf16[64,2,4,128]{3,2,1,0:T(4,128)(2,1)}, bf16[64,2,4,128]{3,2,1,0:T(4,128)(2,1)S(1)}, u32[]{:S(2)}, u32[]{:S(2)}) collective-permute-start(bf16[64,2,4,128]{3,2,1,0:T(4,128)(2,1)} %param.4), channel_id=1, source_target_pairs={{0,16},{16,0},{1,17},{17,1},{2,18},{18,2},{3,19},{19,3},{4,20},{20... | collective-permute-start | bytes 393224 | tf_op jit(solution)/shard_map/ppermute | solution.py:344
  18.6 6.4 %copy-start.2 = (bf16[64,2,4,128]{3,2,1,0:T(4,128)(2,1)S(1)}, bf16[64,2,4,128]{3,2,1,0:T(4,128)(2,1)}, u32[]{:S(2)}) copy-start(bf16[64,2,4,128]{3,2,1,0:T(4,128)(2,1)} %param.4) | copy-start | bytes 393220
  18.6 25.6 %all-to-all-start = ((bf16[32,8,384]{2,1,0:T(8,128)(2,1)}), bf16[32,8,384]{2,1,0:T(8,128)(2,1)S(1)}, u32[]{:S(2)}, u32[]{:S(2)}) async-start(bf16[32,8,384]{2,1,0:T(8,128)(2,1)} %shard_map.77), calls=%async_computation | async-start | bytes 393216 | tf_op jit(solution)/shard_map/all_to_all | solution.py:346
  24.9 14.8 %copy-start = (bf16[3,3,3,128,128]{4,3,2,1,0:T(8,128)(2,1)S(1)}, bf16[3,3,3,128,128]{4,3,2,1,0:T(8,128)(2,1)}, u32[]{:S(2)}) copy-start(bf16[3,3,3,128,128]{4,3,2,1,0:T(8,128)(2,1)} %param.6) | copy-start | bytes 2654212
  26.6 13.1 %copy-start.1 = (bf16[3,3,3,64,128]{4,3,2,1,0:T(8,128)(2,1)S(1)}, bf16[3,3,3,64,128]{4,3,2,1,0:T(8,128)(2,1)}, u32[]{:S(2)}) copy-start(bf16[3,3,3,64,128]{4,3,2,1,0:T(8,128)(2,1)} %param.5) | copy-start | bytes 1327108
  26.6 17.4 %collective-permute-start.1 = (bf16[4,3,64,128]{3,2,1,0:T(8,128)(2,1)S(1)}, bf16[4,3,64,128]{3,2,1,0:T(8,128)(2,1)S(1)}, u32[]{:S(2)}, u32[]{:S(2)}) collective-permute-start(bf16[4,3,64,128]{3,2,1,0:T(8,128)(2,1)S(1)} %slice.36), channel_id=1, source_target_pairs={{0,1},{1,2},{2,3},{3,4},{4,5},{5,6},{6,7},{7,8},{8,9},{9,10},{10,1... | collective-permute-start | bytes 589832 | tf_op jit(solution)/shard_map/ppermute | solution.py:329
  37.8 6.3 %collective-permute-start.2 = (bf16[4,2,64,128]{3,2,1,0:T(8,128)(2,1)S(1)}, bf16[4,2,64,128]{3,2,1,0:T(8,128)(2,1)S(1)}, u32[]{:S(2)}, u32[]{:S(2)}) collective-permute-start(bf16[4,2,64,128]{3,2,1,0:T(8,128)(2,1)S(1)} %slice.37), channel_id=1, source_target_pairs={{1,0},{2,1},{3,2},{4,3},{5,4},{6,5},{7,6},{8,7},{9,8},{10,9},{11,1... | collective-permute-start | bytes 393224 | tf_op jit(solution)/shard_map/ppermute | solution.py:329
  44.5 8.8 %collective-permute-start.3 = (bf16[14,64,128]{2,1,0:T(8,128)(2,1)S(1)}, bf16[14,64,128]{2,1,0:T(8,128)(2,1)S(1)}, u32[]{:S(2)}, u32[]{:S(2)}) collective-permute-start(bf16[14,64,128]{2,1,0:T(8,128)(2,1)S(1)} %pad_maximum_fusion.1), channel_id=1, source_target_pairs={{0,32},{32,64},{64,96},{96,128},{128,160},{160,192},{192,224},{224... | collective-permute-start | bytes 688136 | tf_op jit(solution)/shard_map/ppermute | solution.py:329
  47.7 5.6 %collective-permute-start.4 = (bf16[5,64,128]{2,1,0:T(8,128)(2,1)S(1)}, bf16[5,64,128]{2,1,0:T(8,128)(2,1)S(1)}, u32[]{:S(2)}, u32[]{:S(2)}) collective-permute-start(bf16[5,64,128]{2,1,0:T(8,128)(2,1)S(1)} %get-tuple-element.30), channel_id=1, source_target_pairs={{32,0},{64,32},{96,64},{128,96},{160,128},{192,160},{224,192},{256... | collective-permute-start | bytes 245768 | tf_op jit(solution)/shard_map/ppermute | solution.py:329
  57.3 20.2 %all-to-all-start.1 = ((bf16[16,16,1408]{2,1,0:T(8,128)(2,1)}), bf16[16,16,1408]{2,1,0:T(8,128)(2,1)S(1)}, u32[]{:S(2)}, u32[]{:S(2)}) async-start(bf16[16,16,1408]{2,1,0:T(8,128)(2,1)} %get-tuple-element.20), calls=%async_computation.1 | async-start | bytes 1441792 | tf_op jit(solution)/shard_map/all_to_all | solution.py:392
  65.3 5.9 %collective-permute-start.5 = (bf16[1,4,64,128]{3,2,1,0:T(8,128)(2,1)S(1)}, bf16[1,4,64,128]{3,2,1,0:T(8,128)(2,1)S(1)}, u32[]{:S(2)}, u32[]{:S(2)}) collective-permute-start(bf16[1,4,64,128]{3,2,1,0:T(8,128)(2,1)S(1)} %slice_select_fusion), channel_id=1, source_target_pairs={{0,32},{32,64},{64,96},{96,128},{128,160},{160,192},{192,224},{224... | collective-permute-start | bytes 196616 | tf_op jit(solution)/shard_map/ppermute | solution.py:391
  78.3 18.3 %all-to-all-start.2 = ((bf16[16,8,384]{2,1,0:T(8,128)(2,1)}), bf16[16,8,384]{2,1,0:T(8,128)(2,1)S(1)}, u32[]{:S(2)}, u32[]{:S(2)}) async-start(bf16[16,8,384]{2,1,0:T(8,128)(2,1)} %bitcast.10), calls=%async_computation.2 | async-start | bytes 196608 | tf_op jit(solution)/shard_map/all_to_all | solution.py:403
  85.4 0.7 collective-permute-start.6
